TPU v7x, 32 devices: a whole 2x2x4 slice. The times are simulated.
32 devices in a mesh: groups: 2 (over x), wide: 8 (over z, y), narrow: 2 (over core).
Axes of the slice: x: 2, y: 2, z: 4, core: 2. Of those that a mesh axis runs over, the one named last changes fastest.
Arguments:
- voxels: bfloat16 [131072, 128], P(('groups', 'wide', 'narrow')), parts along dimension 0, may hold values from -6 to 6
- counts: int32 [32], P('groups'), parts along dimension 0, may hold values from 2048 to 4096, as said below
- neighbours: int32 [27, 131072], P(None, ('groups', 'wide', 'narrow')), parts along dimension 1, may hold values from -1 to 65535, as said below
- conv_weight: bfloat16 [2, 27, 128, 128], replicated, may hold values from -0.109375 to 0.109375
- linear_weight: bfloat16 [2, 128, 128], replicated, may hold values from -0.5 to 0.5
- destination: int32 [131072], P(('groups', 'wide', 'narrow')), parts along dimension 0, may hold values from 0 to 65535, as said below
Outputs:
- serial: bfloat16 [131072, 128], P(('groups', 'wide', 'narrow')), parts along dimension 0
There are 2 independent parts, one for each index of `groups`. A program takes and returns all parts, laid end to end along the dimension named above; an argument that names none is the same for every part. Nothing has to cross between parts.
Inputs may be any that keep to these rules, and one draw needn't show every extreme that they name: `counts`: each device's block has 2048 to 4096 live rows, its first ones; some device is full in every draw. `neighbours`: an entry of column i is -1 or a row within 128 of i; offset 13 is row i itself; offsets 0 and 26 are rows i - 128 and i + 128 where those exist. `destination`: A permutation of the rows; the rows of one device go to every device, exactly 256 to each.
All inputs are finite; a program needn't handle non-finite values.
Results may differ from a plain program's by a relative error of at most 0.0056.
Values may be sent and summed in bfloat16 or wider, within the bound.
No kernel may reach another device: no remote copies, remote signals or barrier semaphores. Data moves between devices by JAX's collectives and lax.ppermute only.
A program may use at most 64 MiB of HBM per device.

v0:
```python
import jax
import jax.numpy as jnp
from jax import lax
from jax.sharding import PartitionSpec as P

HALO = 128


def padded_2(block, sides, width):
    for axis, dim in sides:
        count = lax.axis_size(axis)
        forward = [(i, i + 1) for i in range(count - 1)]
        backward = [(target, source) for source, target in forward]
        low = lax.ppermute(
            lax.slice_in_dim(block, block.shape[dim] - width, None, axis=dim), axis, forward
        )
        high = lax.ppermute(lax.slice_in_dim(block, 0, width, axis=dim), axis, backward)
        block = jnp.concatenate([low, block, high], axis=dim)
    return block


def local(voxels, counts, neighbours, conv_weight, linear_weight, destination):
    row_count, channels = voxels.shape
    shards = lax.axis_size(("wide", "narrow"))
    own_index = lax.axis_index(("wide", "narrow"))
    live_count = counts[own_index]
    live = jnp.arange(row_count, dtype=jnp.int32) < live_count
    features = jnp.where(live[:, None], voxels, jnp.zeros_like(voxels))
    first_row = own_index * row_count - HALO
    for layer_index in range(2):
        current = features
        padded = padded_2(current, ((("wide", "narrow"), 0),), HALO)

        def offset_term(running, pieces):
            targets, weight = pieces
            present = targets >= 0
            local_rows = jnp.where(present, targets - first_row, 0)
            picked = jnp.take(padded, local_rows, axis=0)
            picked = jnp.where(present[:, None], picked, jnp.zeros_like(picked))
            return (running + jnp.dot(picked, weight, preferred_element_type=jnp.float32), None)

        start = jnp.zeros((row_count, channels), jnp.float32)
        convolved, _ = lax.scan(offset_term, start, (neighbours, conv_weight[layer_index]))
        convolved = convolved.astype(jnp.bfloat16)
        projected = jnp.dot(
            convolved, linear_weight[layer_index], preferred_element_type=jnp.float32
        )
        average = jnp.mean(projected, axis=1, keepdims=True)
        centred = projected - average
        spread = jnp.mean(centred * centred, axis=1, keepdims=True)
        normed = centred / jnp.sqrt(spread + 1e-05)
        summed = current.astype(jnp.float32) + normed
        features = jnp.where(live[:, None], summed, jnp.zeros_like(summed)).astype(jnp.bfloat16)
    capacity = row_count // shards
    target_dev = destination // row_count
    target_row = destination % row_count
    onehot = (target_dev[:, None] == jnp.arange(shards, dtype=jnp.int32)[None, :]).astype(jnp.int32)
    ranks = jnp.sum((jnp.cumsum(onehot, axis=0) - 1) * onehot, axis=1)
    slot_ids = target_dev * capacity + ranks
    send_rows = jnp.zeros((shards * capacity, channels), jnp.bfloat16).at[slot_ids].set(features)
    send_places = jnp.full((shards * capacity,), -1, jnp.int32).at[slot_ids].set(target_row)
    got_rows, got_places = (
        lax.all_to_all(
            send_rows.reshape(shards, capacity, channels),
            ("wide", "narrow"),
            split_axis=0,
            concat_axis=0,
            tiled=True,
        ),
        lax.all_to_all(
            send_places.reshape(shards, capacity),
            ("wide", "narrow"),
            split_axis=0,
            concat_axis=0,
            tiled=True,
        ),
    )
    got_rows = got_rows.reshape(shards * capacity, channels)
    got_places = got_places.reshape(shards * capacity)
    got_places = jnp.where(got_places >= 0, got_places, row_count)
    serial = jnp.zeros((row_count + 1, channels), jnp.bfloat16).at[got_places].set(got_rows)
    return serial[:row_count]


def solution(mesh):
    in_specs = (
        P(("groups", "wide", "narrow"), None),
        P("groups"),
        P(None, ("groups", "wide", "narrow")),
        P(),
        P(),
        P(("groups", "wide", "narrow")),
    )
    out_specs = P(("groups", "wide", "narrow"), None)
    return jax.shard_map(local, mesh=mesh, in_specs=in_specs, out_specs=out_specs, check_vma=False)
```

profile of v0, /device:TPU:0, one launch (start us, length us, event | category | flops | bytes accessed | tf_op | source)
XLA Modules:
  0.0 1210.4 jit_solution(6630797334949781083)
XLA Ops:
  15.1 550.8 %while.22 = (s32[]{:T(128)}, f32[4096,128]{1,0:T(8,128)}, s32[27,4096]{1,0:T(8,128)}, s32[]{:T(128)}, bf16[4352,128]{1,0:T(8,128)(2,1)S(1)}, /*index=5*/bf16[27,128,128]{2,1,0:T(8,128)(2,1)S(1)}, s32[]{:T(128)}, s32[]{:T(128)}) while((s32[]{:T(128)}, f32[4096,128]{1,0:T(8,128)}, s32[27,4096]{1,0:T(8,128)}, s32[]{:T(128)}, ...), condition=%wide.region_5.7_spmd.clone, body=%wide.region_4.6_spmd.clone.sunk | while | flops 136372224 | bytes 7512175 | solution.py:43
  17.1 12.1 %gather_fusion = bf16[4096,128]{1,0:T(8,128)(2,1)S(1)} fusion(bf16[4352,128]{1,0:T(8,128)(2,1)S(1)} %get-tuple-element.268, s32[4096]{0:T(1024)S(1)} %fusion.48), kind=kCustom, calls=%fused_computation.clone.clone.1 | custom fusion | bytes 2113536 | tf_op jit(solution)/shard_map/while/body/eval_jaxpr/jit(_take)/gather | solution.py:38
  56.2 12.1 %gather_fusion = bf16[4096,128]{1,0:T(8,128)(2,1)S(1)} fusion(bf16[4352,128]{1,0:T(8,128)(2,1)S(1)} %get-tuple-element.268, s32[4096]{0:T(1024)S(1)} %fusion.48), kind=kCustom, calls=%fused_computation.clone.clone.1 | custom fusion | bytes 2113536 | tf_op jit(solution)/shard_map/while/body/eval_jaxpr/jit(_take)/gather | solution.py:38
  76.7 12.1 %gather_fusion = bf16[4096,128]{1,0:T(8,128)(2,1)S(1)} fusion(bf16[4352,128]{1,0:T(8,128)(2,1)S(1)} %get-tuple-element.268, s32[4096]{0:T(1024)S(1)} %fusion.48), kind=kCustom, calls=%fused_computation.clone.clone.1 | custom fusion | bytes 2113536 | tf_op jit(solution)/shard_map/while/body/eval_jaxpr/jit(_take)/gather | solution.py:38
  97.2 12.1 %gather_fusion = bf16[4096,128]{1,0:T(8,128)(2,1)S(1)} fusion(bf16[4352,128]{1,0:T(8,128)(2,1)S(1)} %get-tuple-element.268, s32[4096]{0:T(1024)S(1)} %fusion.48), kind=kCustom, calls=%fused_computation.clone.clone.1 | custom fusion | bytes 2113536 | tf_op jit(solution)/shard_map/while/body/eval_jaxpr/jit(_take)/gather | solution.py:38
  117.6 12.1 %gather_fusion = bf16[4096,128]{1,0:T(8,128)(2,1)S(1)} fusion(bf16[4352,128]{1,0:T(8,128)(2,1)S(1)} %get-tuple-element.268, s32[4096]{0:T(1024)S(1)} %fusion.48), kind=kCustom, calls=%fused_computation.clone.clone.1 | custom fusion | bytes 2113536 | tf_op jit(solution)/shard_map/while/body/eval_jaxpr/jit(_take)/gather | solution.py:38
  138.1 12.1 %gather_fusion = bf16[4096,128]{1,0:T(8,128)(2,1)S(1)} fusion(bf16[4352,128]{1,0:T(8,128)(2,1)S(1)} %get-tuple-element.268, s32[4096]{0:T(1024)S(1)} %fusion.48), kind=kCustom, calls=%fused_computation.clone.clone.1 | custom fusion | bytes 2113536 | tf_op jit(solution)/shard_map/while/body/eval_jaxpr/jit(_take)/gather | solution.py:38
  158.5 12.1 %gather_fusion = bf16[4096,128]{1,0:T(8,128)(2,1)S(1)} fusion(bf16[4352,128]{1,0:T(8,128)(2,1)S(1)} %get-tuple-element.268, s32[4096]{0:T(1024)S(1)} %fusion.48), kind=kCustom, calls=%fused_computation.clone.clone.1 | custom fusion | bytes 2113536 | tf_op jit(solution)/shard_map/while/body/eval_jaxpr/jit(_take)/gather | solution.py:38
  179.0 12.1 %gather_fusion = bf16[4096,128]{1,0:T(8,128)(2,1)S(1)} fusion(bf16[4352,128]{1,0:T(8,128)(2,1)S(1)} %get-tuple-element.268, s32[4096]{0:T(1024)S(1)} %fusion.48), kind=kCustom, calls=%fused_computation.clone.clone.1 | custom fusion | bytes 2113536 | tf_op jit(solution)/shard_map/while/body/eval_jaxpr/jit(_take)/gather | solution.py:38
  199.5 12.1 %gather_fusion = bf16[4096,128]{1,0:T(8,128)(2,1)S(1)} fusion(bf16[4352,128]{1,0:T(8,128)(2,1)S(1)} %get-tuple-element.268, s32[4096]{0:T(1024)S(1)} %fusion.48), kind=kCustom, calls=%fused_computation.clone.clone.1 | custom fusion | bytes 2113536 | tf_op jit(solution)/shard_map/while/body/eval_jaxpr/jit(_take)/gather | solution.py:38
  219.9 12.1 %gather_fusion = bf16[4096,128]{1,0:T(8,128)(2,1)S(1)} fusion(bf16[4352,128]{1,0:T(8,128)(2,1)S(1)} %get-tuple-element.268, s32[4096]{0:T(1024)S(1)} %fusion.48), kind=kCustom, calls=%fused_computation.clone.clone.1 | custom fusion | bytes 2113536 | tf_op jit(solution)/shard_map/while/body/eval_jaxpr/jit(_take)/gather | solution.py:38
  240.4 12.1 %gather_fusion = bf16[4096,128]{1,0:T(8,128)(2,1)S(1)} fusion(bf16[4352,128]{1,0:T(8,128)(2,1)S(1)} %get-tuple-element.268, s32[4096]{0:T(1024)S(1)} %fusion.48), kind=kCustom, calls=%fused_computation.clone.clone.1 | custom fusion | bytes 2113536 | tf_op jit(solution)/shard_map/while/body/eval_jaxpr/jit(_take)/gather | solution.py:38
  260.9 12.1 %gather_fusion = bf16[4096,128]{1,0:T(8,128)(2,1)S(1)} fusion(bf16[4352,128]{1,0:T(8,128)(2,1)S(1)} %get-tuple-element.268, s32[4096]{0:T(1024)S(1)} %fusion.48), kind=kCustom, calls=%fused_computation.clone.clone.1 | custom fusion | bytes 2113536 | tf_op jit(solution)/shard_map/while/body/eval_jaxpr/jit(_take)/gather | solution.py:38
  281.3 12.1 %gather_fusion = bf16[4096,128]{1,0:T(8,128)(2,1)S(1)} fusion(bf16[4352,128]{1,0:T(8,128)(2,1)S(1)} %get-tuple-element.268, s32[4096]{0:T(1024)S(1)} %fusion.48), kind=kCustom, calls=%fused_computation.clone.clone.1 | custom fusion | bytes 2113536 | tf_op jit(solution)/shard_map/while/body/eval_jaxpr/jit(_take)/gather | solution.py:38
  301.8 12.1 %gather_fusion = bf16[4096,128]{1,0:T(8,128)(2,1)S(1)} fusion(bf16[4352,128]{1,0:T(8,128)(2,1)S(1)} %get-tuple-element.268, s32[4096]{0:T(1024)S(1)} %fusion.48), kind=kCustom, calls=%fused_computation.clone.clone.1 | custom fusion | bytes 2113536 | tf_op jit(solution)/shard_map/while/body/eval_jaxpr/jit(_take)/gather | solution.py:38
  322.3 12.1 %gather_fusion = bf16[4096,128]{1,0:T(8,128)(2,1)S(1)} fusion(bf16[4352,128]{1,0:T(8,128)(2,1)S(1)} %get-tuple-element.268, s32[4096]{0:T(1024)S(1)} %fusion.48), kind=kCustom, calls=%fused_computation.clone.clone.1 | custom fusion | bytes 2113536 | tf_op jit(solution)/shard_map/while/body/eval_jaxpr/jit(_take)/gather | solution.py:38
  342.7 12.1 %gather_fusion = bf16[4096,128]{1,0:T(8,128)(2,1)S(1)} fusion(bf16[4352,128]{1,0:T(8,128)(2,1)S(1)} %get-tuple-element.268, s32[4096]{0:T(1024)S(1)} %fusion.48), kind=kCustom, calls=%fused_computation.clone.clone.1 | custom fusion | bytes 2113536 | tf_op jit(solution)/shard_map/while/body/eval_jaxpr/jit(_take)/gather | solution.py:38
  363.2 12.1 %gather_fusion = bf16[4096,128]{1,0:T(8,128)(2,1)S(1)} fusion(bf16[4352,128]{1,0:T(8,128)(2,1)S(1)} %get-tuple-element.268, s32[4096]{0:T(1024)S(1)} %fusion.48), kind=kCustom, calls=%fused_computation.clone.clone.1 | custom fusion | bytes 2113536 | tf_op jit(solution)/shard_map/while/body/eval_jaxpr/jit(_take)/gather | solution.py:38
  404.1 12.1 %gather_fusion = bf16[4096,128]{1,0:T(8,128)(2,1)S(1)} fusion(bf16[4352,128]{1,0:T(8,128)(2,1)S(1)} %get-tuple-element.268, s32[4096]{0:T(1024)S(1)} %fusion.48), kind=kCustom, calls=%fused_computation.clone.clone.1 | custom fusion | bytes 2113536 | tf_op jit(solution)/shard_map/while/body/eval_jaxpr/jit(_take)/gather | solution.py:38
  424.6 12.1 %gather_fusion = bf16[4096,128]{1,0:T(8,128)(2,1)S(1)} fusion(bf16[4352,128]{1,0:T(8,128)(2,1)S(1)} %get-tuple-element.268, s32[4096]{0:T(1024)S(1)} %fusion.48), kind=kCustom, calls=%fused_computation.clone.clone.1 | custom fusion | bytes 2113536 | tf_op jit(solution)/shard_map/while/body/eval_jaxpr/jit(_take)/gather | solution.py:38
  445.0 12.1 %gather_fusion = bf16[4096,128]{1,0:T(8,128)(2,1)S(1)} fusion(bf16[4352,128]{1,0:T(8,128)(2,1)S(1)} %get-tuple-element.268, s32[4096]{0:T(1024)S(1)} %fusion.48), kind=kCustom, calls=%fused_computation.clone.clone.1 | custom fusion | bytes 2113536 | tf_op jit(solution)/shard_map/while/body/eval_jaxpr/jit(_take)/gather | solution.py:38
  465.5 12.1 %gather_fusion = bf16[4096,128]{1,0:T(8,128)(2,1)S(1)} fusion(bf16[4352,128]{1,0:T(8,128)(2,1)S(1)} %get-tuple-element.268, s32[4096]{0:T(1024)S(1)} %fusion.48), kind=kCustom, calls=%fused_computation.clone.clone.1 | custom fusion | bytes 2113536 | tf_op jit(solution)/shard_map/while/body/eval_jaxpr/jit(_take)/gather | solution.py:38
  547.4 12.1 %gather_fusion = bf16[4096,128]{1,0:T(8,128)(2,1)S(1)} fusion(bf16[4352,128]{1,0:T(8,128)(2,1)S(1)} %get-tuple-element.268, s32[4096]{0:T(1024)S(1)} %fusion.48), kind=kCustom, calls=%fused_computation.clone.clone.1 | custom fusion | bytes 2113536 | tf_op jit(solution)/shard_map/while/body/eval_jaxpr/jit(_take)/gather | solution.py:38
  576.2 16.1 %scatter_custom_fusion = s32[4096]{0:T(1024)} fusion(s32[4096]{0:T(1024)S(1)} %compare_select_fusion.4, s32[4096]{0:T(1024)S(1)} %get-tuple-element.168, s32[]{:T(128)} %constant.89.clone.1), kind=kCustom, calls=%fused_computation.82 | custom fusion | bytes 16388 | tf_op jit(solution)/shard_map/scatter | solution.py:61
  602.4 551.5 %while.23 = (s32[]{:T(128)}, f32[4096,128]{1,0:T(8,128)}, s32[27,4096]{1,0:T(8,128)}, s32[]{:T(128)}, bf16[4352,128]{1,0:T(8,128)(2,1)S(1)}, /*index=5*/bf16[27,128,128]{2,1,0:T(8,128)(2,1)}, s32[]{:T(128)}, s32[]{:T(128)}) while((s32[]{:T(128)}, f32[4096,128]{1,0:T(8,128)}, s32[27,4096]{1,0:T(8,128)}, s32[]{:T(128)}, ...), condition=%wide.region_9.11_spmd.clone, body=%wide.region_8.10_spmd.clone.sunk | while | flops 136372224 | bytes 7512683 | solution.py:43
  604.3 12.1 %gather_fusion.1 = bf16[4096,128]{1,0:T(8,128)(2,1)S(1)} fusion(bf16[4352,128]{1,0:T(8,128)(2,1)S(1)} %get-tuple-element.292, s32[4096]{0:T(1024)S(1)} %fusion.50), kind=kCustom, calls=%fused_computation.1.clone.clone.1 | custom fusion | bytes 2113536 | tf_op jit(solution)/shard_map/while/body/eval_jaxpr/jit(_take)/gather | solution.py:38
  644.2 12.1 %gather_fusion.1 = bf16[4096,128]{1,0:T(8,128)(2,1)S(1)} fusion(bf16[4352,128]{1,0:T(8,128)(2,1)S(1)} %get-tuple-element.292, s32[4096]{0:T(1024)S(1)} %fusion.50), kind=kCustom, calls=%fused_computation.1.clone.clone.1 | custom fusion | bytes 2113536 | tf_op jit(solution)/shard_map/while/body/eval_jaxpr/jit(_take)/gather | solution.py:38
  664.7 12.1 %gather_fusion.1 = bf16[4096,128]{1,0:T(8,128)(2,1)S(1)} fusion(bf16[4352,128]{1,0:T(8,128)(2,1)S(1)} %get-tuple-element.292, s32[4096]{0:T(1024)S(1)} %fusion.50), kind=kCustom, calls=%fused_computation.1.clone.clone.1 | custom fusion | bytes 2113536 | tf_op jit(solution)/shard_map/while/body/eval_jaxpr/jit(_take)/gather | solution.py:38
  685.2 12.1 %gather_fusion.1 = bf16[4096,128]{1,0:T(8,128)(2,1)S(1)} fusion(bf16[4352,128]{1,0:T(8,128)(2,1)S(1)} %get-tuple-element.292, s32[4096]{0:T(1024)S(1)} %fusion.50), kind=kCustom, calls=%fused_computation.1.clone.clone.1 | custom fusion | bytes 2113536 | tf_op jit(solution)/shard_map/while/body/eval_jaxpr/jit(_take)/gather | solution.py:38
  705.6 12.1 %gather_fusion.1 = bf16[4096,128]{1,0:T(8,128)(2,1)S(1)} fusion(bf16[4352,128]{1,0:T(8,128)(2,1)S(1)} %get-tuple-element.292, s32[4096]{0:T(1024)S(1)} %fusion.50), kind=kCustom, calls=%fused_computation.1.clone.clone.1 | custom fusion | bytes 2113536 | tf_op jit(solution)/shard_map/while/body/eval_jaxpr/jit(_take)/gather | solution.py:38
  726.1 12.1 %gather_fusion.1 = bf16[4096,128]{1,0:T(8,128)(2,1)S(1)} fusion(bf16[4352,128]{1,0:T(8,128)(2,1)S(1)} %get-tuple-element.292, s32[4096]{0:T(1024)S(1)} %fusion.50), kind=kCustom, calls=%fused_computation.1.clone.clone.1 | custom fusion | bytes 2113536 | tf_op jit(solution)/shard_map/while/body/eval_jaxpr/jit(_take)/gather | solution.py:38
  746.5 12.1 %gather_fusion.1 = bf16[4096,128]{1,0:T(8,128)(2,1)S(1)} fusion(bf16[4352,128]{1,0:T(8,128)(2,1)S(1)} %get-tuple-element.292, s32[4096]{0:T(1024)S(1)} %fusion.50), kind=kCustom, calls=%fused_computation.1.clone.clone.1 | custom fusion | bytes 2113536 | tf_op jit(solution)/shard_map/while/body/eval_jaxpr/jit(_take)/gather | solution.py:38
  767.0 12.1 %gather_fusion.1 = bf16[4096,128]{1,0:T(8,128)(2,1)S(1)} fusion(bf16[4352,128]{1,0:T(8,128)(2,1)S(1)} %get-tuple-element.292, s32[4096]{0:T(1024)S(1)} %fusion.50), kind=kCustom, calls=%fused_computation.1.clone.clone.1 | custom fusion | bytes 2113536 | tf_op jit(solution)/shard_map/while/body/eval_jaxpr/jit(_take)/gather | solution.py:38
  787.5 12.1 %gather_fusion.1 = bf16[4096,128]{1,0:T(8,128)(2,1)S(1)} fusion(bf16[4352,128]{1,0:T(8,128)(2,1)S(1)} %get-tuple-element.292, s32[4096]{0:T(1024)S(1)} %fusion.50), kind=kCustom, calls=%fused_computation.1.clone.clone.1 | custom fusion | bytes 2113536 | tf_op jit(solution)/shard_map/while/body/eval_jaxpr/jit(_take)/gather | solution.py:38
  807.9 12.1 %gather_fusion.1 = bf16[4096,128]{1,0:T(8,128)(2,1)S(1)} fusion(bf16[4352,128]{1,0:T(8,128)(2,1)S(1)} %get-tuple-element.292, s32[4096]{0:T(1024)S(1)} %fusion.50), kind=kCustom, calls=%fused_computation.1.clone.clone.1 | custom fusion | bytes 2113536 | tf_op jit(solution)/shard_map/while/body/eval_jaxpr/jit(_take)/gather | solution.py:38
  828.4 12.1 %gather_fusion.1 = bf16[4096,128]{1,0:T(8,128)(2,1)S(1)} fusion(bf16[4352,128]{1,0:T(8,128)(2,1)S(1)} %get-tuple-element.292, s32[4096]{0:T(1024)S(1)} %fusion.50), kind=kCustom, calls=%fused_computation.1.clone.clone.1 | custom fusion | bytes 2113536 | tf_op jit(solution)/shard_map/while/body/eval_jaxpr/jit(_take)/gather | solution.py:38
  848.9 12.1 %gather_fusion.1 = bf16[4096,128]{1,0:T(8,128)(2,1)S(1)} fusion(bf16[4352,128]{1,0:T(8,128)(2,1)S(1)} %get-tuple-element.292, s32[4096]{0:T(1024)S(1)} %fusion.50), kind=kCustom, calls=%fused_computation.1.clone.clone.1 | custom fusion | bytes 2113536 | tf_op jit(solution)/shard_map/while/body/eval_jaxpr/jit(_take)/gather | solution.py:38
  869.3 12.1 %gather_fusion.1 = bf16[4096,128]{1,0:T(8,128)(2,1)S(1)} fusion(bf16[4352,128]{1,0:T(8,128)(2,1)S(1)} %get-tuple-element.292, s32[4096]{0:T(1024)S(1)} %fusion.50), kind=kCustom, calls=%fused_computation.1.clone.clone.1 | custom fusion | bytes 2113536 | tf_op jit(solution)/shard_map/while/body/eval_jaxpr/jit(_take)/gather | solution.py:38
  889.8 12.1 %gather_fusion.1 = bf16[4096,128]{1,0:T(8,128)(2,1)S(1)} fusion(bf16[4352,128]{1,0:T(8,128)(2,1)S(1)} %get-tuple-element.292, s32[4096]{0:T(1024)S(1)} %fusion.50), kind=kCustom, calls=%fused_computation.1.clone.clone.1 | custom fusion | bytes 2113536 | tf_op jit(solution)/shard_map/while/body/eval_jaxpr/jit(_take)/gather | solution.py:38
  910.3 12.1 %gather_fusion.1 = bf16[4096,128]{1,0:T(8,128)(2,1)S(1)} fusion(bf16[4352,128]{1,0:T(8,128)(2,1)S(1)} %get-tuple-element.292, s32[4096]{0:T(1024)S(1)} %fusion.50), kind=kCustom, calls=%fused_computation.1.clone.clone.1 | custom fusion | bytes 2113536 | tf_op jit(solution)/shard_map/while/body/eval_jaxpr/jit(_take)/gather | solution.py:38
  930.7 12.1 %gather_fusion.1 = bf16[4096,128]{1,0:T(8,128)(2,1)S(1)} fusion(bf16[4352,128]{1,0:T(8,128)(2,1)S(1)} %get-tuple-element.292, s32[4096]{0:T(1024)S(1)} %fusion.50), kind=kCustom, calls=%fused_computation.1.clone.clone.1 | custom fusion | bytes 2113536 | tf_op jit(solution)/shard_map/while/body/eval_jaxpr/jit(_take)/gather | solution.py:38
  951.2 12.1 %gather_fusion.1 = bf16[4096,128]{1,0:T(8,128)(2,1)S(1)} fusion(bf16[4352,128]{1,0:T(8,128)(2,1)S(1)} %get-tuple-element.292, s32[4096]{0:T(1024)S(1)} %fusion.50), kind=kCustom, calls=%fused_computation.1.clone.clone.1 | custom fusion | bytes 2113536 | tf_op jit(solution)/shard_map/while/body/eval_jaxpr/jit(_take)/gather | solution.py:38
  992.1 12.1 %gather_fusion.1 = bf16[4096,128]{1,0:T(8,128)(2,1)S(1)} fusion(bf16[4352,128]{1,0:T(8,128)(2,1)S(1)} %get-tuple-element.292, s32[4096]{0:T(1024)S(1)} %fusion.50), kind=kCustom, calls=%fused_computation.1.clone.clone.1 | custom fusion | bytes 2113536 | tf_op jit(solution)/shard_map/while/body/eval_jaxpr/jit(_take)/gather | solution.py:38
  1012.6 12.1 %gather_fusion.1 = bf16[4096,128]{1,0:T(8,128)(2,1)S(1)} fusion(bf16[4352,128]{1,0:T(8,128)(2,1)S(1)} %get-tuple-element.292, s32[4096]{0:T(1024)S(1)} %fusion.50), kind=kCustom, calls=%fused_computation.1.clone.clone.1 | custom fusion | bytes 2113536 | tf_op jit(solution)/shard_map/while/body/eval_jaxpr/jit(_take)/gather | solution.py:38
  1033.0 12.1 %gather_fusion.1 = bf16[4096,128]{1,0:T(8,128)(2,1)S(1)} fusion(bf16[4352,128]{1,0:T(8,128)(2,1)S(1)} %get-tuple-element.292, s32[4096]{0:T(1024)S(1)} %fusion.50), kind=kCustom, calls=%fused_computation.1.clone.clone.1 | custom fusion | bytes 2113536 | tf_op jit(solution)/shard_map/while/body/eval_jaxpr/jit(_take)/gather | solution.py:38
  1053.5 12.1 %gather_fusion.1 = bf16[4096,128]{1,0:T(8,128)(2,1)S(1)} fusion(bf16[4352,128]{1,0:T(8,128)(2,1)S(1)} %get-tuple-element.292, s32[4096]{0:T(1024)S(1)} %fusion.50), kind=kCustom, calls=%fused_computation.1.clone.clone.1 | custom fusion | bytes 2113536 | tf_op jit(solution)/shard_map/while/body/eval_jaxpr/jit(_take)/gather | solution.py:38
  1135.4 12.1 %gather_fusion.1 = bf16[4096,128]{1,0:T(8,128)(2,1)S(1)} fusion(bf16[4352,128]{1,0:T(8,128)(2,1)S(1)} %get-tuple-element.292, s32[4096]{0:T(1024)S(1)} %fusion.50), kind=kCustom, calls=%fused_computation.1.clone.clone.1 | custom fusion | bytes 2113536 | tf_op jit(solution)/shard_map/while/body/eval_jaxpr/jit(_take)/gather | solution.py:38
  1175.3 22.9 %all-to-all-done.1 = bf16[16,256,128]{2,1,0:T(8,128)(2,1)S(1)} async-done(((bf16[16,256,128]{2,1,0:T(8,128)(2,1)}), bf16[16,256,128]{2,1,0:T(8,128)(2,1)S(1)}, u32[]{:S(2)}, u32[]{:S(2)}) %all-to-all-start.1) | async-done | bytes 1048608 | tf_op jit(solution)/shard_map/all_to_all | solution.py:63
  (337 shorter events, 635.8 us)
Async XLA Ops:
  3.4 5.2 copy-start
  3.4 4.1 copy-start.2
  3.5 5.1 copy-start.4
  3.5 10.7 collective-permute-start
  6.2 8.1 collective-permute-start.1
  15.1 550.8 %copy-start.3 = (bf16[2,128,128]{2,1,0:T(8,128)(2,1)S(1)}, bf16[2,128,128]{2,1,0:T(8,128)(2,1)}, u32[]{:S(2)}) copy-start(bf16[2,128,128]{2,1,0:T(8,128)(2,1)} %param.16) | copy-start | bytes 196612
  568.0 1.2 copy-start.1
  569.7 31.8 %collective-permute-start.2 = (bf16[128,128]{0,1:T(8,128)(2,1)S(1)}, bf16[128,128]{0,1:T(8,128)(2,1)S(1)}, u32[]{:S(2)}, u32[]{:S(2)}) collective-permute-start(bf16[128,128]{0,1:T(8,128)(2,1)S(1)} %get-tuple-element.164), channel_id=1, source_target_pairs={{0,1},{1,2},{2,3},{3,4},{4,5},{5,6},{6,7},{7,8},{8,9},{9,10},{10,1... | collective-permute-start | bytes 98312 | tf_op jit(solution)/shard_map/ppermute | solution.py:14
  574.9 26.7 %collective-permute-start.3 = (bf16[128,128]{0,1:T(8,128)(2,1)S(1)}, bf16[128,128]{0,1:T(8,128)(2,1)S(1)}, u32[]{:S(2)}, u32[]{:S(2)}) collective-permute-start(bf16[128,128]{0,1:T(8,128)(2,1)S(1)} %get-tuple-element.165), channel_id=1, source_target_pairs={{1,0},{2,1},{3,2},{4,3},{5,4},{6,5},{7,6},{8,7},{9,8},{10,9},{11,1... | collective-permute-start | bytes 98312 | tf_op jit(solution)/shard_map/ppermute | solution.py:17
  592.3 576.9 %all-to-all-start = ((s32[16,1,256]{2,1,0:T(1,128)}), s32[16,1,256]{2,1,0:T(1,128)S(1)}, u32[]{:S(2)}, u32[]{:S(2)}) async-start(s32[16,1,256]{2,1,0:T(1,128)} %bitcast.2), calls=%async_computation | async-start | bytes 32768 | tf_op jit(solution)/shard_map/all_to_all | solution.py:70
  1169.2 29.0 %all-to-all-start.1 = ((bf16[16,256,128]{2,1,0:T(8,128)(2,1)}), bf16[16,256,128]{2,1,0:T(8,128)(2,1)S(1)}, u32[]{:S(2)}, u32[]{:S(2)}) async-start(bf16[16,256,128]{2,1,0:T(8,128)(2,1)} %bitcast.10), calls=%async_computation.1 | async-start | bytes 2097152 | tf_op jit(solution)/shard_map/all_to_all | solution.py:63
where the time goes:
time: 1220 us; the launch traced here: 1210 us
  local copies, waits for them, and re-layouts  703 us (58%)
  matrix products  346 us (28%)
  other arithmetic  111 us (9%)
  starting transfers between devices  25.6 us (2%)
  waiting for transfers between devices  22.9 us (2%)
    gather x54, local copies, waits for them, and re-layouts, offset_term(): picked = jnp.take(padded, local_rows, axis=0)  655 us
    dot_general x54, matrix products, offset_term(): jnp.dot(picked, weight, preferred_element_type=jnp.float32)  342 us
    ge x54, other arithmetic, offset_term(): present = targets >= 0  52.6 us
    sub x54, other arithmetic, offset_term(): local_rows = jnp.where(present, targets - first_row, 0)  49.8 us
  transfers between devices with their start and end apart: 6, of which 1 were waited for; matrix products, arithmetic and copies ran while one was open for 49% of the time, Pallas kernels for 0%

commit v1 on v0

v1 whole, which is shorter than its diff:
```python
import functools

import jax
import jax.numpy as jnp
from jax import lax
from jax.experimental import pallas as pl
from jax.experimental.pallas import tpu as pltpu
from jax.sharding import PartitionSpec as P

HALO = 128
BLOCK = 256
WINDOW = 512
BF16 = jnp.bfloat16
F32 = jnp.float32
ABSENT = 256
SMEM = pltpu.SMEM
VMEM = pltpu.VMEM


def params():
    return pltpu.CompilerParams(vmem_limit_bytes=48 * 1024 * 1024)


def selector(row, depth):
    shape = (depth, row.shape[1])
    places = lax.broadcasted_iota(jnp.int16, shape, 0)
    wanted = jnp.broadcast_to(row.astype(jnp.int16), shape)
    return jnp.where(places == wanted, BF16(1), BF16(0))


def dot(a, b):
    return jnp.dot(a, b, preferred_element_type=F32)


def live_lanes(first, width, rows, before, own, after):
    at = first + lax.broadcasted_iota(jnp.int32, (1, width), 1)
    limit = jnp.where(at < 0, before - rows, jnp.where(at < rows, own, after + rows))
    return at < limit


def layer_block(window, targets, weight, linear, live, picked):
    offsets = targets.shape[0]
    channels = linear.shape[0]
    static = {0: 0, offsets // 2: HALO, offsets - 1: 2 * HALO}
    for k in range(offsets):
        if k in static:
            got = window(static[k], BLOCK)
        else:
            got = dot(window(0, WINDOW), selector(targets[k : k + 1, :], WINDOW)).astype(BF16)
        picked[k * channels : (k + 1) * channels, :] = got
    convolved = dot(weight, picked[...]).astype(BF16)
    projected = dot(linear, convolved)
    average = jnp.mean(projected, axis=0, keepdims=True)
    centred = projected - average
    spread = jnp.mean(centred * centred, axis=0, keepdims=True)
    summed = window(HALO, BLOCK).astype(F32) + centred * lax.rsqrt(spread + 1e-05)
    return jnp.where(live, summed, 0.0).astype(BF16)


def turn_weights(weight_ref, turned):
    offsets, channels = weight_ref.shape[1], weight_ref.shape[2]
    for k in range(offsets):
        turned[:, k * channels : (k + 1) * channels] = weight_ref[0, k].T


def device_counts(place_ref, counts_ref):
    own = place_ref[0]
    last = counts_ref.shape[0] - 1
    before = jnp.where(own > 0, counts_ref[jnp.maximum(own - 1, 0)], 0)
    after = jnp.where(own < last, counts_ref[jnp.minimum(own + 1, last)], 0)
    return own, before, counts_ref[own], after


def slots_body(destination_ref, perm_ref, target_ref, shards):
    rows = destination_ref.shape[1]
    capacity = rows // shards
    lanes = 128
    groups = rows // lanes
    tile = 256
    earlier = (
        lax.broadcasted_iota(jnp.int32, (tile, tile), 0) < lax.broadcasted_iota(jnp.int32, (tile, tile), 1)
    ).astype(F32).astype(BF16)
    ones = jnp.ones((tile, tile), BF16)
    devices = lax.broadcasted_iota(jnp.int32, (shards, tile), 0)
    before = (devices * capacity).astype(F32)
    total = jnp.zeros((4 * groups, lanes), F32)
    for c in range(rows // tile):
        goal = destination_ref[:, c * tile : (c + 1) * tile]
        device = goal >> (rows.bit_length() - 1)
        place = goal & (rows - 1)
        member = (jnp.broadcast_to(device, (shards, tile)) == devices).astype(F32)
        member16 = member.astype(BF16)
        slot = jnp.sum(member * (dot(member16, earlier) + before), axis=0, keepdims=True).astype(jnp.int32)
        before = before + dot(member16, ones)
        row = c * tile + lax.broadcasted_iota(jnp.int32, (1, tile), 1)
        total = total + scatter_term(slot, (row, place), groups)
    perm_ref[...] = joined(total, 0, groups)
    target_ref[...] = joined(total, 1, groups)


def scatter_term(at, values, groups):
    tile = at.shape[1]
    high = (lax.broadcasted_iota(jnp.int32, (groups, tile), 0) == jnp.broadcast_to(at >> 7, (groups, tile))).astype(F32)
    low = (lax.broadcasted_iota(jnp.int32, (128, tile), 0) == jnp.broadcast_to(at & 127, (128, tile))).astype(F32)
    parts = []
    for value in values:
        parts.append(high * (value >> 6).astype(F32))
        parts.append(high * (value & 63).astype(F32))
    left = jnp.concatenate(parts, axis=0).astype(BF16)
    return lax.dot_general(left, low.astype(BF16), (((1,), (1,)), ((), ())), preferred_element_type=F32)


def joined(total, n, groups):
    high = total[2 * n * groups : (2 * n + 1) * groups, :]
    low = total[(2 * n + 1) * groups : (2 * n + 2) * groups, :]
    return (high * 64.0 + low).astype(jnp.int32)


def inner_kernel(
    shards, place_ref, counts_ref, voxels_ref, near_ref, weight_ref, linear_ref, destination_ref,
    act_ref, next_ref, perm_ref, target_ref, turned, picked,
):
    rows, channels = voxels_ref.shape
    own, before, count, after = device_counts(place_ref, counts_ref)
    slots_body(destination_ref, perm_ref, target_ref, shards)
    turn_weights(weight_ref, turned)
    for c in range(rows // BLOCK):
        live = live_lanes(c * BLOCK, BLOCK, rows, before, count, after)
        block = voxels_ref[c * BLOCK : (c + 1) * BLOCK, :].T
        act_ref[:, c * BLOCK : (c + 1) * BLOCK] = jnp.where(live, block.astype(F32), 0.0).astype(BF16)
    linear = linear_ref[0].T

    def step(b, _):
        first = pl.multiple_of(b * BLOCK, BLOCK)
        middle = pl.multiple_of(first + HALO, HALO)
        targets = jnp.maximum(near_ref[:, pl.ds(middle, BLOCK)] - (own * rows + first), -1)
        window = lambda at, n: act_ref[:, pl.ds(pl.multiple_of(first + at, HALO), n)]
        live = live_lanes(middle, BLOCK, rows, before, count, after)
        next_ref[:, pl.ds(first, BLOCK)] = layer_block(window, targets, turned[...], linear, live, picked)
        return 0

    lax.fori_loop(0, rows // BLOCK - 1, step, 0)


def outer_kernel(
    place_ref, counts_ref, low_ref, high_ref, act_ref, inner_ref, near_ref, weight0_ref, weight1_ref, linear_ref,
    perm_ref, send_ref, turned, picked, edge, padded, last,
):
    channels, rows = act_ref.shape
    own, before, count, after = device_counts(place_ref, counts_ref)
    extent = 2 * HALO
    turn_weights(weight0_ref, turned)
    linear = linear_ref[0].T
    lanes = lax.broadcasted_iota(jnp.int32, (1, HALO), 1)

    def reached(halo_ref, base):
        relative = halo_ref[extent : extent + near_ref.shape[0], :].astype(F32).astype(jnp.int32)
        return jnp.where(relative == ABSENT, -1, relative + lanes + base)

    def masked(halo_ref, first):
        live = live_lanes(first, extent, rows, before, count, after)
        return jnp.where(live, halo_ref[0:extent, :].T.astype(F32), 0.0).astype(BF16)

    window = lambda at, n: edge[:, at : at + n]

    edge[:, 0:extent] = masked(low_ref, -extent)
    edge[:, extent:] = act_ref[:, 0:extent]
    targets = jnp.concatenate(
        [reached(low_ref, HALO), jnp.maximum(near_ref[:, 0:HALO] - own * rows + extent, -1)], axis=1
    )
    live = live_lanes(-HALO, BLOCK, rows, before, count, after)
    padded[:, 0:BLOCK] = layer_block(window, targets, turned[...], linear, live, picked)

    edge[:, 0:extent] = act_ref[:, rows - extent : rows]
    edge[:, extent:] = masked(high_ref, rows)
    targets = jnp.concatenate(
        [jnp.maximum(near_ref[:, rows - HALO : rows] - own * rows - (rows - extent), -1), reached(high_ref, 2 * HALO)],
        axis=1,
    )
    live = live_lanes(rows - HALO, BLOCK, rows, before, count, after)
    padded[:, rows : rows + BLOCK] = layer_block(window, targets, turned[...], linear, live, picked)
    padded[:, BLOCK:rows] = inner_ref[...]

    turn_weights(weight1_ref, turned)
    linear = linear_ref[1].T

    def step(b, _):
        first = pl.multiple_of(b * BLOCK, BLOCK)
        targets = jnp.maximum(near_ref[:, pl.ds(first, BLOCK)] - (own * rows + first - HALO), -1)
        window = lambda at, n: padded[:, pl.ds(pl.multiple_of(first + at, HALO), n)]
        live = live_lanes(first, BLOCK, rows, before, count, after)
        last[:, pl.ds(first, BLOCK)] = layer_block(window, targets, turned[...], linear, live, picked)
        return 0

    lax.fori_loop(0, rows // BLOCK, step, 0)
    reorder(last, perm_ref, send_ref)


def reorder(source, from_ref, out_ref):
    channels, rows = source.shape

    def step(b, _):
        pair = from_ref[pl.ds(b * 2, 2), :]
        wanted = jnp.concatenate([pair[0:1, :], pair[1:2, :]], axis=1)
        total = jnp.zeros((channels, BLOCK), F32)
        for w in range(rows // WINDOW):
            total = total + dot(source[:, w * WINDOW : (w + 1) * WINDOW], selector(wanted - w * WINDOW, WINDOW))
        out_ref[pl.ds(pl.multiple_of(b * BLOCK, BLOCK), BLOCK), :] = total.astype(BF16).T
        return 0

    lax.fori_loop(0, rows // BLOCK, step, 0)


def inverse_kernel(places_ref, from_ref):
    groups = places_ref.shape[0]
    total = jnp.zeros((2 * groups, 128), F32)
    lanes = lax.broadcasted_iota(jnp.int32, (1, 128), 1)
    for g in range(groups):
        total = total + scatter_term(places_ref[g : g + 1, :], (g * 128 + lanes,), groups)
    from_ref[...] = joined(total, 0, groups)


def final_kernel(from_ref, got_ref, out_ref, turned):
    rows = got_ref.shape[0]
    for c in range(rows // BLOCK):
        turned[:, c * BLOCK : (c + 1) * BLOCK] = got_ref[c * BLOCK : (c + 1) * BLOCK, :].T
    reorder(turned, from_ref, out_ref)


def local(voxels, counts, neighbours, conv_weight, linear_weight, destination):
    rows, channels = voxels.shape
    offsets = neighbours.shape[0]
    both = ("wide", "narrow")
    shards = lax.axis_size(both)
    own = lax.axis_index(both)
    place = jnp.reshape(own, (1,)).astype(jnp.int32)
    extent = 2 * HALO
    struct = jax.ShapeDtypeStruct
    vmem = pl.BlockSpec(memory_space=VMEM)
    smem = pl.BlockSpec(memory_space=SMEM)

    def packed(first_voxel, first_near):
        near = lax.slice_in_dim(neighbours, first_near, first_near + HALO, axis=1)
        ids = own * rows + first_near + jnp.arange(HALO, dtype=jnp.int32)[None, :]
        relative = jnp.where(near >= 0, near - ids, ABSENT).astype(BF16)
        pad = jnp.zeros((32 - offsets, channels), BF16)
        return jnp.concatenate(
            [lax.slice_in_dim(voxels, first_voxel, first_voxel + extent, axis=0), relative, pad], axis=0
        )

    forward = [(i, i + 1) for i in range(shards - 1)]
    backward = [(target, source) for source, target in forward]
    low = lax.ppermute(packed(rows - extent, rows - HALO), both, forward)
    high = lax.ppermute(packed(0, 0), both, backward)

    def weight_spec(layer):
        return pl.BlockSpec((1,) + conv_weight.shape[1:], lambda i: (layer, 0, 0, 0))

    whole = lambda shape: pl.BlockSpec(shape, lambda i: (0,) * len(shape))
    act, inner, perm, target = pl.pallas_call(
        functools.partial(inner_kernel, shards),
        grid=(1,),
        out_shape=(
            struct((channels, rows), BF16),
            struct((channels, rows - BLOCK), BF16),
            struct((rows // 128, 128), jnp.int32),
            struct((rows // 128, 128), jnp.int32),
        ),
        in_specs=[
            smem, smem, whole(voxels.shape), whole(neighbours.shape), weight_spec(0), whole(linear_weight.shape),
            whole((1, rows)),
        ],
        out_specs=(
            whole((channels, rows)), whole((channels, rows - BLOCK)), whole((rows // 128, 128)), whole((rows // 128, 128)),
        ),
        scratch_shapes=[VMEM((channels, offsets * channels), BF16), VMEM((offsets * channels, BLOCK), BF16)],
        compiler_params=params(),
        cost_estimate=pl.CostEstimate(flops=20_000_000_000, bytes_accessed=6_000_000, transcendentals=0),
        name="first_layer",
    )(place, counts, voxels, neighbours, conv_weight, linear_weight, destination.reshape(1, rows))

    targets = lax.all_gather(target, both, axis=0, tiled=False)

    send = pl.pallas_call(
        outer_kernel,
        grid=(1,),
        out_shape=struct((rows, channels), BF16),
        in_specs=[
            smem, smem, whole(low.shape), whole(high.shape), whole((channels, rows)), whole((channels, rows - BLOCK)),
            whole(neighbours.shape), weight_spec(0), weight_spec(1), whole(linear_weight.shape),
            whole((rows // 128, 128)),
        ],
        out_specs=whole((rows, channels)),
        scratch_shapes=[
            VMEM((channels, offsets * channels), BF16),
            VMEM((offsets * channels, BLOCK), BF16),
            VMEM((channels, WINDOW), BF16),
            VMEM((channels, rows + 2 * HALO), BF16),
            VMEM((channels, rows), BF16),
        ],
        compiler_params=params(),
        cost_estimate=pl.CostEstimate(flops=30_000_000_000, bytes_accessed=8_000_000, transcendentals=0),
        name="second_layer",
    )(place, counts, low, high, act, inner, neighbours, conv_weight, conv_weight, linear_weight, perm)

    got = lax.all_to_all(
        send.reshape(shards, rows // shards, channels), both, split_axis=0, concat_axis=0, tiled=True
    ).reshape(rows, channels)

    per_device = rows // shards // 128
    mine = lax.dynamic_slice_in_dim(targets, own * per_device, per_device, axis=1).reshape(rows // 128, 128)
    source = pl.pallas_call(
        inverse_kernel,
        out_shape=struct((rows // 128, 128), jnp.int32),
        in_specs=[vmem],
        out_specs=vmem,
        compiler_params=params(),
        name="sources",
    )(mine)
    return pl.pallas_call(
        final_kernel,
        out_shape=struct((rows, channels), BF16),
        in_specs=[vmem, vmem],
        out_specs=vmem,
        scratch_shapes=[VMEM((channels, rows), BF16)],
        compiler_params=params(),
        name="hilbert_order",
    )(source, got)


def solution(mesh):
    in_specs = (
        P(("groups", "wide", "narrow"), None),
        P("groups"),
        P(None, ("groups", "wide", "narrow")),
        P(),
        P(),
        P(("groups", "wide", "narrow")),
    )
    out_specs = P(("groups", "wide", "narrow"), None)
    return jax.shard_map(local, mesh=mesh, in_specs=in_specs, out_specs=out_specs, check_vma=False)
```

time: 1220 us -> 131 us (0.11)
  local copies, waits for them, and re-layouts: 703 us -> 6.93 us
  matrix products: 346 us -> 0 us
  other arithmetic: 111 us -> 0.86 us
  Pallas kernels: 0 us -> 75.4 us
  blocking collectives: 0 us -> 34.5 us
  waiting for transfers between devices: 22.9 us -> 0.01 us
  starting transfers between devices: 25.6 us -> 12.3 us
    gather x54 -> x0, local copies, waits for them, and re-layouts: 655 us -> none  [offset_term(): picked = jnp.take(padded, local_rows, axis=0)]
    dot_general x56 -> x0, matrix products: 346 us -> none  [the longest x54 342 us: offset_term(): jnp.dot(picked, weight, preferred_element_type=jnp.float32)]
    pallas_call x0 -> x4, Pallas kernels: none -> 75.4 us  [the longest x1 38.8 us: local(): pl.pallas_call(outer_kernel, grid=(1,), out_shape=struct((rows, channels)...]
    ge x54 -> x0, other arithmetic: 52.6 us -> none  [offset_term(): present = targets >= 0]
    sub x55 -> x0, other arithmetic: 49.9 us -> none  [the longest x54 49.8 us: offset_term(): local_rows = jnp.where(present, targets - first_row, 0)]
    scatter x3 -> x0, local copies, waits for them, and re-layouts: 39.1 us -> none  [the longest x1 16.1 us: local(): jnp.full((shards * capacity,), -1, jnp.int32).at[slot_ids].set(target_row)]
    all_gather x0 -> x1, blocking collectives: none -> 34.5 us  [local(): targets = lax.all_gather(target, both, axis=0, tiled=False)]
    all_to_all x2 -> x1, waiting for transfers between devices: 22.9 us -> 0.01 us  [local(): lax.all_to_all(send.reshape(shards, rows // shards, channels), both, spli...]
  transfers between devices with their start and end apart: 6 -> 3, of which waited for: 1 -> 0; matrix products, arithmetic and copies ran while one was open for 49% -> 0% of each run, Pallas kernels for 0% -> 21%
where the time goes in v1:
time: 131 us; the launch traced here: 130 us
  Pallas kernels  75.4 us (58%)
  blocking collectives  34.5 us (26%)
  starting transfers between devices  12.3 us (9%)
  local copies, waits for them, and re-layouts  6.93 us (5%)
    pallas_call x1, Pallas kernels, local(): pl.pallas_call(outer_kernel, grid=(1,), out_shape=struct((rows, channels)...  38.8 us
    all_gather x1, blocking collectives, local(): targets = lax.all_gather(target, both, axis=0, tiled=False)  34.5 us
    pallas_call x1, Pallas kernels, local(): pl.pallas_call(functools.partial(inner_kernel, shards), grid=(1,), out_sh...  26.4 us
    pallas_call x1, Pallas kernels, local(): pl.pallas_call(final_kernel, out_shape=struct((rows, channels), BF16), in...  9.38 us
    all_to_all x1, starting transfers between devices, local(): lax.all_to_all(send.reshape(shards, rows // shards, channels), both, spli...  7.95 us
    unnamed x18, local copies, waits for them, and re-layouts  5.96 us
    ppermute x1, starting transfers between devices, local(): low = lax.ppermute(packed(rows - extent, rows - HALO), both, forward)  3.03 us
  transfers between devices with their start and end apart: 3, of which 0 were waited for; matrix products, arithmetic and copies ran while one was open for 0% of the time, Pallas kernels for 21%

profile of v1, /device:TPU:0, one launch (start us, length us, event | category | flops | bytes accessed | tf_op | source)
XLA Modules:
  0.0 130.1 jit_solution(14141210477113768417)
XLA Ops:
  0.0 0.9 fusion
  0.9 0.1 pad.5.clone
  1.0 0.7 select_convert_fusion
  1.7 0.1 maximum_maximum_fusion.1
  1.8 1.3 collective-permute-start.1
  3.1 3.0 %collective-permute-start = (bf16[288,128]{1,0:T(8,128)(2,1)S(1)}, bf16[288,128]{1,0:T(8,128)(2,1)S(1)}, u32[]{:S(2)}, u32[]{:S(2)}) collective-permute-start(bf16[288,128]{1,0:T(8,128)(2,1)S(1)} %get-tuple-element.18), channel_id=1, source_target_pairs={{0,1},{1,2},{2,3},{3,4},{4,5},{5,6},{6,7},{7,8},{8,9},{9,10},{10,1... | collective-permute-start | bytes 221192 | tf_op jit(solution)/shard_map/ppermute | solution.py:253
  6.2 0.0 copy-start
  6.2 1.2 copy-done
  7.4 0.0 copy-start.1
  7.4 1.0 copy-done.1
  8.5 0.0 copy-start.3
  8.5 1.5 %copy-done.3 = bf16[2,27,128,128]{3,2,1,0:T(8,128)(2,1)S(1)} copy-done((bf16[2,27,128,128]{3,2,1,0:T(8,128)(2,1)S(1)}, bf16[2,27,128,128]{3,2,1,0:T(8,128)(2,1)}, u32[]{:S(2)}) %copy-start.3) | copy-done | bytes 1769496
  9.9 0.0 copy-start.5
  9.9 0.8 copy-done.5
  10.8 0.0 copy-start.7
  10.8 0.7 copy-done.7
  11.5 0.0 copy-start.8
  11.5 0.7 copy-done.8
  12.1 0.0 copy-start.2
  12.1 0.0 copy-start.4
  12.1 0.0 copy-start.6
  12.2 26.4 %first_layer.1 = (bf16[128,4096]{1,0:T(8,128)(2,1)S(1)}, bf16[128,3840]{1,0:T(8,128)(2,1)S(1)}, s32[32,128]{1,0:T(8,128)S(1)}, s32[32,128]{1,0:T(8,128)S(1)}) custom-call(s32[1]{0:T(128)} %bitcast.place_ref, s32[16]{0:T(128)S(1)} %copy-done.8, bf16[4096,128]{1,0:T(8,128)(2,1)S(1)} %copy-done, s32[27,4096]{1,0:T(8,128)S(1)} %copy-done.1, ...), custom_call_target="tpu_custom_call" | custom-call | flops 20000000000 | bytes 6000000 | tf_op jit(solution)/shard_map/first_layer/pallas_call | solution.py:260
  38.5 0.0 collective-permute-done.1.high_ref
  38.5 0.0 collective-permute-done.low_ref
  38.5 0.0 copy-done.2
  38.6 0.0 copy-done.4
  38.6 0.0 copy-done.6
  38.6 38.8 %second_layer.1 = bf16[4096,128]{1,0:T(8,128)(2,1)} custom-call(s32[1]{0:T(128)} %bitcast.place_ref, s32[16]{0:T(128)S(1)} %copy-done.8, bf16[288,128]{1,0:T(8,128)(2,1)S(1)} %collective-permute-done.low_ref, bf16[288,128]{1,0:T(8,128)(2,1)S(1)} %collective-permute-done.1.high_ref, bf16[128,4096]{1,0:T(8,128)(2,1)S(1)} %get-tuple-element.10.act_ref, ...), custom_call_target="tpu_custom_call" | custom-call | flops 30000001024 | bytes 8000000 | tf_op jit(solution)/shard_map/second_layer/pallas_call | solution.py:284
  77.4 7.9 %all-to-all-start = ((bf16[16,256,128]{2,1,0:T(8,128)(2,1)}), bf16[16,256,128]{2,1,0:T(8,128)(2,1)S(1)}, u32[]{:S(2)}, u32[]{:S(2)}) async-start(bf16[16,256,128]{2,1,0:T(8,128)(2,1)} %bitcast.4), calls=%async_computation | async-start | bytes 2097152 | tf_op jit(solution)/shard_map/all_to_all | solution.py:306
  85.3 34.5 %all-gather = s32[512,128]{1,0:T(8,128)S(1)} all-gather(s32[32,128]{1,0:T(8,128)S(1)} %get-tuple-element.9), channel_id=2, replica_groups=mesh['groups'=2,'wide'=8,'narrow'=2] {'wide','narrow'}, dimensions={0}, use_global_device_ids=true | all-gather | bytes 278528 | tf_op jit(solution)/shard_map/all_gather | solution.py:282
  119.8 0.8 sources.1.from_ref
  120.7 0.0 all-to-all-done
  120.7 9.4 %hilbert_order.1 = bf16[4096,128]{1,0:T(8,128)(2,1)} custom-call(s32[32,128]{1,0:T(8,128)S(1)} %sources.1.from_ref, bf16[4096,128]{1,0:T(8,128)(2,1)S(1)} %bitcast.6), custom_call_target="tpu_custom_call" | custom-call | tf_op jit(solution)/shard_map/hilbert_order/pallas_call | solution.py:320
  (4 shorter events, 0.0 us)
Async XLA Ops:
  1.8 36.7 %collective-permute-start.1 = (bf16[288,128]{1,0:T(8,128)(2,1)S(1)}, bf16[288,128]{1,0:T(8,128)(2,1)S(1)}, u32[]{:S(2)}, u32[]{:S(2)}) collective-permute-start(bf16[288,128]{1,0:T(8,128)(2,1)S(1)} %get-tuple-element.17), channel_id=1, source_target_pairs={{1,0},{2,1},{3,2},{4,3},{5,4},{6,5},{7,6},{8,7},{9,8},{10,9},{11,1... | collective-permute-start | bytes 221192 | tf_op jit(solution)/shard_map/ppermute | solution.py:254
  3.1 35.4 %collective-permute-start = (bf16[288,128]{1,0:T(8,128)(2,1)S(1)}, bf16[288,128]{1,0:T(8,128)(2,1)S(1)}, u32[]{:S(2)}, u32[]{:S(2)}) collective-permute-start(bf16[288,128]{1,0:T(8,128)(2,1)S(1)} %get-tuple-element.18), channel_id=1, source_target_pairs={{0,1},{1,2},{2,3},{3,4},{4,5},{5,6},{6,7},{7,8},{8,9},{9,10},{10,1... | collective-permute-start | bytes 221192 | tf_op jit(solution)/shard_map/ppermute | solution.py:253
  6.2 1.2 copy-start
  7.4 1.0 copy-start.1
  8.5 1.5 %copy-start.3 = (bf16[2,27,128,128]{3,2,1,0:T(8,128)(2,1)S(1)}, bf16[2,27,128,128]{3,2,1,0:T(8,128)(2,1)}, u32[]{:S(2)}) copy-start(bf16[2,27,128,128]{3,2,1,0:T(8,128)(2,1)} %weight1_ref.1) | copy-start | bytes 5308420
  9.9 0.8 copy-start.5
  10.8 0.7 copy-start.7
  11.5 0.7 copy-start.8
  12.1 26.4 %copy-start.2 = (s32[27,4096]{1,0:T(8,128)S(1)}, s32[27,4096]{1,0:T(8,128)}, u32[]{:S(2)}) copy-start(s32[27,4096]{1,0:T(8,128)} %near_ref.3) | copy-start | bytes 1327108
  12.1 26.4 %copy-start.4 = (bf16[2,27,128,128]{3,2,1,0:T(8,128)(2,1)S(1)}, bf16[2,27,128,128]{3,2,1,0:T(8,128)(2,1)}, u32[]{:S(2)}) copy-start(bf16[2,27,128,128]{3,2,1,0:T(8,128)(2,1)} %weight1_ref.1) | copy-start | bytes 5308420
  12.1 26.4 %copy-start.6 = (bf16[2,128,128]{2,1,0:T(8,128)(2,1)S(1)}, bf16[2,128,128]{2,1,0:T(8,128)(2,1)}, u32[]{:S(2)}) copy-start(bf16[2,128,128]{2,1,0:T(8,128)(2,1)} %linear_ref.3) | copy-start | bytes 196612
  77.4 43.3 %all-to-all-start = ((bf16[16,256,128]{2,1,0:T(8,128)(2,1)}), bf16[16,256,128]{2,1,0:T(8,128)(2,1)S(1)}, u32[]{:S(2)}, u32[]{:S(2)}) async-start(bf16[16,256,128]{2,1,0:T(8,128)(2,1)} %bitcast.4), calls=%async_computation | async-start | bytes 2097152 | tf_op jit(solution)/shard_map/all_to_all | solution.py:306

commit v2 on v1

v2 whole, which is shorter than its diff:
```python
import functools

import jax
import jax.numpy as jnp
from jax import lax
from jax.experimental import pallas as pl
from jax.experimental.pallas import tpu as pltpu
from jax.sharding import PartitionSpec as P

HALO = 128
BLOCK = 256
WINDOW = 512
BF16 = jnp.bfloat16
F32 = jnp.float32
ABSENT = 256
SMEM = pltpu.SMEM
VMEM = pltpu.VMEM


def params():
    return pltpu.CompilerParams(vmem_limit_bytes=48 * 1024 * 1024)


def selector(row, depth):
    shape = (depth, row.shape[1])
    places = lax.broadcasted_iota(jnp.int16, shape, 0)
    wanted = jnp.broadcast_to(row.astype(jnp.int16), shape)
    return jnp.where(places == wanted, BF16(1), BF16(0))


def dot(a, b):
    return jnp.dot(a, b, preferred_element_type=F32)


def live_lanes(first, width, rows, before, own, after):
    at = first + lax.broadcasted_iota(jnp.int32, (1, width), 1)
    limit = jnp.where(at < 0, before - rows, jnp.where(at < rows, own, after + rows))
    return at < limit


def lane_pick(block, lanes):
    numbers = lax.GatherDimensionNumbers(
        offset_dims=(), collapsed_slice_dims=(1,), start_index_map=(1,),
        operand_batching_dims=(0,), start_indices_batching_dims=(0,),
    )
    index = jnp.broadcast_to(lanes.astype(jnp.int16), block.shape)
    return lax.gather(block, index[..., None], numbers, (1, 1), mode=lax.GatherScatterMode.PROMISE_IN_BOUNDS)


def gather_block(window, targets, picked):
    offsets = targets.shape[0]
    channels = picked.shape[0] // offsets
    static = {0: 0, offsets // 2: HALO, offsets - 1: 2 * HALO}
    turn = 0
    for k in range(offsets):
        at = slice(k * channels, (k + 1) * channels)
        if k in static:
            picked[at, :] = window(static[k], BLOCK)
            continue
        turn += 1
        row = targets[k : k + 1, :]
        if turn % 2:
            picked[at, :] = dot(window(0, WINDOW), selector(row, WINDOW)).astype(BF16)
            continue
        for half in range(2):
            part = row[:, half * HALO : (half + 1) * HALO]
            lanes = part & (HALO - 1)
            chunk = jnp.broadcast_to((part >> 7).astype(jnp.int16), (channels, HALO))
            total = jnp.zeros((channels, HALO), BF16)
            for j in range(half, half + 3):
                total = jnp.where(chunk == j, lane_pick(window(j * HALO, HALO), lanes), total)
            picked[at, half * HALO : (half + 1) * HALO] = total


def finish_block(current, weight, linear, live, picked):
    convolved = dot(weight, picked[...]).astype(BF16)
    projected = dot(linear, convolved)
    average = jnp.mean(projected, axis=0, keepdims=True)
    centred = projected - average
    spread = jnp.mean(centred * centred, axis=0, keepdims=True)
    summed = current.astype(F32) + centred * lax.rsqrt(spread + 1e-05)
    return jnp.where(live, summed, 0.0).astype(BF16)


def turn_weights(weight_ref, turned):
    offsets, channels = weight_ref.shape[1], weight_ref.shape[2]
    for k in range(offsets):
        turned[:, k * channels : (k + 1) * channels] = weight_ref[0, k].T


def device_counts(place_ref, counts_ref):
    own = place_ref[0]
    last = counts_ref.shape[0] - 1
    before = jnp.where(own > 0, counts_ref[jnp.maximum(own - 1, 0)], 0)
    after = jnp.where(own < last, counts_ref[jnp.minimum(own + 1, last)], 0)
    return own, before, counts_ref[own], after


def slots_body(destination_ref, perm_ref, high_ref, low_ref, shards):
    rows = destination_ref.shape[1]
    capacity = rows // shards
    lanes = 128
    groups = rows // lanes
    tile = 256
    earlier = (
        lax.broadcasted_iota(jnp.int32, (tile, tile), 0) < lax.broadcasted_iota(jnp.int32, (tile, tile), 1)
    ).astype(F32).astype(BF16)
    ones = jnp.ones((tile, tile), BF16)
    devices = lax.broadcasted_iota(jnp.int32, (shards, tile), 0)
    before = (devices * capacity).astype(F32)
    total = jnp.zeros((4 * groups, lanes), F32)
    for c in range(rows // tile):
        goal = destination_ref[:, c * tile : (c + 1) * tile]
        device = goal >> (rows.bit_length() - 1)
        place = goal & (rows - 1)
        member = (jnp.broadcast_to(device, (shards, tile)) == devices).astype(F32)
        member16 = member.astype(BF16)
        slot = jnp.sum(member * (dot(member16, earlier) + before), axis=0, keepdims=True).astype(jnp.int32)
        before = before + dot(member16, ones)
        row = c * tile + lax.broadcasted_iota(jnp.int32, (1, tile), 1)
        total = total + scatter_term(slot, (row, place), groups)
    perm_ref[...] = joined(total, 0, groups)
    high_ref[...] = total[2 * groups : 3 * groups, :]
    low_ref[...] = total[3 * groups :, :]


def scatter_term(at, values, groups):
    tile = at.shape[1]
    high = (lax.broadcasted_iota(jnp.int32, (groups, tile), 0) == jnp.broadcast_to(at >> 7, (groups, tile))).astype(F32)
    low = (lax.broadcasted_iota(jnp.int32, (128, tile), 0) == jnp.broadcast_to(at & 127, (128, tile))).astype(F32)
    parts = []
    for value in values:
        parts.append(high * (value >> 6).astype(F32))
        parts.append(high * (value & 63).astype(F32))
    left = jnp.concatenate(parts, axis=0).astype(BF16)
    return lax.dot_general(left, low.astype(BF16), (((1,), (1,)), ((), ())), preferred_element_type=F32)


def joined(total, n, groups):
    high = total[2 * n * groups : (2 * n + 1) * groups, :]
    low = total[(2 * n + 1) * groups : (2 * n + 2) * groups, :]
    return (high * 64.0 + low).astype(jnp.int32)


def inner_kernel(
    shards, place_ref, counts_ref, voxels_ref, near_ref, weight_ref, linear_ref, destination_ref,
    act_ref, next_ref, perm_ref, high_ref, low_ref, turned, even, odd,
):
    rows, channels = voxels_ref.shape
    own, before, count, after = device_counts(place_ref, counts_ref)
    slots_body(destination_ref, perm_ref, high_ref, low_ref, shards)
    turn_weights(weight_ref, turned)
    for c in range(rows // BLOCK):
        live = live_lanes(c * BLOCK, BLOCK, rows, before, count, after)
        block = voxels_ref[c * BLOCK : (c + 1) * BLOCK, :].T
        act_ref[:, c * BLOCK : (c + 1) * BLOCK] = jnp.where(live, block.astype(F32), 0.0).astype(BF16)
    linear = linear_ref[0].T

    def gather(b, picked):
        first = pl.multiple_of((b - 1) * BLOCK, BLOCK)
        targets = jnp.maximum(near_ref[:, pl.ds(pl.multiple_of(first + HALO, HALO), BLOCK)] - (own * rows + first), -1)
        gather_block(lambda at, n: act_ref[:, pl.ds(pl.multiple_of(first + at, HALO), n)], targets, picked)

    def finish(b, picked):
        first = b * BLOCK - HALO
        current = act_ref[:, pl.ds(pl.multiple_of(jnp.maximum(first, 0), HALO), BLOCK)]
        live = live_lanes(first, BLOCK, rows, before, count, after)
        next_ref[:, pl.ds(pl.multiple_of(b * BLOCK, BLOCK), BLOCK)] = finish_block(
            current, turned[...], linear, live, picked
        )

    blocks = rows // BLOCK
    odd[...] = jnp.zeros_like(odd)

    def step(t, _):
        gather(2 * t + 1, even)
        finish(2 * t, odd)
        gather(2 * t + 2, odd)
        finish(2 * t + 1, even)
        return 0

    lax.fori_loop(0, (blocks - 2) // 2, step, 0)
    gather(blocks - 1, even)
    finish(blocks - 2, odd)
    finish(blocks - 1, even)


def outer_kernel(
    place_ref, counts_ref, low_ref, high_ref, act_ref, inner_ref, near_ref, weight0_ref, weight1_ref, linear_ref,
    perm_ref, place_high_ref, place_low_ref, send_ref, turned, even, odd, edge, padded, last,
):
    channels, rows = act_ref.shape
    own, before, count, after = device_counts(place_ref, counts_ref)
    extent = 2 * HALO
    turn_weights(weight0_ref, turned)
    linear = linear_ref[0].T
    lanes = lax.broadcasted_iota(jnp.int32, (1, HALO), 1)

    def reached(halo_ref, base):
        relative = halo_ref[extent : extent + near_ref.shape[0], :].astype(F32).astype(jnp.int32)
        return jnp.where(relative == ABSENT, -1, relative + lanes + base)

    def masked(halo_ref, first):
        live = live_lanes(first, extent, rows, before, count, after)
        return jnp.where(live, halo_ref[0:extent, :].T.astype(F32), 0.0).astype(BF16)

    edges = (edge.at[:, 0:WINDOW], edge.at[:, WINDOW:])
    edges[0][:, 0:extent] = masked(low_ref, -extent)
    edges[0][:, extent:] = act_ref[:, 0:extent]
    edges[1][:, 0:extent] = act_ref[:, rows - extent : rows]
    edges[1][:, extent:] = masked(high_ref, rows)
    near = (
        jnp.concatenate(
            [reached(low_ref, HALO), jnp.maximum(near_ref[:, 0:HALO] - own * rows + extent, -1)], axis=1
        ),
        jnp.concatenate(
            [
                jnp.maximum(near_ref[:, rows - HALO : rows] - own * rows - (rows - extent), -1),
                reached(high_ref, 2 * HALO),
            ],
            axis=1,
        ),
    )
    picks = (even, odd)
    for n in range(2):
        gather_block(lambda at, size: edges[n][:, at : at + size], near[n], picks[n])
    for n in range(2):
        at = n * rows
        live = live_lanes(at - HALO, BLOCK, rows, before, count, after)
        padded[:, at : at + BLOCK] = finish_block(
            edges[n][:, HALO : HALO + BLOCK], turned[...], linear, live, picks[n]
        )
    padded[:, BLOCK:rows] = inner_ref[:, BLOCK:rows]

    turn_weights(weight1_ref, turned)
    linear = linear_ref[1].T

    def gather(b, picked):
        first = pl.multiple_of(b * BLOCK, BLOCK)
        targets = jnp.maximum(near_ref[:, pl.ds(first, BLOCK)] - (own * rows + first - HALO), -1)
        gather_block(lambda at, n: padded[:, pl.ds(pl.multiple_of(first + at, HALO), n)], targets, picked)

    def finish(b, picked):
        first = b * BLOCK
        current = padded[:, pl.ds(pl.multiple_of(jnp.maximum(first, 0) + HALO, HALO), BLOCK)]
        live = live_lanes(first, BLOCK, rows, before, count, after)
        last[:, pl.ds(pl.multiple_of(first + BLOCK, BLOCK), BLOCK)] = finish_block(
            current, turned[...], linear, live, picked
        )

    def step(t, _):
        gather(2 * t, even)
        finish(2 * t - 1, odd)
        gather(2 * t + 1, odd)
        finish(2 * t, even)
        return 0

    lax.fori_loop(0, rows // BLOCK // 2, step, 0)
    finish(rows // BLOCK - 1, odd)

    shards, depth, _ = send_ref.shape
    capacity = rows // shards
    pieces = BLOCK // capacity

    def store(b, block):
        for p in range(pieces):
            send_ref[b * pieces + p, 0:capacity, :] = block[p * capacity : (p + 1) * capacity, :]

    reorder(last.at[:, BLOCK:], perm_ref, store)
    held = capacity // 128
    pad = jnp.zeros((depth - capacity - 2 * held, 128), F32)
    for d in range(shards):
        at = slice(d * held, (d + 1) * held)
        extra = jnp.concatenate([place_high_ref[at, :], place_low_ref[at, :], pad], axis=0)
        send_ref[d, capacity:, :] = extra.astype(BF16)


def reorder(source, from_ref, store):
    channels, rows = source.shape
    unroll = 4

    def one(b):
        pair = from_ref[pl.ds(b * 2, 2), :]
        wanted = jnp.concatenate([pair[0:1, :], pair[1:2, :]], axis=1)
        total = jnp.zeros((channels, BLOCK), F32)
        for w in range(rows // WINDOW):
            total = total + dot(source[:, w * WINDOW : (w + 1) * WINDOW], selector(wanted - w * WINDOW, WINDOW))
        store(b, total.astype(BF16).T)

    def step(t, _):
        for u in range(unroll):
            one(t * unroll + u)
        return 0

    lax.fori_loop(0, rows // BLOCK // unroll, step, 0)


def final_kernel(got_ref, out_ref, turned, from_ref):
    rows = out_ref.shape[0]
    shards = got_ref.shape[0]
    groups = rows // 128
    capacity = rows // shards
    held = capacity // 128
    lanes = lax.broadcasted_iota(jnp.int32, (1, 128), 1)
    total = jnp.zeros((2 * groups, 128), F32)
    for s in range(shards):
        turned[:, s * capacity : (s + 1) * capacity] = got_ref[s, 0:capacity, :].T
        extra = got_ref[s, capacity:, :].astype(F32)
        place = (extra[0:held, :] * 64.0 + extra[held : 2 * held, :]).astype(jnp.int32)
        for h in range(held):
            total = total + scatter_term(place[h : h + 1, :], (s * capacity + h * 128 + lanes,), groups)
    from_ref[...] = joined(total, 0, groups)

    def store(b, block):
        out_ref[pl.ds(pl.multiple_of(b * BLOCK, BLOCK), BLOCK), :] = block

    reorder(turned, from_ref, store)


def local(voxels, counts, neighbours, conv_weight, linear_weight, destination):
    rows, channels = voxels.shape
    offsets = neighbours.shape[0]
    both = ("wide", "narrow")
    shards = lax.axis_size(both)
    own = lax.axis_index(both)
    place = jnp.reshape(own, (1,)).astype(jnp.int32)
    extent = 2 * HALO
    struct = jax.ShapeDtypeStruct
    vmem = pl.BlockSpec(memory_space=VMEM)
    smem = pl.BlockSpec(memory_space=SMEM)

    def packed(first_voxel, first_near):
        near = lax.slice_in_dim(neighbours, first_near, first_near + HALO, axis=1)
        ids = own * rows + first_near + jnp.arange(HALO, dtype=jnp.int32)[None, :]
        relative = jnp.where(near >= 0, near - ids, ABSENT).astype(BF16)
        pad = jnp.zeros((32 - offsets, channels), BF16)
        return jnp.concatenate(
            [lax.slice_in_dim(voxels, first_voxel, first_voxel + extent, axis=0), relative, pad], axis=0
        )

    forward = [(i, i + 1) for i in range(shards - 1)]
    backward = [(target, source) for source, target in forward]
    low = lax.ppermute(packed(rows - extent, rows - HALO), both, forward)
    high = lax.ppermute(packed(0, 0), both, backward)

    def weight_spec(layer):
        return pl.BlockSpec((1,) + conv_weight.shape[1:], lambda i: (layer, 0, 0, 0))

    whole = lambda shape: pl.BlockSpec(shape, lambda i: (0,) * len(shape))
    table = (rows // 128, 128)
    padded = (channels, rows + BLOCK)
    picked = VMEM((offsets * channels, BLOCK), BF16)
    turned = VMEM((channels, offsets * channels), BF16)
    act, inner, perm, place_high, place_low = pl.pallas_call(
        functools.partial(inner_kernel, shards),
        grid=(1,),
        out_shape=(
            struct((channels, rows), BF16), struct(padded, BF16), struct(table, jnp.int32), struct(table, F32),
            struct(table, F32),
        ),
        in_specs=[
            smem, smem, whole(voxels.shape), whole(neighbours.shape), weight_spec(0), whole(linear_weight.shape),
            whole((1, rows)),
        ],
        out_specs=(whole((channels, rows)), whole(padded), whole(table), whole(table), whole(table)),
        scratch_shapes=[turned, picked, picked],
        compiler_params=params(),
        cost_estimate=pl.CostEstimate(flops=20_000_000_000, bytes_accessed=6_000_000, transcendentals=0),
        name="first_layer",
    )(place, counts, voxels, neighbours, conv_weight, linear_weight, destination.reshape(1, rows))

    depth = rows // shards + 16
    send = pl.pallas_call(
        outer_kernel,
        grid=(1,),
        out_shape=struct((shards, depth, channels), BF16),
        in_specs=[
            smem, smem, whole(low.shape), whole(high.shape), whole((channels, rows)), whole(padded),
            whole(neighbours.shape), weight_spec(0), weight_spec(1), whole(linear_weight.shape),
            whole(table), whole(table), whole(table),
        ],
        out_specs=whole((shards, depth, channels)),
        scratch_shapes=[
            turned,
            picked,
            picked,
            VMEM((channels, 2 * WINDOW), BF16),
            VMEM(padded, BF16),
            VMEM(padded, BF16),
        ],
        compiler_params=params(),
        cost_estimate=pl.CostEstimate(flops=30_000_000_000, bytes_accessed=8_000_000, transcendentals=0),
        name="second_layer",
    )(
        place, counts, low, high, act, inner, neighbours, conv_weight, conv_weight, linear_weight, perm, place_high,
        place_low,
    )

    got = lax.all_to_all(send, both, split_axis=0, concat_axis=0, tiled=True)
    return pl.pallas_call(
        final_kernel,
        out_shape=struct((rows, channels), BF16),
        in_specs=[vmem],
        out_specs=vmem,
        scratch_shapes=[VMEM((channels, rows), BF16), VMEM(table, jnp.int32)],
        compiler_params=params(),
        name="hilbert_order",
    )(got)


def solution(mesh):
    in_specs = (
        P(("groups", "wide", "narrow"), None),
        P("groups"),
        P(None, ("groups", "wide", "narrow")),
        P(),
        P(),
        P(("groups", "wide", "narrow")),
    )
    out_specs = P(("groups", "wide", "narrow"), None)
    return jax.shard_map(local, mesh=mesh, in_specs=in_specs, out_specs=out_specs, check_vma=False)
```

time: 131 us -> 112 us (0.85)
  Pallas kernels: 75.4 us -> 62.8 us
  starting transfers between devices: 12.3 us -> 4.33 us
  blocking collectives: 34.5 us -> 36.3 us
    all_to_all x0 -> x1, blocking collectives: none -> 36.3 us  [local(): got = lax.all_to_all(send, both, split_axis=0, concat_axis=0, tiled=True)]
    all_gather x1 -> x0, blocking collectives: 34.5 us -> none  [local(): targets = lax.all_gather(target, both, axis=0, tiled=False)]
    pallas_call x2 -> x1, Pallas kernels: 39.6 us -> 31.5 us  [local(): pl.pallas_call(outer_kernel, grid=(1,), out_shape=struct((shards, depth,...]
    all_to_all x1 -> x0, starting transfers between devices: 7.95 us -> none  [local(): lax.all_to_all(send.reshape(shards, rows // shards, channels), both, spli...]
    pallas_call x1, Pallas kernels: 26.4 us -> 24.1 us  [local(): pl.pallas_call(functools.partial(inner_kernel, shards), grid=(1,), out_sh...]
    pallas_call x1, Pallas kernels: 9.38 us -> 7.15 us  [local(): pl.pallas_call(final_kernel, out_shape=struct((rows, channels), BF16), in...]
  transfers between devices with their start and end apart: 3 -> 2, of which waited for: 0 -> 0; matrix products, arithmetic and copies ran while one was open for 0% -> 0% of each run, Pallas kernels for 21% -> 22%
where the time goes in v2:
time: 112 us; the launch traced here: 111 us
  Pallas kernels  62.8 us (56%)
  blocking collectives  36.3 us (32%)
  local copies, waits for them, and re-layouts  6.92 us (6%)
  starting transfers between devices  4.33 us (4%)
    all_to_all x1, blocking collectives, local(): got = lax.all_to_all(send, both, split_axis=0, concat_axis=0, tiled=True)  36.3 us
    pallas_call x1, Pallas kernels, local(): pl.pallas_call(outer_kernel, grid=(1,), out_shape=struct((shards, depth,...  31.5 us
    pallas_call x1, Pallas kernels, local(): pl.pallas_call(functools.partial(inner_kernel, shards), grid=(1,), out_sh...  24.1 us
    pallas_call x1, Pallas kernels, local(): pl.pallas_call(final_kernel, out_shape=struct((rows, channels), BF16), in...  7.15 us
    unnamed x18, local copies, waits for them, and re-layouts  5.96 us
    ppermute x1, starting transfers between devices, local(): low = lax.ppermute(packed(rows - extent, rows - HALO), both, forward)  3.03 us
  transfers between devices with their start and end apart: 2, of which 0 were waited for; matrix products, arithmetic and copies ran while one was open for 0% of the time, Pallas kernels for 22%

profile of v2, /device:TPU:0, one launch (start us, length us, event | category | flops | bytes accessed | tf_op | source)
XLA Modules:
  0.0 111.3 jit_solution(17773517492421204909)
XLA Ops:
  0.0 0.9 fusion
  0.9 0.1 pad.5.clone
  1.0 0.7 select_convert_fusion
  1.7 0.1 maximum_maximum_fusion.1
  1.8 1.3 %collective-permute-start.1 = (bf16[288,128]{1,0:T(8,128)(2,1)S(1)}, bf16[288,128]{1,0:T(8,128)(2,1)S(1)}, u32[]{:S(2)}, u32[]{:S(2)}) collective-permute-start(bf16[288,128]{1,0:T(8,128)(2,1)S(1)} %get-tuple-element.19), channel_id=1, source_target_pairs={{1,0},{2,1},{3,2},{4,3},{5,4},{6,5},{7,6},{8,7},{9,8},{10,9},{11,1... | collective-permute-start | bytes 221192 | tf_op jit(solution)/shard_map/ppermute | solution.py:344
  3.1 3.0 %collective-permute-start = (bf16[288,128]{1,0:T(8,128)(2,1)S(1)}, bf16[288,128]{1,0:T(8,128)(2,1)S(1)}, u32[]{:S(2)}, u32[]{:S(2)}) collective-permute-start(bf16[288,128]{1,0:T(8,128)(2,1)S(1)} %get-tuple-element.20), channel_id=1, source_target_pairs={{0,1},{1,2},{2,3},{3,4},{4,5},{5,6},{6,7},{7,8},{8,9},{9,10},{10,1... | collective-permute-start | bytes 221192 | tf_op jit(solution)/shard_map/ppermute | solution.py:343
  6.2 0.0 copy-start
  6.2 1.2 %copy-done = bf16[4096,128]{1,0:T(8,128)(2,1)S(1)} copy-done((bf16[4096,128]{1,0:T(8,128)(2,1)S(1)}, bf16[4096,128]{1,0:T(8,128)(2,1)}, u32[]{:S(2)}) %copy-start) | copy-done | bytes 1048600
  7.4 0.0 copy-start.1
  7.4 1.0 copy-done.1
  8.4 0.0 copy-start.3
  8.5 1.5 %copy-done.3 = bf16[2,27,128,128]{3,2,1,0:T(8,128)(2,1)S(1)} copy-done((bf16[2,27,128,128]{3,2,1,0:T(8,128)(2,1)S(1)}, bf16[2,27,128,128]{3,2,1,0:T(8,128)(2,1)}, u32[]{:S(2)}) %copy-start.3) | copy-done | bytes 1769496
  9.9 0.0 copy-start.5
  9.9 0.8 copy-done.5
  10.8 0.0 copy-start.7
  10.8 0.7 copy-done.7
  11.5 0.0 copy-start.8
  11.5 0.7 copy-done.8
  12.1 0.0 copy-start.2
  12.1 0.0 copy-start.4
  12.1 0.0 copy-start.6
  12.1 24.1 %first_layer.1 = (bf16[128,4096]{1,0:T(8,128)(2,1)S(1)}, bf16[128,4352]{1,0:T(8,128)(2,1)S(1)}, s32[32,128]{1,0:T(8,128)S(1)}, f32[32,128]{1,0:T(8,128)S(1)}, f32[32,128]{1,0:T(8,128)S(1)}) custom-call(s32[1]{0:T(128)} %bitcast.place_ref, s32[16]{0:T(128)S(1)} %copy-done.8, bf16[4096,128]{1,0:T(8,128)(2,1)S(1)} %copy-done, s32[27,4096]{1,0:T(8,128)S(1)} %copy-done.1, ...), custom_call_target="tpu_custom_call" | custom-call | flops 20000000000 | bytes 6000000 | tf_op jit(solution)/shard_map/first_layer/pallas_call | solution.py:354
  36.3 0.0 collective-permute-done.1.high_ref
  36.3 0.0 collective-permute-done.low_ref
  36.3 0.0 copy-done.2
  36.3 0.0 copy-done.4
  36.3 0.0 copy-done.6
  36.3 31.5 %second_layer.1 = bf16[16,272,128]{2,1,0:T(8,128)(2,1)S(1)} custom-call(s32[1]{0:T(128)} %bitcast.place_ref, s32[16]{0:T(128)S(1)} %copy-done.8, bf16[288,128]{1,0:T(8,128)(2,1)S(1)} %collective-permute-done.low_ref, bf16[288,128]{1,0:T(8,128)(2,1)S(1)} %collective-permute-done.1.high_ref, bf16[128,4096]{1,0:T(8,128)(2,1)S(1)} %get-tuple-element.10.act_ref, ...), custom_call_target="tpu_custom_call" | custom-call | flops 30000001024 | bytes 8000000 | tf_op jit(solution)/shard_map/second_layer/pallas_call | solution.py:373
  67.9 36.3 %all_to_all.5.got_ref = bf16[16,272,128]{2,1,0:T(8,128)(2,1)S(1)} all-to-all(bf16[16,272,128]{2,1,0:T(8,128)(2,1)S(1)} %second_layer.1), channel_id=1, replica_groups=mesh['groups'=2,'wide'=8,'narrow'=2] {'wide','narrow'}, dimensions={0} | all-to-all | bytes 2228224 | tf_op jit(solution)/shard_map/all_to_all | solution.py:399
  104.1 7.1 %hilbert_order.1 = bf16[4096,128]{1,0:T(8,128)(2,1)} custom-call(bf16[16,272,128]{2,1,0:T(8,128)(2,1)S(1)} %all_to_all.5.got_ref), custom_call_target="tpu_custom_call" | custom-call | tf_op jit(solution)/shard_map/hilbert_order/pallas_call | solution.py:400
  (2 shorter events, 0.0 us)
Async XLA Ops:
  1.8 34.4 %collective-permute-start.1 = (bf16[288,128]{1,0:T(8,128)(2,1)S(1)}, bf16[288,128]{1,0:T(8,128)(2,1)S(1)}, u32[]{:S(2)}, u32[]{:S(2)}) collective-permute-start(bf16[288,128]{1,0:T(8,128)(2,1)S(1)} %get-tuple-element.19), channel_id=1, source_target_pairs={{1,0},{2,1},{3,2},{4,3},{5,4},{6,5},{7,6},{8,7},{9,8},{10,9},{11,1... | collective-permute-start | bytes 221192 | tf_op jit(solution)/shard_map/ppermute | solution.py:344
  3.1 33.2 %collective-permute-start = (bf16[288,128]{1,0:T(8,128)(2,1)S(1)}, bf16[288,128]{1,0:T(8,128)(2,1)S(1)}, u32[]{:S(2)}, u32[]{:S(2)}) collective-permute-start(bf16[288,128]{1,0:T(8,128)(2,1)S(1)} %get-tuple-element.20), channel_id=1, source_target_pairs={{0,1},{1,2},{2,3},{3,4},{4,5},{5,6},{6,7},{7,8},{8,9},{9,10},{10,1... | collective-permute-start | bytes 221192 | tf_op jit(solution)/shard_map/ppermute | solution.py:343
  6.2 1.2 %copy-start = (bf16[4096,128]{1,0:T(8,128)(2,1)S(1)}, bf16[4096,128]{1,0:T(8,128)(2,1)}, u32[]{:S(2)}) copy-start(bf16[4096,128]{1,0:T(8,128)(2,1)} %voxels_ref.1) | copy-start | bytes 3145732
  7.4 1.0 copy-start.1
  8.4 1.5 %copy-start.3 = (bf16[2,27,128,128]{3,2,1,0:T(8,128)(2,1)S(1)}, bf16[2,27,128,128]{3,2,1,0:T(8,128)(2,1)}, u32[]{:S(2)}) copy-start(bf16[2,27,128,128]{3,2,1,0:T(8,128)(2,1)} %weight1_ref.1) | copy-start | bytes 5308420
  9.9 0.8 copy-start.5
  10.8 0.7 copy-start.7
  11.5 0.7 copy-start.8
  12.1 24.2 %copy-start.2 = (s32[27,4096]{1,0:T(8,128)S(1)}, s32[27,4096]{1,0:T(8,128)}, u32[]{:S(2)}) copy-start(s32[27,4096]{1,0:T(8,128)} %near_ref.3) | copy-start | bytes 1327108
  12.1 24.2 %copy-start.4 = (bf16[2,27,128,128]{3,2,1,0:T(8,128)(2,1)S(1)}, bf16[2,27,128,128]{3,2,1,0:T(8,128)(2,1)}, u32[]{:S(2)}) copy-start(bf16[2,27,128,128]{3,2,1,0:T(8,128)(2,1)} %weight1_ref.1) | copy-start | bytes 5308420
  12.1 24.2 %copy-start.6 = (bf16[2,128,128]{2,1,0:T(8,128)(2,1)S(1)}, bf16[2,128,128]{2,1,0:T(8,128)(2,1)}, u32[]{:S(2)}) copy-start(bf16[2,128,128]{2,1,0:T(8,128)(2,1)} %linear_ref.3) | copy-start | bytes 196612

commit v3 on v2

--- a/solution.py
+++ b/solution.py
@@ -72,8 +72,7 @@
             picked[at, half * HALO : (half + 1) * HALO] = total
 
 
-def finish_block(current, weight, linear, live, picked):
-    convolved = dot(weight, picked[...]).astype(BF16)
+def norm_block(current, convolved, linear, live):
     projected = dot(linear, convolved)
     average = jnp.mean(projected, axis=0, keepdims=True)
     centred = projected - average
@@ -82,10 +81,14 @@
     return jnp.where(live, summed, 0.0).astype(BF16)
 
 
-def turn_weights(weight_ref, turned):
+def columns(start):
+    return pl.ds(pl.multiple_of(start, HALO), BLOCK)
+
+
+def turn_weights(weight_ref, layer, turned):
     offsets, channels = weight_ref.shape[1], weight_ref.shape[2]
     for k in range(offsets):
-        turned[:, k * channels : (k + 1) * channels] = weight_ref[0, k].T
+        turned[:, k * channels : (k + 1) * channels] = weight_ref[layer, k].T
 
 
 def device_counts(place_ref, counts_ref):
@@ -143,56 +146,89 @@
 
 
 def inner_kernel(
-    shards, place_ref, counts_ref, voxels_ref, near_ref, weight_ref, linear_ref, destination_ref,
-    act_ref, next_ref, perm_ref, high_ref, low_ref, turned, even, odd,
+    shards, place_ref, counts_ref, voxels_hbm, near_hbm, weight_hbm, linear_ref, destination_hbm,
+    act_ref, next_ref, perm_ref, high_ref, low_ref, turned_ref,
+    voxels_ref, near_ref, weight_ref, destination_ref, even, odd, conv, sems,
 ):
+    copies = [
+        pltpu.make_async_copy(source, target, sems.at[n])
+        for n, (source, target) in enumerate(
+            (
+                (destination_hbm, destination_ref),
+                (voxels_hbm, voxels_ref),
+                (near_hbm, near_ref),
+                (weight_hbm, weight_ref),
+            )
+        )
+    ]
+    for copy in copies:
+        copy.start()
     rows, channels = voxels_ref.shape
     own, before, count, after = device_counts(place_ref, counts_ref)
+    copies[0].wait()
     slots_body(destination_ref, perm_ref, high_ref, low_ref, shards)
-    turn_weights(weight_ref, turned)
+    copies[1].wait()
     for c in range(rows // BLOCK):
         live = live_lanes(c * BLOCK, BLOCK, rows, before, count, after)
         block = voxels_ref[c * BLOCK : (c + 1) * BLOCK, :].T
         act_ref[:, c * BLOCK : (c + 1) * BLOCK] = jnp.where(live, block.astype(F32), 0.0).astype(BF16)
     linear = linear_ref[0].T
+    copies[3].wait()
+    for layer in range(2):
+        turn_weights(weight_ref, layer, turned_ref.at[layer])
+    copies[2].wait()
 
     def gather(b, picked):
-        first = pl.multiple_of((b - 1) * BLOCK, BLOCK)
-        targets = jnp.maximum(near_ref[:, pl.ds(pl.multiple_of(first + HALO, HALO), BLOCK)] - (own * rows + first), -1)
+        first = (b - 1) * BLOCK
+        targets = jnp.maximum(near_ref[:, columns(first + HALO)] - (own * rows + first), -1)
         gather_block(lambda at, n: act_ref[:, pl.ds(pl.multiple_of(first + at, HALO), n)], targets, picked)
 
-    def finish(b, picked):
-        first = b * BLOCK - HALO
-        current = act_ref[:, pl.ds(pl.multiple_of(jnp.maximum(first, 0), HALO), BLOCK)]
-        live = live_lanes(first, BLOCK, rows, before, count, after)
-        next_ref[:, pl.ds(pl.multiple_of(b * BLOCK, BLOCK), BLOCK)] = finish_block(
-            current, turned[...], linear, live, picked
-        )
+    def convolve(b, picked):
+        conv[:, columns(b * BLOCK)] = dot(turned_ref[0], picked[...]).astype(BF16)
 
     blocks = rows // BLOCK
-    odd[...] = jnp.zeros_like(odd)
 
     def step(t, _):
         gather(2 * t + 1, even)
-        finish(2 * t, odd)
+        convolve(2 * t, odd)
         gather(2 * t + 2, odd)
-        finish(2 * t + 1, even)
+        convolve(2 * t + 1, even)
         return 0
 
     lax.fori_loop(0, (blocks - 2) // 2, step, 0)
     gather(blocks - 1, even)
-    finish(blocks - 2, odd)
-    finish(blocks - 1, even)
+    convolve(blocks - 2, odd)
+    convolve(blocks - 1, even)
+
+    def norm(b):
+        first = b * BLOCK - HALO
+        live = live_lanes(first, BLOCK, rows, before, count, after)
+        next_ref[:, columns(b * BLOCK)] = norm_block(
+            act_ref[:, columns(first)], conv[:, columns(b * BLOCK)], linear, live
+        )
+
+    in_turn(1, blocks, norm)
+
+
+def in_turn(first, last, body):
+    count = last - first
+    unroll = max(u for u in range(1, 6) if count % u == 0)
+
+    def step(t, _):
+        for u in range(unroll):
+            body(first + t * unroll + u)
+        return 0
+
+    lax.fori_loop(0, count // unroll, step, 0)
 
 
 def outer_kernel(
-    place_ref, counts_ref, low_ref, high_ref, act_ref, inner_ref, near_ref, weight0_ref, weight1_ref, linear_ref,
-    perm_ref, place_high_ref, place_low_ref, send_ref, turned, even, odd, edge, padded, last,
+    place_ref, counts_ref, low_ref, high_ref, act_ref, inner_ref, near_ref, turned_ref, linear_ref,
+    perm_ref, place_high_ref, place_low_ref, send_ref, even, odd, edge, padded, conv, last,
 ):
     channels, rows = act_ref.shape
     own, before, count, after = device_counts(place_ref, counts_ref)
     extent = 2 * HALO
-    turn_weights(weight0_ref, turned)
     linear = linear_ref[0].T
     lanes = lax.broadcasted_iota(jnp.int32, (1, HALO), 1)
 
@@ -225,38 +261,44 @@
     for n in range(2):
         gather_block(lambda at, size: edges[n][:, at : at + size], near[n], picks[n])
     for n in range(2):
+        conv[:, n * BLOCK : (n + 1) * BLOCK] = dot(turned_ref[0], picks[n][...]).astype(BF16)
+    for n in range(2):
         at = n * rows
         live = live_lanes(at - HALO, BLOCK, rows, before, count, after)
-        padded[:, at : at + BLOCK] = finish_block(
-            edges[n][:, HALO : HALO + BLOCK], turned[...], linear, live, picks[n]
+        padded[:, at : at + BLOCK] = norm_block(
+            edges[n][:, HALO : HALO + BLOCK], conv[:, n * BLOCK : (n + 1) * BLOCK], linear, live
         )
     padded[:, BLOCK:rows] = inner_ref[:, BLOCK:rows]
 
-    turn_weights(weight1_ref, turned)
     linear = linear_ref[1].T
 
     def gather(b, picked):
-        first = pl.multiple_of(b * BLOCK, BLOCK)
-        targets = jnp.maximum(near_ref[:, pl.ds(first, BLOCK)] - (own * rows + first - HALO), -1)
+        first = b * BLOCK
+        targets = jnp.maximum(near_ref[:, columns(first)] - (own * rows + first - HALO), -1)
         gather_block(lambda at, n: padded[:, pl.ds(pl.multiple_of(first + at, HALO), n)], targets, picked)
 
-    def finish(b, picked):
-        first = b * BLOCK
-        current = padded[:, pl.ds(pl.multiple_of(jnp.maximum(first, 0) + HALO, HALO), BLOCK)]
-        live = live_lanes(first, BLOCK, rows, before, count, after)
-        last[:, pl.ds(pl.multiple_of(first + BLOCK, BLOCK), BLOCK)] = finish_block(
-            current, turned[...], linear, live, picked
-        )
+    def convolve(b, picked):
+        conv[:, columns((b + 1) * BLOCK)] = dot(turned_ref[1], picked[...]).astype(BF16)
 
     def step(t, _):
         gather(2 * t, even)
-        finish(2 * t - 1, odd)
+        convolve(2 * t - 1, odd)
         gather(2 * t + 1, odd)
-        finish(2 * t, even)
+        convolve(2 * t, even)
         return 0
 
-    lax.fori_loop(0, rows // BLOCK // 2, step, 0)
-    finish(rows // BLOCK - 1, odd)
+    blocks = rows // BLOCK
+    lax.fori_loop(0, blocks // 2, step, 0)
+    convolve(blocks - 1, odd)
+
+    def norm(b):
+        first = b * BLOCK
+        live = live_lanes(first, BLOCK, rows, before, count, after)
+        last[:, columns(first)] = norm_block(
+            padded[:, columns(first + HALO)], conv[:, columns(first + BLOCK)], linear, live
+        )
+
+    in_turn(0, blocks, norm)
 
     shards, depth, _ = send_ref.shape
     capacity = rows // shards
@@ -266,7 +308,7 @@
         for p in range(pieces):
             send_ref[b * pieces + p, 0:capacity, :] = block[p * capacity : (p + 1) * capacity, :]
 
-    reorder(last.at[:, BLOCK:], perm_ref, store)
+    reorder(last, perm_ref, store)
     held = capacity // 128
     pad = jnp.zeros((depth - capacity - 2 * held, 128), F32)
     for d in range(shards):
@@ -275,17 +317,28 @@
         send_ref[d, capacity:, :] = extra.astype(BF16)
 
 
-def reorder(source, from_ref, store):
+def reorder(source, from_ref, store, dots=6, unroll=8):
     channels, rows = source.shape
-    unroll = 4
+    windows = rows // WINDOW
 
     def one(b):
         pair = from_ref[pl.ds(b * 2, 2), :]
         wanted = jnp.concatenate([pair[0:1, :], pair[1:2, :]], axis=1)
         total = jnp.zeros((channels, BLOCK), F32)
-        for w in range(rows // WINDOW):
+        halves = [jnp.zeros((channels, 128), BF16) for _ in range(2)]
+        lanes = [pair[h : h + 1, :] & 127 for h in range(2)]
+        chunks = [jnp.broadcast_to((pair[h : h + 1, :] >> 7).astype(jnp.int16), (channels, 128)) for h in range(2)]
+        rest = [(j, h) for j in range(dots * WINDOW // 128, rows // 128) for h in range(2)]
+        done = 0
+        for w in range(dots):
             total = total + dot(source[:, w * WINDOW : (w + 1) * WINDOW], selector(wanted - w * WINDOW, WINDOW))
-        store(b, total.astype(BF16).T)
+            until = len(rest) * (w + 1) // dots
+            for j, h in rest[done:until]:
+                halves[h] = jnp.where(
+                    chunks[h] == j, lane_pick(source[:, j * 128 : (j + 1) * 128], lanes[h]), halves[h]
+                )
+            done = until
+        store(b, (total + jnp.concatenate(halves, axis=1).astype(F32)).astype(BF16).T)
 
     def step(t, _):
         for u in range(unroll):
@@ -343,27 +396,23 @@
     low = lax.ppermute(packed(rows - extent, rows - HALO), both, forward)
     high = lax.ppermute(packed(0, 0), both, backward)
 
-    def weight_spec(layer):
-        return pl.BlockSpec((1,) + conv_weight.shape[1:], lambda i: (layer, 0, 0, 0))
-
-    whole = lambda shape: pl.BlockSpec(shape, lambda i: (0,) * len(shape))
     table = (rows // 128, 128)
     padded = (channels, rows + BLOCK)
     picked = VMEM((offsets * channels, BLOCK), BF16)
-    turned = VMEM((channels, offsets * channels), BF16)
-    act, inner, perm, place_high, place_low = pl.pallas_call(
+    turned = (2, channels, offsets * channels)
+    hbm = pl.BlockSpec(memory_space=pltpu.HBM)
+    act, inner, perm, place_high, place_low, weights = pl.pallas_call(
         functools.partial(inner_kernel, shards),
-        grid=(1,),
         out_shape=(
             struct((channels, rows), BF16), struct(padded, BF16), struct(table, jnp.int32), struct(table, F32),
-            struct(table, F32),
+            struct(table, F32), struct(turned, BF16),
         ),
-        in_specs=[
-            smem, smem, whole(voxels.shape), whole(neighbours.shape), weight_spec(0), whole(linear_weight.shape),
-            whole((1, rows)),
+        in_specs=[smem, smem, hbm, hbm, hbm, vmem, hbm],
+        out_specs=(vmem,) * 6,
+        scratch_shapes=[
+            VMEM(voxels.shape, BF16), VMEM(neighbours.shape, jnp.int32), VMEM(conv_weight.shape, BF16),
+            VMEM((1, rows), jnp.int32), picked, picked, VMEM(padded, BF16), pltpu.SemaphoreType.DMA((4,)),
         ],
-        out_specs=(whole((channels, rows)), whole(padded), whole(table), whole(table), whole(table)),
-        scratch_shapes=[turned, picked, picked],
         compiler_params=params(),
         cost_estimate=pl.CostEstimate(flops=20_000_000_000, bytes_accessed=6_000_000, transcendentals=0),
         name="first_layer",
@@ -372,29 +421,21 @@
     depth = rows // shards + 16
     send = pl.pallas_call(
         outer_kernel,
-        grid=(1,),
         out_shape=struct((shards, depth, channels), BF16),
-        in_specs=[
-            smem, smem, whole(low.shape), whole(high.shape), whole((channels, rows)), whole(padded),
-            whole(neighbours.shape), weight_spec(0), weight_spec(1), whole(linear_weight.shape),
-            whole(table), whole(table), whole(table),
-        ],
-        out_specs=whole((shards, depth, channels)),
+        in_specs=[smem, smem] + [vmem] * 10,
+        out_specs=vmem,
         scratch_shapes=[
-            turned,
             picked,
             picked,
             VMEM((channels, 2 * WINDOW), BF16),
             VMEM(padded, BF16),
             VMEM(padded, BF16),
+            VMEM((channels, rows), BF16),
         ],
         compiler_params=params(),
         cost_estimate=pl.CostEstimate(flops=30_000_000_000, bytes_accessed=8_000_000, transcendentals=0),
         name="second_layer",
-    )(
-        place, counts, low, high, act, inner, neighbours, conv_weight, conv_weight, linear_weight, perm, place_high,
-        place_low,
-    )
+    )(place, counts, low, high, act, inner, neighbours, weights, linear_weight, perm, place_high, place_low)
 
     got = lax.all_to_all(send, both, split_axis=0, concat_axis=0, tiled=True)
     return pl.pallas_call(

time: 112 us -> 94.7 us (0.85)
  Pallas kernels: 62.8 us -> 47.2 us
  local copies, waits for them, and re-layouts: 6.92 us -> 5.44 us
    pallas_call x2, Pallas kernels: 55.6 us -> 41.5 us  [the longest x1 22.8 us: local(): pl.pallas_call(outer_kernel, out_shape=struct((shards, depth, channels),...]
    pallas_call x1, Pallas kernels: 7.15 us -> 5.66 us  [local(): pl.pallas_call(final_kernel, out_shape=struct((rows, channels), BF16), in...]
    unnamed x18 -> x14, local copies, waits for them, and re-layouts: 5.96 us -> 4.48 us
  transfers between devices with their start and end apart: 2 -> 2, of which waited for: 0 -> 0; matrix products, arithmetic and copies ran while one was open for 0% -> 0% of each run, Pallas kernels for 22% -> 20%
where the time goes in v3:
time: 94.7 us; the launch traced here: 94.2 us
  Pallas kernels  47.2 us (50%)
  blocking collectives  36.3 us (38%)
  local copies, waits for them, and re-layouts  5.44 us (6%)
  starting transfers between devices  4.33 us (5%)
    all_to_all x1, blocking collectives, local(): got = lax.all_to_all(send, both, split_axis=0, concat_axis=0, tiled=True)  36.3 us
    pallas_call x1, Pallas kernels, local(): pl.pallas_call(outer_kernel, out_shape=struct((shards, depth, channels),...  22.8 us
    pallas_call x1, Pallas kernels, local(): pl.pallas_call(functools.partial(inner_kernel, shards), out_shape=(struct...  18.7 us
    pallas_call x1, Pallas kernels, local(): pl.pallas_call(final_kernel, out_shape=struct((rows, channels), BF16), in...  5.66 us
    unnamed x14, local copies, waits for them, and re-layouts  4.48 us
    ppermute x1, starting transfers between devices, local(): low = lax.ppermute(packed(rows - extent, rows - HALO), both, forward)  3.03 us
  transfers between devices with their start and end apart: 2, of which 0 were waited for; matrix products, arithmetic and copies ran while one was open for 0% of the time, Pallas kernels for 20%

profile of v3, /device:TPU:0, one launch (start us, length us, event | category | flops | bytes accessed | tf_op | source)
XLA Modules:
  0.0 94.2 jit_solution(5308482609276155383)
XLA Ops:
  0.0 0.9 fusion
  0.9 0.1 pad.5.clone
  1.0 0.7 select_convert_fusion
  1.7 0.1 maximum_maximum_fusion.1
  1.8 1.3 %collective-permute-start.1 = (bf16[288,128]{1,0:T(8,128)(2,1)S(1)}, bf16[288,128]{1,0:T(8,128)(2,1)S(1)}, u32[]{:S(2)}, u32[]{:S(2)}) collective-permute-start(bf16[288,128]{1,0:T(8,128)(2,1)S(1)} %get-tuple-element.21), channel_id=1, source_target_pairs={{1,0},{2,1},{3,2},{4,3},{5,4},{6,5},{7,6},{8,7},{9,8},{10,9},{11,1... | collective-permute-start | bytes 221192 | tf_op jit(solution)/shard_map/ppermute | solution.py:397
  3.1 3.0 %collective-permute-start = (bf16[288,128]{1,0:T(8,128)(2,1)S(1)}, bf16[288,128]{1,0:T(8,128)(2,1)S(1)}, u32[]{:S(2)}, u32[]{:S(2)}) collective-permute-start(bf16[288,128]{1,0:T(8,128)(2,1)S(1)} %get-tuple-element.22), channel_id=1, source_target_pairs={{0,1},{1,2},{2,3},{3,4},{4,5},{5,6},{6,7},{7,8},{8,9},{9,10},{10,1... | collective-permute-start | bytes 221192 | tf_op jit(solution)/shard_map/ppermute | solution.py:396
  6.2 0.0 copy-start
  6.2 1.2 %copy-done = bf16[4096,128]{1,0:T(8,128)(2,1)S(1)} copy-done((bf16[4096,128]{1,0:T(8,128)(2,1)S(1)}, bf16[4096,128]{1,0:T(8,128)(2,1)}, u32[]{:S(2)}) %copy-start) | copy-done | bytes 1048600
  7.4 0.0 copy-start.1
  7.4 1.0 %copy-done.1 = s32[27,4096]{1,0:T(8,128)S(1)} copy-done((s32[27,4096]{1,0:T(8,128)S(1)}, s32[27,4096]{1,0:T(8,128)}, u32[]{:S(2)}) %copy-start.1) | copy-done | bytes 442392
  8.4 0.0 copy-start.3
  8.5 0.8 copy-done.3
  9.3 0.0 copy-start.5
  9.3 0.7 copy-done.5
  10.0 0.0 copy-start.6
  10.0 0.7 copy-done.6
  10.7 0.0 copy-start.2
  10.7 0.0 copy-start.4
  10.7 18.7 %first_layer.1 = (bf16[128,4096]{1,0:T(8,128)(2,1)S(1)}, bf16[128,4352]{1,0:T(8,128)(2,1)S(1)}, s32[32,128]{1,0:T(8,128)S(1)}, f32[32,128]{1,0:T(8,128)S(1)}, f3...) custom-call(s32[1]{0:T(128)} %bitcast.place_ref, s32[16]{0:T(128)S(1)} %copy-done.6, ...), custom_call_target="tpu_custom_call" | custom-call | flops 20000000000 | bytes 6000000 | tf_op jit(solution)/shard_map/first_layer/pallas_call | solution.py:404
  29.4 0.0 collective-permute-done.1.high_ref
  29.4 0.0 collective-permute-done.low_ref
  29.4 0.0 copy-done.2
  29.4 0.0 copy-done.4
  29.4 22.8 %second_layer.1 = bf16[16,272,128]{2,1,0:T(8,128)(2,1)S(1)} custom-call(s32[1]{0:T(128)} %bitcast.place_ref, s32[16]{0:T(128)S(1)} %copy-done.6, bf16[288,128]{1,0:T(8,128)(2,1)S(1)} %collective-permute-done.low_ref, bf16[288,128]{1,0:T(8,128)(2,1)S(1)} %collective-permute-done.1.high_ref, bf16[128,4096]{1,0:T(8,128)(2,1)S(1)} %get-tuple-element.11.act_ref, ...), custom_call_target="tpu_custom_call" | custom-call | flops 30000001024 | bytes 8000000 | tf_op jit(solution)/shard_map/second_layer/pallas_call | solution.py:422
  52.2 36.3 %all_to_all.5.got_ref = bf16[16,272,128]{2,1,0:T(8,128)(2,1)S(1)} all-to-all(bf16[16,272,128]{2,1,0:T(8,128)(2,1)S(1)} %second_layer.1), channel_id=1, replica_groups=mesh['groups'=2,'wide'=8,'narrow'=2] {'wide','narrow'}, dimensions={0} | all-to-all | bytes 2228224 | tf_op jit(solution)/shard_map/all_to_all | solution.py:440
  88.5 5.7 %hilbert_order.1 = bf16[4096,128]{1,0:T(8,128)(2,1)} custom-call(bf16[16,272,128]{2,1,0:T(8,128)(2,1)S(1)} %all_to_all.5.got_ref), custom_call_target="tpu_custom_call" | custom-call | tf_op jit(solution)/shard_map/hilbert_order/pallas_call | solution.py:441
  (2 shorter events, 0.0 us)
Async XLA Ops:
  1.8 27.5 %collective-permute-start.1 = (bf16[288,128]{1,0:T(8,128)(2,1)S(1)}, bf16[288,128]{1,0:T(8,128)(2,1)S(1)}, u32[]{:S(2)}, u32[]{:S(2)}) collective-permute-start(bf16[288,128]{1,0:T(8,128)(2,1)S(1)} %get-tuple-element.21), channel_id=1, source_target_pairs={{1,0},{2,1},{3,2},{4,3},{5,4},{6,5},{7,6},{8,7},{9,8},{10,9},{11,1... | collective-permute-start | bytes 221192 | tf_op jit(solution)/shard_map/ppermute | solution.py:397
  3.1 26.2 %collective-permute-start = (bf16[288,128]{1,0:T(8,128)(2,1)S(1)}, bf16[288,128]{1,0:T(8,128)(2,1)S(1)}, u32[]{:S(2)}, u32[]{:S(2)}) collective-permute-start(bf16[288,128]{1,0:T(8,128)(2,1)S(1)} %get-tuple-element.22), channel_id=1, source_target_pairs={{0,1},{1,2},{2,3},{3,4},{4,5},{5,6},{6,7},{7,8},{8,9},{9,10},{10,1... | collective-permute-start | bytes 221192 | tf_op jit(solution)/shard_map/ppermute | solution.py:396
  6.2 1.2 %copy-start = (bf16[4096,128]{1,0:T(8,128)(2,1)S(1)}, bf16[4096,128]{1,0:T(8,128)(2,1)}, u32[]{:S(2)}) copy-start(bf16[4096,128]{1,0:T(8,128)(2,1)} %voxels_hbm.1) | copy-start | bytes 3145732
  7.4 1.0 %copy-start.1 = (s32[27,4096]{1,0:T(8,128)S(1)}, s32[27,4096]{1,0:T(8,128)}, u32[]{:S(2)}) copy-start(s32[27,4096]{1,0:T(8,128)} %near_ref.1) | copy-start | bytes 1327108
  8.4 0.8 copy-start.3
  9.3 0.7 copy-start.5
  10.0 0.7 copy-start.6
  10.7 18.7 %copy-start.2 = (s32[27,4096]{1,0:T(8,128)S(1)}, s32[27,4096]{1,0:T(8,128)}, u32[]{:S(2)}) copy-start(s32[27,4096]{1,0:T(8,128)} %near_ref.1) | copy-start | bytes 1327108
  10.7 18.7 %copy-start.4 = (bf16[2,128,128]{2,1,0:T(8,128)(2,1)S(1)}, bf16[2,128,128]{2,1,0:T(8,128)(2,1)}, u32[]{:S(2)}) copy-start(bf16[2,128,128]{2,1,0:T(8,128)(2,1)} %linear_ref.3) | copy-start | bytes 196612

commit v4 on v3

--- a/solution.py
+++ b/solution.py
@@ -17,8 +17,8 @@
 VMEM = pltpu.VMEM
 
 
-def params():
-    return pltpu.CompilerParams(vmem_limit_bytes=48 * 1024 * 1024)
+def params(mebibytes=48):
+    return pltpu.CompilerParams(vmem_limit_bytes=mebibytes * 1024 * 1024)
 
 
 def selector(row, depth):
@@ -99,32 +99,24 @@
     return own, before, counts_ref[own], after
 
 
-def slots_body(destination_ref, perm_ref, high_ref, low_ref, shards):
+def slots_tile(c, destination_ref, before_ref, total_ref):
     rows = destination_ref.shape[1]
-    capacity = rows // shards
-    lanes = 128
-    groups = rows // lanes
-    tile = 256
+    shards, tile = before_ref.shape
+    groups = rows // 128
     earlier = (
         lax.broadcasted_iota(jnp.int32, (tile, tile), 0) < lax.broadcasted_iota(jnp.int32, (tile, tile), 1)
     ).astype(F32).astype(BF16)
-    ones = jnp.ones((tile, tile), BF16)
     devices = lax.broadcasted_iota(jnp.int32, (shards, tile), 0)
-    before = (devices * capacity).astype(F32)
-    total = jnp.zeros((4 * groups, lanes), F32)
-    for c in range(rows // tile):
-        goal = destination_ref[:, c * tile : (c + 1) * tile]
-        device = goal >> (rows.bit_length() - 1)
-        place = goal & (rows - 1)
-        member = (jnp.broadcast_to(device, (shards, tile)) == devices).astype(F32)
-        member16 = member.astype(BF16)
-        slot = jnp.sum(member * (dot(member16, earlier) + before), axis=0, keepdims=True).astype(jnp.int32)
-        before = before + dot(member16, ones)
-        row = c * tile + lax.broadcasted_iota(jnp.int32, (1, tile), 1)
-        total = total + scatter_term(slot, (row, place), groups)
-    perm_ref[...] = joined(total, 0, groups)
-    high_ref[...] = total[2 * groups : 3 * groups, :]
-    low_ref[...] = total[3 * groups :, :]
+    goal = destination_ref[:, columns(c * tile)]
+    device = goal >> (rows.bit_length() - 1)
+    place = goal & (rows - 1)
+    member = (jnp.broadcast_to(device, (shards, tile)) == devices).astype(F32)
+    member16 = member.astype(BF16)
+    before = before_ref[...]
+    slot = jnp.sum(member * (dot(member16, earlier) + before), axis=0, keepdims=True).astype(jnp.int32)
+    before_ref[...] = before + dot(member16, jnp.ones((tile, tile), BF16))
+    row = c * tile + lax.broadcasted_iota(jnp.int32, (1, tile), 1)
+    total_ref[...] += scatter_term(slot, (row, place), groups)
 
 
 def scatter_term(at, values, groups):
@@ -145,38 +137,56 @@
     return (high * 64.0 + low).astype(jnp.int32)
 
 
-def inner_kernel(
-    shards, place_ref, counts_ref, voxels_hbm, near_hbm, weight_hbm, linear_ref, destination_hbm,
-    act_ref, next_ref, perm_ref, high_ref, low_ref, turned_ref,
-    voxels_ref, near_ref, weight_ref, destination_ref, even, odd, conv, sems,
-):
+def edges_kernel(place_ref, voxels_hbm, near_hbm, first_ref, last_ref, near_first, near_last, sems):
+    rows = voxels_hbm.shape[0]
+    extent = 2 * HALO
     copies = [
         pltpu.make_async_copy(source, target, sems.at[n])
         for n, (source, target) in enumerate(
             (
-                (destination_hbm, destination_ref),
-                (voxels_hbm, voxels_ref),
-                (near_hbm, near_ref),
-                (weight_hbm, weight_ref),
+                (near_hbm.at[:, 0:HALO], near_first),
+                (near_hbm.at[:, rows - HALO : rows], near_last),
+                (voxels_hbm.at[0:extent, :], first_ref.at[0:extent, :]),
+                (voxels_hbm.at[rows - extent : rows, :], last_ref.at[0:extent, :]),
             )
         )
     ]
     for copy in copies:
         copy.start()
+    own = place_ref[0]
+    lanes = lax.broadcasted_iota(jnp.int32, (1, HALO), 1)
+    for n, (near_ref, out_ref, first) in enumerate(((near_first, first_ref, 0), (near_last, last_ref, rows - HALO))):
+        copies[n].wait()
+        near = near_ref[...]
+        relative = jnp.where(near >= 0, near - (own * rows + first + lanes), ABSENT).astype(F32)
+        pad = jnp.zeros((out_ref.shape[0] - extent - near.shape[0], HALO), F32)
+        out_ref[extent:, :] = jnp.concatenate([relative, pad], axis=0).astype(BF16)
+    copies[2].wait()
+    copies[3].wait()
+
+
+def inner_kernel(
+    shards, place_ref, counts_ref, voxels_ref, near_ref, weight_hbm, linear_ref, destination_ref,
+    act_ref, next_ref, perm_ref, high_ref, low_ref, turned_ref,
+    weight_ref, even, odd, conv, before_ref, total_ref, sem,
+):
+    weights_in = pltpu.make_async_copy(weight_hbm, weight_ref, sem)
+    weights_in.start()
     rows, channels = voxels_ref.shape
     own, before, count, after = device_counts(place_ref, counts_ref)
-    copies[0].wait()
-    slots_body(destination_ref, perm_ref, high_ref, low_ref, shards)
-    copies[1].wait()
+    before_ref[...] = (lax.broadcasted_iota(jnp.int32, before_ref.shape, 0) * (rows // shards)).astype(F32)
+    total_ref[...] = jnp.zeros_like(total_ref)
+    slots = lambda c: slots_tile(c, destination_ref, before_ref, total_ref)
+    slots(0)
+    slots(1)
     for c in range(rows // BLOCK):
         live = live_lanes(c * BLOCK, BLOCK, rows, before, count, after)
         block = voxels_ref[c * BLOCK : (c + 1) * BLOCK, :].T
         act_ref[:, c * BLOCK : (c + 1) * BLOCK] = jnp.where(live, block.astype(F32), 0.0).astype(BF16)
-    linear = linear_ref[0].T
-    copies[3].wait()
+    weights_in.wait()
     for layer in range(2):
         turn_weights(weight_ref, layer, turned_ref.at[layer])
-    copies[2].wait()
+    linear = linear_ref[0].T
 
     def gather(b, picked):
         first = (b - 1) * BLOCK
@@ -190,8 +200,10 @@
 
     def step(t, _):
         gather(2 * t + 1, even)
+        slots(2 * t + 2)
         convolve(2 * t, odd)
         gather(2 * t + 2, odd)
+        slots(2 * t + 3)
         convolve(2 * t + 1, even)
         return 0
 
@@ -208,6 +220,10 @@
         )
 
     in_turn(1, blocks, norm)
+    groups = rows // 128
+    perm_ref[...] = joined(total_ref[...], 0, groups)
+    high_ref[...] = total_ref[2 * groups : 3 * groups, :]
+    low_ref[...] = total_ref[3 * groups :, :]
 
 
 def in_turn(first, last, body):
@@ -381,37 +397,39 @@
     struct = jax.ShapeDtypeStruct
     vmem = pl.BlockSpec(memory_space=VMEM)
     smem = pl.BlockSpec(memory_space=SMEM)
-
-    def packed(first_voxel, first_near):
-        near = lax.slice_in_dim(neighbours, first_near, first_near + HALO, axis=1)
-        ids = own * rows + first_near + jnp.arange(HALO, dtype=jnp.int32)[None, :]
-        relative = jnp.where(near >= 0, near - ids, ABSENT).astype(BF16)
-        pad = jnp.zeros((32 - offsets, channels), BF16)
-        return jnp.concatenate(
-            [lax.slice_in_dim(voxels, first_voxel, first_voxel + extent, axis=0), relative, pad], axis=0
-        )
-
+    hbm = pl.BlockSpec(memory_space=pltpu.HBM)
+
+    packed = struct((extent + 32, channels), BF16)
+    first, final = pl.pallas_call(
+        edges_kernel,
+        out_shape=(packed, packed),
+        in_specs=[smem, hbm, hbm],
+        out_specs=(vmem, vmem),
+        scratch_shapes=[VMEM((offsets, HALO), jnp.int32), VMEM((offsets, HALO), jnp.int32), pltpu.SemaphoreType.DMA((4,))],
+        cost_estimate=pl.CostEstimate(flops=20_000_000_000, bytes_accessed=500_000, transcendentals=0),
+        compiler_params=params(60),
+        name="edges",
+    )(place, voxels, neighbours)
     forward = [(i, i + 1) for i in range(shards - 1)]
     backward = [(target, source) for source, target in forward]
-    low = lax.ppermute(packed(rows - extent, rows - HALO), both, forward)
-    high = lax.ppermute(packed(0, 0), both, backward)
+    low = lax.ppermute(final, both, forward)
+    high = lax.ppermute(first, both, backward)
 
     table = (rows // 128, 128)
     padded = (channels, rows + BLOCK)
     picked = VMEM((offsets * channels, BLOCK), BF16)
     turned = (2, channels, offsets * channels)
-    hbm = pl.BlockSpec(memory_space=pltpu.HBM)
     act, inner, perm, place_high, place_low, weights = pl.pallas_call(
         functools.partial(inner_kernel, shards),
         out_shape=(
             struct((channels, rows), BF16), struct(padded, BF16), struct(table, jnp.int32), struct(table, F32),
             struct(table, F32), struct(turned, BF16),
         ),
-        in_specs=[smem, smem, hbm, hbm, hbm, vmem, hbm],
+        in_specs=[smem, smem, vmem, vmem, hbm, vmem, vmem],
         out_specs=(vmem,) * 6,
         scratch_shapes=[
-            VMEM(voxels.shape, BF16), VMEM(neighbours.shape, jnp.int32), VMEM(conv_weight.shape, BF16),
-            VMEM((1, rows), jnp.int32), picked, picked, VMEM(padded, BF16), pltpu.SemaphoreType.DMA((4,)),
+            VMEM(conv_weight.shape, BF16), picked, picked, VMEM(padded, BF16), VMEM((shards, BLOCK), F32),
+            VMEM((4 * rows // 128, 128), F32), pltpu.SemaphoreType.DMA,
         ],
         compiler_params=params(),
         cost_estimate=pl.CostEstimate(flops=20_000_000_000, bytes_accessed=6_000_000, transcendentals=0),

time: 94.7 us -> 91.7 us (0.968)
  local copies, waits for them, and re-layouts: 5.44 us -> 0.02 us
  Pallas kernels: 47.2 us -> 50 us
  blocking collectives: 36.3 us -> 37.6 us
    unnamed x14 -> x10, local copies, waits for them, and re-layouts: 4.48 us -> 0.02 us
    pallas_call x0 -> x1, Pallas kernels: none -> 1.73 us  [local(): pl.pallas_call(edges_kernel, out_shape=(packed, packed), in_specs=[smem,...]
    all_to_all x1, blocking collectives: 36.3 us -> 37.6 us  [local(): got = lax.all_to_all(send, both, split_axis=0, concat_axis=0, tiled=True)]
    pallas_call x1, Pallas kernels: 18.7 us -> 19.8 us  [local(): pl.pallas_call(functools.partial(inner_kernel, shards), out_shape=(struct...]
  transfers between devices with their start and end apart: 2 -> 2, of which waited for: 0 -> 0; matrix products, arithmetic and copies ran while one was open for 0% -> 0% of each run, Pallas kernels for 20% -> 22%
where the time goes in v4:
time: 91.7 us; the launch traced here: 91.4 us
  Pallas kernels  50 us (55%)
  blocking collectives  37.6 us (41%)
  starting transfers between devices  3.66 us (4%)
    all_to_all x1, blocking collectives, local(): got = lax.all_to_all(send, both, split_axis=0, concat_axis=0, tiled=True)  37.6 us
    pallas_call x1, Pallas kernels, local(): pl.pallas_call(outer_kernel, out_shape=struct((shards, depth, channels),...  22.8 us
    pallas_call x1, Pallas kernels, local(): pl.pallas_call(functools.partial(inner_kernel, shards), out_shape=(struct...  19.8 us
    pallas_call x1, Pallas kernels, local(): pl.pallas_call(final_kernel, out_shape=struct((rows, channels), BF16), in...  5.66 us
    ppermute x1, starting transfers between devices, local(): low = lax.ppermute(final, both, forward)  2.37 us
  transfers between devices with their start and end apart: 2, of which 0 were waited for; matrix products, arithmetic and copies ran while one was open for 0% of the time, Pallas kernels for 22%

profile of v4, /device:TPU:0, one launch (start us, length us, event | category | flops | bytes accessed | tf_op | source)
XLA Modules:
  0.0 91.4 jit_solution(5793370923786106931)
XLA Ops:
  0.0 0.0 copy-start
  0.0 0.0 copy-start.1
  0.0 0.0 copy-start.2
  0.0 0.0 copy-start.3
  0.0 0.0 copy-start.4
  0.0 1.7 %edges.1 = (bf16[288,128]{1,0:T(8,128)(2,1)}, bf16[288,128]{1,0:T(8,128)(2,1)}) custom-call(s32[1]{0:T(128)} %bitcast.place_ref, bf16[4096,128]{1,0:T(8,128)(2,1)} %voxels_ref.1, s32[27,4096]{1,0:T(8,128)} %near_ref.3), custom_call_target="tpu_custom_call" | custom-call | flops 20000000000 | bytes 500000 | tf_op jit(solution)/shard_map/edges/pallas_call | solution.py:403
  1.8 2.4 %collective-permute-start = (bf16[288,128]{1,0:T(8,128)(2,1)}, bf16[288,128]{1,0:T(8,128)(2,1)S(1)}, u32[]{:S(2)}, u32[]{:S(2)}) collective-permute-start(bf16[288,128]{1,0:T(8,128)(2,1)} %get-tuple-element.13), channel_id=1, source_target_pairs={{0,1},{1,2},{2,3},{3,4},{4,5},{5,6},{6,7},{7,8},{8,9},{9,10},{10,1... | collective-permute-start | bytes 221192 | tf_op jit(solution)/shard_map/ppermute | solution.py:415
  4.1 1.3 %collective-permute-start.1 = (bf16[288,128]{1,0:T(8,128)(2,1)}, bf16[288,128]{1,0:T(8,128)(2,1)S(1)}, u32[]{:S(2)}, u32[]{:S(2)}) collective-permute-start(bf16[288,128]{1,0:T(8,128)(2,1)} %get-tuple-element.14), channel_id=1, source_target_pairs={{1,0},{2,1},{3,2},{4,3},{5,4},{6,5},{7,6},{8,7},{9,8},{10,9},{11,1... | collective-permute-start | bytes 221192 | tf_op jit(solution)/shard_map/ppermute | solution.py:416
  5.4 0.0 copy-done
  5.4 0.0 copy-done.1
  5.5 0.0 copy-done.2
  5.5 0.0 copy-done.3
  5.5 0.0 copy-done.4
  5.5 19.8 %first_layer.1 = (bf16[128,4096]{1,0:T(8,128)(2,1)S(1)}, bf16[128,4352]{1,0:T(8,128)(2,1)S(1)}, s32[32,128]{1,0:T(8,128)S(1)}, f32[32,128]{1,0:T(8,128)S(1)}, f3...) custom-call(s32[1]{0:T(128)} %bitcast.place_ref, s32[16]{0:T(128)S(1)} %copy-done.4, ...), custom_call_target="tpu_custom_call" | custom-call | flops 20000000000 | bytes 6000000 | tf_op jit(solution)/shard_map/first_layer/pallas_call | solution.py:422
  25.3 0.0 collective-permute-done.low_ref
  25.3 0.0 collective-permute-done.1.high_ref
  25.3 22.8 %second_layer.1 = bf16[16,272,128]{2,1,0:T(8,128)(2,1)S(1)} custom-call(s32[1]{0:T(128)} %bitcast.place_ref, s32[16]{0:T(128)S(1)} %copy-done.4, bf16[288,128]{1,0:T(8,128)(2,1)S(1)} %collective-permute-done.low_ref, bf16[288,128]{1,0:T(8,128)(2,1)S(1)} %collective-permute-done.1.high_ref, bf16[128,4096]{1,0:T(8,128)(2,1)S(1)} %get-tuple-element.15.act_ref, ...), custom_call_target="tpu_custom_call" | custom-call | flops 30000001024 | bytes 8000000 | tf_op jit(solution)/shard_map/second_layer/pallas_call | solution.py:440
  48.1 37.6 %all_to_all.5.got_ref = bf16[16,272,128]{2,1,0:T(8,128)(2,1)S(1)} all-to-all(bf16[16,272,128]{2,1,0:T(8,128)(2,1)S(1)} %second_layer.1), channel_id=1, replica_groups=mesh['groups'=2,'wide'=8,'narrow'=2] {'wide','narrow'}, dimensions={0} | all-to-all | bytes 2228224 | tf_op jit(solution)/shard_map/all_to_all | solution.py:458
  85.8 5.7 %hilbert_order.1 = bf16[4096,128]{1,0:T(8,128)(2,1)} custom-call(bf16[16,272,128]{2,1,0:T(8,128)(2,1)S(1)} %all_to_all.5.got_ref), custom_call_target="tpu_custom_call" | custom-call | tf_op jit(solution)/shard_map/hilbert_order/pallas_call | solution.py:459
Async XLA Ops:
  0.0 5.4 %copy-start = (bf16[4096,128]{1,0:T(8,128)(2,1)S(1)}, bf16[4096,128]{1,0:T(8,128)(2,1)}, u32[]{:S(2)}) copy-start(bf16[4096,128]{1,0:T(8,128)(2,1)} %voxels_ref.1) | copy-start | bytes 3145732
  0.0 5.4 %copy-start.1 = (s32[27,4096]{1,0:T(8,128)S(1)}, s32[27,4096]{1,0:T(8,128)}, u32[]{:S(2)}) copy-start(s32[27,4096]{1,0:T(8,128)} %near_ref.3) | copy-start | bytes 1327108
  0.0 5.5 %copy-start.2 = (bf16[2,128,128]{2,1,0:T(8,128)(2,1)S(1)}, bf16[2,128,128]{2,1,0:T(8,128)(2,1)}, u32[]{:S(2)}) copy-start(bf16[2,128,128]{2,1,0:T(8,128)(2,1)} %linear_ref.3) | copy-start | bytes 196612
  0.0 5.5 %copy-start.3 = (s32[4096]{0:T(1024)S(1)}, s32[4096]{0:T(1024)}, u32[]{:S(2)}) copy-start(s32[4096]{0:T(1024)} %param.11) | copy-start | bytes 49156
  0.0 5.5 %copy-start.4 = (s32[16]{0:T(128)S(1)}, s32[16]{0:T(128)}, u32[]{:S(2)}) copy-start(s32[16]{0:T(128)} %counts_ref.3) | copy-start | bytes 196
  1.8 23.6 %collective-permute-start = (bf16[288,128]{1,0:T(8,128)(2,1)}, bf16[288,128]{1,0:T(8,128)(2,1)S(1)}, u32[]{:S(2)}, u32[]{:S(2)}) collective-permute-start(bf16[288,128]{1,0:T(8,128)(2,1)} %get-tuple-element.13), channel_id=1, source_target_pairs={{0,1},{1,2},{2,3},{3,4},{4,5},{5,6},{6,7},{7,8},{8,9},{9,10},{10,1... | collective-permute-start | bytes 221192 | tf_op jit(solution)/shard_map/ppermute | solution.py:415
  4.1 21.2 %collective-permute-start.1 = (bf16[288,128]{1,0:T(8,128)(2,1)}, bf16[288,128]{1,0:T(8,128)(2,1)S(1)}, u32[]{:S(2)}, u32[]{:S(2)}) collective-permute-start(bf16[288,128]{1,0:T(8,128)(2,1)} %get-tuple-element.14), channel_id=1, source_target_pairs={{1,0},{2,1},{3,2},{4,3},{5,4},{6,5},{7,6},{8,7},{9,8},{10,9},{11,1... | collective-permute-start | bytes 221192 | tf_op jit(solution)/shard_map/ppermute | solution.py:416

commit v5 on v4

--- a/solution.py
+++ b/solution.py
@@ -99,24 +99,29 @@
     return own, before, counts_ref[own], after
 
 
-def slots_tile(c, destination_ref, before_ref, total_ref):
+def slots_table(destination_ref, shards):
     rows = destination_ref.shape[1]
-    shards, tile = before_ref.shape
+    capacity = rows // shards
     groups = rows // 128
+    tile = 256
     earlier = (
         lax.broadcasted_iota(jnp.int32, (tile, tile), 0) < lax.broadcasted_iota(jnp.int32, (tile, tile), 1)
     ).astype(F32).astype(BF16)
+    ones = jnp.ones((tile, tile), BF16)
     devices = lax.broadcasted_iota(jnp.int32, (shards, tile), 0)
-    goal = destination_ref[:, columns(c * tile)]
-    device = goal >> (rows.bit_length() - 1)
-    place = goal & (rows - 1)
-    member = (jnp.broadcast_to(device, (shards, tile)) == devices).astype(F32)
-    member16 = member.astype(BF16)
-    before = before_ref[...]
-    slot = jnp.sum(member * (dot(member16, earlier) + before), axis=0, keepdims=True).astype(jnp.int32)
-    before_ref[...] = before + dot(member16, jnp.ones((tile, tile), BF16))
-    row = c * tile + lax.broadcasted_iota(jnp.int32, (1, tile), 1)
-    total_ref[...] += scatter_term(slot, (row, place), groups)
+    before = (devices * capacity).astype(F32)
+    total = jnp.zeros((4 * groups, 128), F32)
+    for c in range(rows // tile):
+        goal = destination_ref[:, c * tile : (c + 1) * tile]
+        device = goal >> (rows.bit_length() - 1)
+        place = goal & (rows - 1)
+        member = (jnp.broadcast_to(device, (shards, tile)) == devices).astype(F32)
+        member16 = member.astype(BF16)
+        slot = jnp.sum(member * (dot(member16, earlier) + before), axis=0, keepdims=True).astype(jnp.int32)
+        before = before + dot(member16, ones)
+        row = c * tile + lax.broadcasted_iota(jnp.int32, (1, tile), 1)
+        total = total + scatter_term(slot, (row, place), groups)
+    return total
 
 
 def scatter_term(at, values, groups):
@@ -168,17 +173,17 @@
 def inner_kernel(
     shards, place_ref, counts_ref, voxels_ref, near_ref, weight_hbm, linear_ref, destination_ref,
     act_ref, next_ref, perm_ref, high_ref, low_ref, turned_ref,
-    weight_ref, even, odd, conv, before_ref, total_ref, sem,
+    weight_ref, even, odd, conv, sem,
 ):
     weights_in = pltpu.make_async_copy(weight_hbm, weight_ref, sem)
     weights_in.start()
     rows, channels = voxels_ref.shape
     own, before, count, after = device_counts(place_ref, counts_ref)
-    before_ref[...] = (lax.broadcasted_iota(jnp.int32, before_ref.shape, 0) * (rows // shards)).astype(F32)
-    total_ref[...] = jnp.zeros_like(total_ref)
-    slots = lambda c: slots_tile(c, destination_ref, before_ref, total_ref)
-    slots(0)
-    slots(1)
+    groups = rows // 128
+    total = slots_table(destination_ref, shards)
+    perm_ref[...] = joined(total, 0, groups)
+    high_ref[...] = total[2 * groups : 3 * groups, :]
+    low_ref[...] = total[3 * groups :, :]
     for c in range(rows // BLOCK):
         live = live_lanes(c * BLOCK, BLOCK, rows, before, count, after)
         block = voxels_ref[c * BLOCK : (c + 1) * BLOCK, :].T
@@ -200,10 +205,8 @@
 
     def step(t, _):
         gather(2 * t + 1, even)
-        slots(2 * t + 2)
         convolve(2 * t, odd)
         gather(2 * t + 2, odd)
-        slots(2 * t + 3)
         convolve(2 * t + 1, even)
         return 0
 
@@ -220,10 +223,6 @@
         )
 
     in_turn(1, blocks, norm)
-    groups = rows // 128
-    perm_ref[...] = joined(total_ref[...], 0, groups)
-    high_ref[...] = total_ref[2 * groups : 3 * groups, :]
-    low_ref[...] = total_ref[3 * groups :, :]
 
 
 def in_turn(first, last, body):
@@ -240,12 +239,11 @@
 
 def outer_kernel(
     place_ref, counts_ref, low_ref, high_ref, act_ref, inner_ref, near_ref, turned_ref, linear_ref,
-    perm_ref, place_high_ref, place_low_ref, send_ref, even, odd, edge, padded, conv, last,
+    perm_ref, place_high_ref, place_low_ref, send_ref, even, odd, edge, edge_conv, padded, conv, last,
 ):
     channels, rows = act_ref.shape
     own, before, count, after = device_counts(place_ref, counts_ref)
     extent = 2 * HALO
-    linear = linear_ref[0].T
     lanes = lax.broadcasted_iota(jnp.int32, (1, HALO), 1)
 
     def reached(halo_ref, base):
@@ -273,20 +271,21 @@
             axis=1,
         ),
     )
-    picks = (even, odd)
-    for n in range(2):
-        gather_block(lambda at, size: edges[n][:, at : at + size], near[n], picks[n])
-    for n in range(2):
-        conv[:, n * BLOCK : (n + 1) * BLOCK] = dot(turned_ref[0], picks[n][...]).astype(BF16)
-    for n in range(2):
+    blocks = rows // BLOCK
+    padded[:, BLOCK:rows] = inner_ref[:, BLOCK:rows]
+
+    def gather_edge(n, picked):
+        gather_block(lambda at, size: edges[n][:, at : at + size], near[n], picked)
+
+    def convolve_edge(n, picked):
+        edge_conv[:, n * BLOCK : (n + 1) * BLOCK] = dot(turned_ref[0], picked[...]).astype(BF16)
+
+    def norm_edge(n):
         at = n * rows
         live = live_lanes(at - HALO, BLOCK, rows, before, count, after)
         padded[:, at : at + BLOCK] = norm_block(
-            edges[n][:, HALO : HALO + BLOCK], conv[:, n * BLOCK : (n + 1) * BLOCK], linear, live
+            edges[n][:, HALO : HALO + BLOCK], edge_conv[:, n * BLOCK : (n + 1) * BLOCK], linear_ref[0].T, live
         )
-    padded[:, BLOCK:rows] = inner_ref[:, BLOCK:rows]
-
-    linear = linear_ref[1].T
 
     def gather(b, picked):
         first = b * BLOCK
@@ -294,24 +293,38 @@
         gather_block(lambda at, n: padded[:, pl.ds(pl.multiple_of(first + at, HALO), n)], targets, picked)
 
     def convolve(b, picked):
-        conv[:, columns((b + 1) * BLOCK)] = dot(turned_ref[1], picked[...]).astype(BF16)
+        conv[:, columns(b * BLOCK)] = dot(turned_ref[1], picked[...]).astype(BF16)
+
+    gather_edge(0, even)
+    gather_edge(1, odd)
+    convolve_edge(0, even)
+    gather(1, even)
+    convolve_edge(1, odd)
 
     def step(t, _):
-        gather(2 * t, even)
-        convolve(2 * t - 1, odd)
-        gather(2 * t + 1, odd)
-        convolve(2 * t, even)
+        gather(2 * t + 2, odd)
+        convolve(2 * t + 1, even)
+        gather(2 * t + 3, even)
+        convolve(2 * t + 2, odd)
         return 0
 
-    blocks = rows // BLOCK
-    lax.fori_loop(0, blocks // 2, step, 0)
+    lax.fori_loop(0, (blocks - 4) // 2, step, 0)
+    norm_edge(0)
+    norm_edge(1)
+    gather(blocks - 2, odd)
+    convolve(blocks - 3, even)
+    gather(0, even)
+    convolve(blocks - 2, odd)
+    gather(blocks - 1, odd)
+    convolve(0, even)
     convolve(blocks - 1, odd)
+    linear = linear_ref[1].T
 
     def norm(b):
         first = b * BLOCK
         live = live_lanes(first, BLOCK, rows, before, count, after)
         last[:, columns(first)] = norm_block(
-            padded[:, columns(first + HALO)], conv[:, columns(first + BLOCK)], linear, live
+            padded[:, columns(first + HALO)], conv[:, columns(first)], linear, live
         )
 
     in_turn(0, blocks, norm)
@@ -333,7 +346,7 @@
         send_ref[d, capacity:, :] = extra.astype(BF16)
 
 
-def reorder(source, from_ref, store, dots=6, unroll=8):
+def reorder(source, from_ref, store, dots=6, unroll=16):
     channels, rows = source.shape
     windows = rows // WINDOW
 
@@ -370,14 +383,14 @@
     groups = rows // 128
     capacity = rows // shards
     held = capacity // 128
-    lanes = lax.broadcasted_iota(jnp.int32, (1, 128), 1)
+    lanes = lax.broadcasted_iota(jnp.int32, (1, capacity), 1)
     total = jnp.zeros((2 * groups, 128), F32)
     for s in range(shards):
         turned[:, s * capacity : (s + 1) * capacity] = got_ref[s, 0:capacity, :].T
         extra = got_ref[s, capacity:, :].astype(F32)
         place = (extra[0:held, :] * 64.0 + extra[held : 2 * held, :]).astype(jnp.int32)
-        for h in range(held):
-            total = total + scatter_term(place[h : h + 1, :], (s * capacity + h * 128 + lanes,), groups)
+        place = jnp.concatenate([place[h : h + 1, :] for h in range(held)], axis=1)
+        total = total + scatter_term(place, (s * capacity + lanes,), groups)
     from_ref[...] = joined(total, 0, groups)
 
     def store(b, block):
@@ -428,8 +441,7 @@
         in_specs=[smem, smem, vmem, vmem, hbm, vmem, vmem],
         out_specs=(vmem,) * 6,
         scratch_shapes=[
-            VMEM(conv_weight.shape, BF16), picked, picked, VMEM(padded, BF16), VMEM((shards, BLOCK), F32),
-            VMEM((4 * rows // 128, 128), F32), pltpu.SemaphoreType.DMA,
+            VMEM(conv_weight.shape, BF16), picked, picked, VMEM(padded, BF16), pltpu.SemaphoreType.DMA,
         ],
         compiler_params=params(),
         cost_estimate=pl.CostEstimate(flops=20_000_000_000, bytes_accessed=6_000_000, transcendentals=0),
@@ -446,8 +458,9 @@
             picked,
             picked,
             VMEM((channels, 2 * WINDOW), BF16),
+            VMEM((channels, 2 * BLOCK), BF16),
             VMEM(padded, BF16),
-            VMEM(padded, BF16),
+            VMEM((channels, rows), BF16),
             VMEM((channels, rows), BF16),
         ],
         compiler_params=params(),

time: 91.7 us -> 88.8 us (0.968)
  Pallas kernels: 50 us -> 47.2 us
    pallas_call x1, Pallas kernels: 19.8 us -> 18.2 us  [local(): pl.pallas_call(functools.partial(inner_kernel, shards), out_shape=(struct...]
    pallas_call x1, Pallas kernels: 22.8 us -> 21.4 us  [local(): pl.pallas_call(outer_kernel, out_shape=struct((shards, depth, channels),...]
  transfers between devices with their start and end apart: 2 -> 2, of which waited for: 0 -> 0; matrix products, arithmetic and copies ran while one was open for 0% -> 0% of each run, Pallas kernels for 22% -> 21%
where the time goes in v5:
time: 88.8 us; the launch traced here: 88.6 us
  Pallas kernels  47.2 us (53%)
  blocking collectives  37.6 us (42%)
  starting transfers between devices  3.66 us (4%)
    all_to_all x1, blocking collectives, local(): got = lax.all_to_all(send, both, split_axis=0, concat_axis=0, tiled=True)  37.6 us
    pallas_call x1, Pallas kernels, local(): pl.pallas_call(outer_kernel, out_shape=struct((shards, depth, channels),...  21.4 us
    pallas_call x1, Pallas kernels, local(): pl.pallas_call(functools.partial(inner_kernel, shards), out_shape=(struct...  18.2 us
    pallas_call x1, Pallas kernels, local(): pl.pallas_call(final_kernel, out_shape=struct((rows, channels), BF16), in...  5.82 us
    ppermute x1, starting transfers between devices, local(): low = lax.ppermute(final, both, forward)  2.37 us
  transfers between devices with their start and end apart: 2, of which 0 were waited for; matrix products, arithmetic and copies ran while one was open for 0% of the time, Pallas kernels for 21%

profile of v5, /device:TPU:0, one launch (start us, length us, event | category | flops | bytes accessed | tf_op | source)
XLA Modules:
  0.0 88.6 jit_solution(2375874762992766061)
XLA Ops:
  0.0 0.0 copy-start
  0.0 0.0 copy-start.1
  0.0 0.0 copy-start.2
  0.0 0.0 copy-start.3
  0.0 0.0 copy-start.4
  0.0 1.7 %edges.1 = (bf16[288,128]{1,0:T(8,128)(2,1)}, bf16[288,128]{1,0:T(8,128)(2,1)}) custom-call(s32[1]{0:T(128)} %bitcast.place_ref, bf16[4096,128]{1,0:T(8,128)(2,1)} %voxels_ref.1, s32[27,4096]{1,0:T(8,128)} %near_ref.3), custom_call_target="tpu_custom_call" | custom-call | flops 20000000000 | bytes 500000 | tf_op jit(solution)/shard_map/edges/pallas_call | solution.py:416
  1.8 2.4 %collective-permute-start = (bf16[288,128]{1,0:T(8,128)(2,1)}, bf16[288,128]{1,0:T(8,128)(2,1)S(1)}, u32[]{:S(2)}, u32[]{:S(2)}) collective-permute-start(bf16[288,128]{1,0:T(8,128)(2,1)} %get-tuple-element.13), channel_id=1, source_target_pairs={{0,1},{1,2},{2,3},{3,4},{4,5},{5,6},{6,7},{7,8},{8,9},{9,10},{10,1... | collective-permute-start | bytes 221192 | tf_op jit(solution)/shard_map/ppermute | solution.py:428
  4.1 1.3 %collective-permute-start.1 = (bf16[288,128]{1,0:T(8,128)(2,1)}, bf16[288,128]{1,0:T(8,128)(2,1)S(1)}, u32[]{:S(2)}, u32[]{:S(2)}) collective-permute-start(bf16[288,128]{1,0:T(8,128)(2,1)} %get-tuple-element.14), channel_id=1, source_target_pairs={{1,0},{2,1},{3,2},{4,3},{5,4},{6,5},{7,6},{8,7},{9,8},{10,9},{11,1... | collective-permute-start | bytes 221192 | tf_op jit(solution)/shard_map/ppermute | solution.py:429
  5.4 0.0 copy-done
  5.4 0.0 copy-done.1
  5.5 0.0 copy-done.2
  5.5 0.0 copy-done.3
  5.5 0.0 copy-done.4
  5.5 18.2 %first_layer.1 = (bf16[128,4096]{1,0:T(8,128)(2,1)S(1)}, bf16[128,4352]{1,0:T(8,128)(2,1)S(1)}, s32[32,128]{1,0:T(8,128)S(1)}, f32[32,128]{1,0:T(8,128)S(1)}, f3...) custom-call(s32[1]{0:T(128)} %bitcast.place_ref, s32[16]{0:T(128)S(1)} %copy-done.4, ...), custom_call_target="tpu_custom_call" | custom-call | flops 20000000000 | bytes 6000000 | tf_op jit(solution)/shard_map/first_layer/pallas_call | solution.py:435
  23.7 0.0 collective-permute-done.low_ref
  23.7 0.0 collective-permute-done.1.high_ref
  23.7 21.4 %second_layer.1 = bf16[16,272,128]{2,1,0:T(8,128)(2,1)S(1)} custom-call(s32[1]{0:T(128)} %bitcast.place_ref, s32[16]{0:T(128)S(1)} %copy-done.4, bf16[288,128]{1,0:T(8,128)(2,1)S(1)} %collective-permute-done.low_ref, bf16[288,128]{1,0:T(8,128)(2,1)S(1)} %collective-permute-done.1.high_ref, bf16[128,4096]{1,0:T(8,128)(2,1)S(1)} %get-tuple-element.15.act_ref, ...), custom_call_target="tpu_custom_call" | custom-call | flops 30000001024 | bytes 8000000 | tf_op jit(solution)/shard_map/second_layer/pallas_call | solution.py:452
  45.2 37.6 %all_to_all.5.got_ref = bf16[16,272,128]{2,1,0:T(8,128)(2,1)S(1)} all-to-all(bf16[16,272,128]{2,1,0:T(8,128)(2,1)S(1)} %second_layer.1), channel_id=1, replica_groups=mesh['groups'=2,'wide'=8,'narrow'=2] {'wide','narrow'}, dimensions={0} | all-to-all | bytes 2228224 | tf_op jit(solution)/shard_map/all_to_all | solution.py:471
  82.8 5.8 %hilbert_order.1 = bf16[4096,128]{1,0:T(8,128)(2,1)} custom-call(bf16[16,272,128]{2,1,0:T(8,128)(2,1)S(1)} %all_to_all.5.got_ref), custom_call_target="tpu_custom_call" | custom-call | tf_op jit(solution)/shard_map/hilbert_order/pallas_call | solution.py:472
Async XLA Ops:
  0.0 5.4 %copy-start = (bf16[4096,128]{1,0:T(8,128)(2,1)S(1)}, bf16[4096,128]{1,0:T(8,128)(2,1)}, u32[]{:S(2)}) copy-start(bf16[4096,128]{1,0:T(8,128)(2,1)} %voxels_ref.1) | copy-start | bytes 3145732
  0.0 5.4 %copy-start.1 = (s32[27,4096]{1,0:T(8,128)S(1)}, s32[27,4096]{1,0:T(8,128)}, u32[]{:S(2)}) copy-start(s32[27,4096]{1,0:T(8,128)} %near_ref.3) | copy-start | bytes 1327108
  0.0 5.5 %copy-start.2 = (bf16[2,128,128]{2,1,0:T(8,128)(2,1)S(1)}, bf16[2,128,128]{2,1,0:T(8,128)(2,1)}, u32[]{:S(2)}) copy-start(bf16[2,128,128]{2,1,0:T(8,128)(2,1)} %linear_ref.3) | copy-start | bytes 196612
  0.0 5.5 %copy-start.3 = (s32[4096]{0:T(1024)S(1)}, s32[4096]{0:T(1024)}, u32[]{:S(2)}) copy-start(s32[4096]{0:T(1024)} %param.11) | copy-start | bytes 49156
  0.0 5.5 %copy-start.4 = (s32[16]{0:T(128)S(1)}, s32[16]{0:T(128)}, u32[]{:S(2)}) copy-start(s32[16]{0:T(128)} %counts_ref.3) | copy-start | bytes 196
  1.8 22.0 %collective-permute-start = (bf16[288,128]{1,0:T(8,128)(2,1)}, bf16[288,128]{1,0:T(8,128)(2,1)S(1)}, u32[]{:S(2)}, u32[]{:S(2)}) collective-permute-start(bf16[288,128]{1,0:T(8,128)(2,1)} %get-tuple-element.13), channel_id=1, source_target_pairs={{0,1},{1,2},{2,3},{3,4},{4,5},{5,6},{6,7},{7,8},{8,9},{9,10},{10,1... | collective-permute-start | bytes 221192 | tf_op jit(solution)/shard_map/ppermute | solution.py:428
  4.1 19.6 %collective-permute-start.1 = (bf16[288,128]{1,0:T(8,128)(2,1)}, bf16[288,128]{1,0:T(8,128)(2,1)S(1)}, u32[]{:S(2)}, u32[]{:S(2)}) collective-permute-start(bf16[288,128]{1,0:T(8,128)(2,1)} %get-tuple-element.14), channel_id=1, source_target_pairs={{1,0},{2,1},{3,2},{4,3},{5,4},{6,5},{7,6},{8,7},{9,8},{10,9},{11,1... | collective-permute-start | bytes 221192 | tf_op jit(solution)/shard_map/ppermute | solution.py:429

commit v6 on v5

--- a/solution.py
+++ b/solution.py
@@ -107,33 +107,35 @@
     earlier = (
         lax.broadcasted_iota(jnp.int32, (tile, tile), 0) < lax.broadcasted_iota(jnp.int32, (tile, tile), 1)
     ).astype(F32).astype(BF16)
-    ones = jnp.ones((tile, tile), BF16)
     devices = lax.broadcasted_iota(jnp.int32, (shards, tile), 0)
+    tiles = rows // tile
+    goals = [destination_ref[:, c * tile : (c + 1) * tile] for c in range(tiles)]
+    members = [
+        (jnp.broadcast_to(goal >> (rows.bit_length() - 1), (shards, tile)) == devices).astype(F32) for goal in goals
+    ]
+    stacked = jnp.concatenate([member.astype(BF16) for member in members], axis=0)
+    ranks = dot(stacked, earlier)
+    sums = dot(stacked, jnp.ones((tile, tile), BF16))
     before = (devices * capacity).astype(F32)
     total = jnp.zeros((4 * groups, 128), F32)
-    for c in range(rows // tile):
-        goal = destination_ref[:, c * tile : (c + 1) * tile]
-        device = goal >> (rows.bit_length() - 1)
-        place = goal & (rows - 1)
-        member = (jnp.broadcast_to(device, (shards, tile)) == devices).astype(F32)
-        member16 = member.astype(BF16)
-        slot = jnp.sum(member * (dot(member16, earlier) + before), axis=0, keepdims=True).astype(jnp.int32)
-        before = before + dot(member16, ones)
+    for c in range(tiles):
+        part = slice(c * shards, (c + 1) * shards)
+        slot = jnp.sum(members[c] * (ranks[part, :] + before), axis=0, keepdims=True).astype(jnp.int32)
+        before = before + sums[part, :]
         row = c * tile + lax.broadcasted_iota(jnp.int32, (1, tile), 1)
-        total = total + scatter_term(slot, (row, place), groups)
+        total = total + scatter_term(slot, (row, goals[c] & (rows - 1)), groups)
     return total
 
 
 def scatter_term(at, values, groups):
-    tile = at.shape[1]
-    high = (lax.broadcasted_iota(jnp.int32, (groups, tile), 0) == jnp.broadcast_to(at >> 7, (groups, tile))).astype(F32)
-    low = (lax.broadcasted_iota(jnp.int32, (128, tile), 0) == jnp.broadcast_to(at & 127, (128, tile))).astype(F32)
+    high = selector(at >> 7, groups)
     parts = []
     for value in values:
-        parts.append(high * (value >> 6).astype(F32))
-        parts.append(high * (value & 63).astype(F32))
-    left = jnp.concatenate(parts, axis=0).astype(BF16)
-    return lax.dot_general(left, low.astype(BF16), (((1,), (1,)), ((), ())), preferred_element_type=F32)
+        for part in (value >> 6, value & 63):
+            parts.append(high * jnp.broadcast_to(part.astype(F32).astype(BF16), high.shape))
+    left = jnp.concatenate(parts, axis=0)
+    low = selector(at & 127, 128)
+    return lax.dot_general(left, low, (((1,), (1,)), ((), ())), preferred_element_type=F32)
 
 
 def joined(total, n, groups):
@@ -225,9 +227,9 @@
     in_turn(1, blocks, norm)
 
 
-def in_turn(first, last, body):
+def in_turn(first, last, body, most=16):
     count = last - first
-    unroll = max(u for u in range(1, 6) if count % u == 0)
+    unroll = max(u for u in range(1, most + 1) if count % u == 0)
 
     def step(t, _):
         for u in range(unroll):
@@ -377,7 +379,7 @@
     lax.fori_loop(0, rows // BLOCK // unroll, step, 0)
 
 
-def final_kernel(got_ref, out_ref, turned, from_ref):
+def final_kernel(got_ref, out_hbm, out_ref, turned, from_ref, sems):
     rows = out_ref.shape[0]
     shards = got_ref.shape[0]
     groups = rows // 128
@@ -393,10 +395,17 @@
         total = total + scatter_term(place, (s * capacity + lanes,), groups)
     from_ref[...] = joined(total, 0, groups)
 
+    def copy(b):
+        at = pl.ds(pl.multiple_of(b * BLOCK, BLOCK), BLOCK)
+        return pltpu.make_async_copy(out_ref.at[at, :], out_hbm.at[at, :], sems.at[b])
+
     def store(b, block):
         out_ref[pl.ds(pl.multiple_of(b * BLOCK, BLOCK), BLOCK), :] = block
+        copy(b).start()
 
     reorder(turned, from_ref, store)
+    for b in range(rows // BLOCK):
+        copy(b).wait()
 
 
 def local(voxels, counts, neighbours, conv_weight, linear_weight, destination):
@@ -473,8 +482,11 @@
         final_kernel,
         out_shape=struct((rows, channels), BF16),
         in_specs=[vmem],
-        out_specs=vmem,
-        scratch_shapes=[VMEM((channels, rows), BF16), VMEM(table, jnp.int32)],
+        out_specs=hbm,
+        scratch_shapes=[
+            VMEM((rows, channels), BF16), VMEM((channels, rows), BF16), VMEM(table, jnp.int32),
+            pltpu.SemaphoreType.DMA((rows // BLOCK,)),
+        ],
         compiler_params=params(),
         name="hilbert_order",
     )(got)

time: 88.8 us -> 87.6 us (0.986)
  Pallas kernels: 47.2 us -> 45.8 us
  transfers between devices with their start and end apart: 2 -> 2, of which waited for: 0 -> 0; matrix products, arithmetic and copies ran while one was open for 0% -> 0% of each run, Pallas kernels for 21% -> 20%
where the time goes in v6:
time: 87.6 us; the launch traced here: 87.4 us
  Pallas kernels  45.8 us (52%)
  blocking collectives  37.6 us (43%)
  starting transfers between devices  3.66 us (4%)
    all_to_all x1, blocking collectives, local(): got = lax.all_to_all(send, both, split_axis=0, concat_axis=0, tiled=True)  37.6 us
    pallas_call x1, Pallas kernels, local(): pl.pallas_call(outer_kernel, out_shape=struct((shards, depth, channels),...  20.8 us
    pallas_call x1, Pallas kernels, local(): pl.pallas_call(functools.partial(inner_kernel, shards), out_shape=(struct...  17.6 us
    pallas_call x1, Pallas kernels, local(): pl.pallas_call(final_kernel, out_shape=struct((rows, channels), BF16), in...  5.65 us
    ppermute x1, starting transfers between devices, local(): low = lax.ppermute(final, both, forward)  2.37 us
  transfers between devices with their start and end apart: 2, of which 0 were waited for; matrix products, arithmetic and copies ran while one was open for 0% of the time, Pallas kernels for 20%

profile of v6, /device:TPU:0, one launch (start us, length us, event | category | flops | bytes accessed | tf_op | source)
XLA Modules:
  0.0 87.4 jit_solution(37231074863806896)
XLA Ops:
  0.0 0.0 copy-start
  0.0 0.0 copy-start.1
  0.0 0.0 copy-start.2
  0.0 0.0 copy-start.3
  0.0 0.0 copy-start.4
  0.0 1.7 %edges.1 = (bf16[288,128]{1,0:T(8,128)(2,1)}, bf16[288,128]{1,0:T(8,128)(2,1)}) custom-call(s32[1]{0:T(128)} %bitcast.place_ref, bf16[4096,128]{1,0:T(8,128)(2,1)} %voxels_ref.1, s32[27,4096]{1,0:T(8,128)} %near_ref.3), custom_call_target="tpu_custom_call" | custom-call | flops 20000000000 | bytes 500000 | tf_op jit(solution)/shard_map/edges/pallas_call | solution.py:425
  1.8 2.4 %collective-permute-start = (bf16[288,128]{1,0:T(8,128)(2,1)}, bf16[288,128]{1,0:T(8,128)(2,1)S(1)}, u32[]{:S(2)}, u32[]{:S(2)}) collective-permute-start(bf16[288,128]{1,0:T(8,128)(2,1)} %get-tuple-element.13), channel_id=1, source_target_pairs={{0,1},{1,2},{2,3},{3,4},{4,5},{5,6},{6,7},{7,8},{8,9},{9,10},{10,1... | collective-permute-start | bytes 221192 | tf_op jit(solution)/shard_map/ppermute | solution.py:437
  4.1 1.3 %collective-permute-start.1 = (bf16[288,128]{1,0:T(8,128)(2,1)}, bf16[288,128]{1,0:T(8,128)(2,1)S(1)}, u32[]{:S(2)}, u32[]{:S(2)}) collective-permute-start(bf16[288,128]{1,0:T(8,128)(2,1)} %get-tuple-element.14), channel_id=1, source_target_pairs={{1,0},{2,1},{3,2},{4,3},{5,4},{6,5},{7,6},{8,7},{9,8},{10,9},{11,1... | collective-permute-start | bytes 221192 | tf_op jit(solution)/shard_map/ppermute | solution.py:438
  5.4 0.0 copy-done
  5.4 0.0 copy-done.1
  5.5 0.0 copy-done.2
  5.5 0.0 copy-done.3
  5.5 0.0 copy-done.4
  5.5 17.6 %first_layer.1 = (bf16[128,4096]{1,0:T(8,128)(2,1)S(1)}, bf16[128,4352]{1,0:T(8,128)(2,1)S(1)}, s32[32,128]{1,0:T(8,128)S(1)}, f32[32,128]{1,0:T(8,128)S(1)}, f3...) custom-call(s32[1]{0:T(128)} %bitcast.place_ref, s32[16]{0:T(128)S(1)} %copy-done.4, ...), custom_call_target="tpu_custom_call" | custom-call | flops 20000000000 | bytes 6000000 | tf_op jit(solution)/shard_map/first_layer/pallas_call | solution.py:444
  23.1 0.0 collective-permute-done.low_ref
  23.1 0.0 collective-permute-done.1.high_ref
  23.1 20.8 %second_layer.1 = bf16[16,272,128]{2,1,0:T(8,128)(2,1)S(1)} custom-call(s32[1]{0:T(128)} %bitcast.place_ref, s32[16]{0:T(128)S(1)} %copy-done.4, bf16[288,128]{1,0:T(8,128)(2,1)S(1)} %collective-permute-done.low_ref, bf16[288,128]{1,0:T(8,128)(2,1)S(1)} %collective-permute-done.1.high_ref, bf16[128,4096]{1,0:T(8,128)(2,1)S(1)} %get-tuple-element.15.act_ref, ...), custom_call_target="tpu_custom_call" | custom-call | flops 30000001024 | bytes 8000000 | tf_op jit(solution)/shard_map/second_layer/pallas_call | solution.py:461
  43.9 37.6 %all_to_all.5.got_ref = bf16[16,272,128]{2,1,0:T(8,128)(2,1)S(1)} all-to-all(bf16[16,272,128]{2,1,0:T(8,128)(2,1)S(1)} %second_layer.1), channel_id=1, replica_groups=mesh['groups'=2,'wide'=8,'narrow'=2] {'wide','narrow'}, dimensions={0} | all-to-all | bytes 2228224 | tf_op jit(solution)/shard_map/all_to_all | solution.py:480
  81.5 5.6 %hilbert_order.1 = bf16[4096,128]{1,0:T(8,128)(2,1)} custom-call(bf16[16,272,128]{2,1,0:T(8,128)(2,1)S(1)} %all_to_all.5.got_ref), custom_call_target="tpu_custom_call" | custom-call | tf_op jit(solution)/shard_map/hilbert_order/pallas_call | solution.py:481
Async XLA Ops:
  0.0 5.4 %copy-start = (bf16[4096,128]{1,0:T(8,128)(2,1)S(1)}, bf16[4096,128]{1,0:T(8,128)(2,1)}, u32[]{:S(2)}) copy-start(bf16[4096,128]{1,0:T(8,128)(2,1)} %voxels_ref.1) | copy-start | bytes 3145732
  0.0 5.4 %copy-start.1 = (s32[27,4096]{1,0:T(8,128)S(1)}, s32[27,4096]{1,0:T(8,128)}, u32[]{:S(2)}) copy-start(s32[27,4096]{1,0:T(8,128)} %near_ref.3) | copy-start | bytes 1327108
  0.0 5.5 %copy-start.2 = (bf16[2,128,128]{2,1,0:T(8,128)(2,1)S(1)}, bf16[2,128,128]{2,1,0:T(8,128)(2,1)}, u32[]{:S(2)}) copy-start(bf16[2,128,128]{2,1,0:T(8,128)(2,1)} %linear_ref.3) | copy-start | bytes 196612
  0.0 5.5 %copy-start.3 = (s32[4096]{0:T(1024)S(1)}, s32[4096]{0:T(1024)}, u32[]{:S(2)}) copy-start(s32[4096]{0:T(1024)} %param.11) | copy-start | bytes 49156
  0.0 5.5 %copy-start.4 = (s32[16]{0:T(128)S(1)}, s32[16]{0:T(128)}, u32[]{:S(2)}) copy-start(s32[16]{0:T(128)} %counts_ref.3) | copy-start | bytes 196
  1.8 21.4 %collective-permute-start = (bf16[288,128]{1,0:T(8,128)(2,1)}, bf16[288,128]{1,0:T(8,128)(2,1)S(1)}, u32[]{:S(2)}, u32[]{:S(2)}) collective-permute-start(bf16[288,128]{1,0:T(8,128)(2,1)} %get-tuple-element.13), channel_id=1, source_target_pairs={{0,1},{1,2},{2,3},{3,4},{4,5},{5,6},{6,7},{7,8},{8,9},{9,10},{10,1... | collective-permute-start | bytes 221192 | tf_op jit(solution)/shard_map/ppermute | solution.py:437
  4.1 19.0 %collective-permute-start.1 = (bf16[288,128]{1,0:T(8,128)(2,1)}, bf16[288,128]{1,0:T(8,128)(2,1)S(1)}, u32[]{:S(2)}, u32[]{:S(2)}) collective-permute-start(bf16[288,128]{1,0:T(8,128)(2,1)} %get-tuple-element.14), channel_id=1, source_target_pairs={{1,0},{2,1},{3,2},{4,3},{5,4},{6,5},{7,6},{8,7},{9,8},{10,9},{11,1... | collective-permute-start | bytes 221192 | tf_op jit(solution)/shard_map/ppermute | solution.py:438

commit v7 on v6

--- a/solution.py
+++ b/solution.py
@@ -144,41 +144,41 @@
     return (high * 64.0 + low).astype(jnp.int32)
 
 
-def edges_kernel(place_ref, voxels_hbm, near_hbm, first_ref, last_ref, near_first, near_last, sems):
+def edges_kernel(place_ref, voxels_hbm, near_hbm, pair_ref, side_ref, near_pair, near_side, sems):
     rows = voxels_hbm.shape[0]
     extent = 2 * HALO
-    copies = [
-        pltpu.make_async_copy(source, target, sems.at[n])
-        for n, (source, target) in enumerate(
-            (
-                (near_hbm.at[:, 0:HALO], near_first),
-                (near_hbm.at[:, rows - HALO : rows], near_last),
-                (voxels_hbm.at[0:extent, :], first_ref.at[0:extent, :]),
-                (voxels_hbm.at[rows - extent : rows, :], last_ref.at[0:extent, :]),
-            )
-        )
-    ]
+    own = place_ref[0]
+    odd = own & 1
+    parts = ((pair_ref, near_pair, 1 - odd), (side_ref, near_side, odd))
+    copies = []
+    for n, (out_ref, near_ref, upper) in enumerate(parts):
+        near_at = pl.ds(pl.multiple_of(upper * (rows - HALO), HALO), HALO)
+        voxels_at = pl.ds(pl.multiple_of(upper * (rows - extent), extent), extent)
+        copies.append(pltpu.make_async_copy(near_hbm.at[:, near_at], near_ref, sems.at[n]))
+        copies.append(pltpu.make_async_copy(voxels_hbm.at[voxels_at, :], out_ref.at[0:extent, :], sems.at[2 + n]))
     for copy in copies:
         copy.start()
-    own = place_ref[0]
     lanes = lax.broadcasted_iota(jnp.int32, (1, HALO), 1)
-    for n, (near_ref, out_ref, first) in enumerate(((near_first, first_ref, 0), (near_last, last_ref, rows - HALO))):
-        copies[n].wait()
+    for n, (out_ref, near_ref, upper) in enumerate(parts):
+        copies[2 * n].wait()
         near = near_ref[...]
-        relative = jnp.where(near >= 0, near - (own * rows + first + lanes), ABSENT).astype(F32)
+        relative = jnp.where(near >= 0, near - (own * rows + upper * (rows - HALO) + lanes), ABSENT).astype(F32)
         pad = jnp.zeros((out_ref.shape[0] - extent - near.shape[0], HALO), F32)
         out_ref[extent:, :] = jnp.concatenate([relative, pad], axis=0).astype(BF16)
-    copies[2].wait()
+    copies[1].wait()
     copies[3].wait()
 
 
 def inner_kernel(
     shards, place_ref, counts_ref, voxels_ref, near_ref, weight_hbm, linear_ref, destination_ref,
     act_ref, next_ref, perm_ref, high_ref, low_ref, turned_ref,
-    weight_ref, even, odd, conv, sem,
+    weight_ref, even, odd, conv, sems,
 ):
-    weights_in = pltpu.make_async_copy(weight_hbm, weight_ref, sem)
-    weights_in.start()
+    weights_in = [
+        pltpu.make_async_copy(weight_hbm.at[layer], weight_ref.at[layer], sems.at[layer]) for layer in range(2)
+    ]
+    for copy in weights_in:
+        copy.start()
     rows, channels = voxels_ref.shape
     own, before, count, after = device_counts(place_ref, counts_ref)
     groups = rows // 128
@@ -190,9 +190,8 @@
         live = live_lanes(c * BLOCK, BLOCK, rows, before, count, after)
         block = voxels_ref[c * BLOCK : (c + 1) * BLOCK, :].T
         act_ref[:, c * BLOCK : (c + 1) * BLOCK] = jnp.where(live, block.astype(F32), 0.0).astype(BF16)
-    weights_in.wait()
-    for layer in range(2):
-        turn_weights(weight_ref, layer, turned_ref.at[layer])
+    weights_in[0].wait()
+    turn_weights(weight_ref, 0, turned_ref.at[0])
     linear = linear_ref[0].T
 
     def gather(b, picked):
@@ -225,6 +224,8 @@
         )
 
     in_turn(1, blocks, norm)
+    weights_in[1].wait()
+    turn_weights(weight_ref, 1, turned_ref.at[1])
 
 
 def in_turn(first, last, body, most=16):
@@ -240,11 +241,22 @@
 
 
 def outer_kernel(
-    place_ref, counts_ref, low_ref, high_ref, act_ref, inner_ref, near_ref, turned_ref, linear_ref,
-    perm_ref, place_high_ref, place_low_ref, send_ref, even, odd, edge, edge_conv, padded, conv, last,
+    place_ref, counts_ref, pair_ref, side_ref, act_ref, inner_ref, near_ref, turned_ref, linear_ref,
+    perm_ref, place_high_ref, place_low_ref, send_ref, low_ref, high_ref, even, odd, edge, edge_conv, padded, conv, last,
 ):
     channels, rows = act_ref.shape
     own, before, count, after = device_counts(place_ref, counts_ref)
+
+    @pl.when(own & 1 == 0)
+    def _():
+        low_ref[...] = side_ref[...]
+        high_ref[...] = pair_ref[...]
+
+    @pl.when(own & 1 == 1)
+    def _():
+        low_ref[...] = pair_ref[...]
+        high_ref[...] = side_ref[...]
+
     extent = 2 * HALO
     lanes = lax.broadcasted_iota(jnp.int32, (1, HALO), 1)
 
@@ -422,7 +434,7 @@
     hbm = pl.BlockSpec(memory_space=pltpu.HBM)
 
     packed = struct((extent + 32, channels), BF16)
-    first, final = pl.pallas_call(
+    to_pair, to_side = pl.pallas_call(
         edges_kernel,
         out_shape=(packed, packed),
         in_specs=[smem, hbm, hbm],
@@ -432,10 +444,11 @@
         compiler_params=params(60),
         name="edges",
     )(place, voxels, neighbours)
-    forward = [(i, i + 1) for i in range(shards - 1)]
-    backward = [(target, source) for source, target in forward]
-    low = lax.ppermute(final, both, forward)
-    high = lax.ppermute(first, both, backward)
+    others = [(0, 0), (shards - 1, shards - 1)]
+    for i in range(1, shards - 1, 2):
+        others += [(i, i + 1), (i + 1, i)]
+    side = lax.ppermute(to_side, both, others)
+    pair = lax.ppermute(to_pair, both, [(i, i ^ 1) for i in range(shards)])
 
     table = (rows // 128, 128)
     padded = (channels, rows + BLOCK)
@@ -450,7 +463,7 @@
         in_specs=[smem, smem, vmem, vmem, hbm, vmem, vmem],
         out_specs=(vmem,) * 6,
         scratch_shapes=[
-            VMEM(conv_weight.shape, BF16), picked, picked, VMEM(padded, BF16), pltpu.SemaphoreType.DMA,
+            VMEM(conv_weight.shape, BF16), picked, picked, VMEM(padded, BF16), pltpu.SemaphoreType.DMA((2,)),
         ],
         compiler_params=params(),
         cost_estimate=pl.CostEstimate(flops=20_000_000_000, bytes_accessed=6_000_000, transcendentals=0),
@@ -464,6 +477,8 @@
         in_specs=[smem, smem] + [vmem] * 10,
         out_specs=vmem,
         scratch_shapes=[
+            VMEM(packed.shape, BF16),
+            VMEM(packed.shape, BF16),
             picked,
             picked,
             VMEM((channels, 2 * WINDOW), BF16),
@@ -475,7 +490,7 @@
         compiler_params=params(),
         cost_estimate=pl.CostEstimate(flops=30_000_000_000, bytes_accessed=8_000_000, transcendentals=0),
         name="second_layer",
-    )(place, counts, low, high, act, inner, neighbours, weights, linear_weight, perm, place_high, place_low)
+    )(place, counts, pair, side, act, inner, neighbours, weights, linear_weight, perm, place_high, place_low)
 
     got = lax.all_to_all(send, both, split_axis=0, concat_axis=0, tiled=True)
     return pl.pallas_call(

time: 87.6 us -> 84.7 us (0.967)
  starting transfers between devices: 3.66 us -> 2.06 us
  blocking collectives: 37.6 us -> 36.3 us
    ppermute x2, starting transfers between devices: 3.66 us -> 2.06 us  [the longest x1 1.53 us: local(): side = lax.ppermute(to_side, both, others)]
    all_to_all x1, blocking collectives: 37.6 us -> 36.3 us  [local(): got = lax.all_to_all(send, both, split_axis=0, concat_axis=0, tiled=True)]
  transfers between devices with their start and end apart: 2 -> 2, of which waited for: 0 -> 0; matrix products, arithmetic and copies ran while one was open for 0% -> 0% of each run, Pallas kernels for 20% -> 21%
where the time goes in v7:
time: 84.7 us; the launch traced here: 84.5 us
  Pallas kernels  45.9 us (54%)
  blocking collectives  36.3 us (43%)
  starting transfers between devices  2.06 us (2%)
    all_to_all x1, blocking collectives, local(): got = lax.all_to_all(send, both, split_axis=0, concat_axis=0, tiled=True)  36.3 us
    pallas_call x1, Pallas kernels, local(): pl.pallas_call(outer_kernel, out_shape=struct((shards, depth, channels),...  20.8 us
    pallas_call x1, Pallas kernels, local(): pl.pallas_call(functools.partial(inner_kernel, shards), out_shape=(struct...  17.7 us
    pallas_call x1, Pallas kernels, local(): pl.pallas_call(final_kernel, out_shape=struct((rows, channels), BF16), in...  5.64 us
    pallas_call x1, Pallas kernels, local(): pl.pallas_call(edges_kernel, out_shape=(packed, packed), in_specs=[smem,...  1.72 us
  transfers between devices with their start and end apart: 2, of which 0 were waited for; matrix products, arithmetic and copies ran while one was open for 0% of the time, Pallas kernels for 21%

profile of v7, /device:TPU:0, one launch (start us, length us, event | category | flops | bytes accessed | tf_op | source)
XLA Modules:
  0.0 84.5 jit_solution(11210293949466610200)
XLA Ops:
  0.0 0.0 copy-start
  0.0 0.0 copy-start.1
  0.0 0.0 copy-start.2
  0.0 0.0 copy-start.3
  0.0 0.0 copy-start.4
  0.0 1.7 %edges.1 = (bf16[288,128]{1,0:T(8,128)(2,1)}, bf16[288,128]{1,0:T(8,128)(2,1)}) custom-call(s32[1]{0:T(128)} %bitcast.place_ref, bf16[4096,128]{1,0:T(8,128)(2,1)} %voxels_ref.1, s32[27,4096]{1,0:T(8,128)} %near_ref.3), custom_call_target="tpu_custom_call" | custom-call | flops 20000000000 | bytes 500000 | tf_op jit(solution)/shard_map/edges/pallas_call | solution.py:437
  1.7 0.5 collective-permute-start
  2.3 1.5 %collective-permute-start.1 = (bf16[288,128]{1,0:T(8,128)(2,1)}, bf16[288,128]{1,0:T(8,128)(2,1)S(1)}, u32[]{:S(2)}, u32[]{:S(2)}) collective-permute-start(bf16[288,128]{1,0:T(8,128)(2,1)} %get-tuple-element.14), channel_id=1, source_target_pairs={{0,0},{15,15},{1,2},{2,1},{3,4},{4,3},{5,6},{6,5},{7,8},{8,7},{9,1... | collective-permute-start | bytes 221192 | tf_op jit(solution)/shard_map/ppermute | solution.py:450
  3.8 0.0 copy-done
  3.8 0.0 copy-done.1
  3.8 0.0 copy-done.2
  3.8 0.0 copy-done.3
  3.8 0.0 copy-done.4
  3.8 17.7 %first_layer.1 = (bf16[128,4096]{1,0:T(8,128)(2,1)S(1)}, bf16[128,4352]{1,0:T(8,128)(2,1)S(1)}, s32[32,128]{1,0:T(8,128)S(1)}, f32[32,128]{1,0:T(8,128)S(1)}, f3...) custom-call(s32[1]{0:T(128)} %bitcast.place_ref, s32[16]{0:T(128)S(1)} %copy-done.4, ...), custom_call_target="tpu_custom_call" | custom-call | flops 20000000000 | bytes 6000000 | tf_op jit(solution)/shard_map/first_layer/pallas_call | solution.py:457
  21.5 0.0 collective-permute-done.pair_ref
  21.5 0.0 collective-permute-done.1.side_ref
  21.6 20.8 %second_layer.1 = bf16[16,272,128]{2,1,0:T(8,128)(2,1)S(1)} custom-call(s32[1]{0:T(128)} %bitcast.place_ref, s32[16]{0:T(128)S(1)} %copy-done.4, bf16[288,128]{1,0:T(8,128)(2,1)S(1)} %collective-permute-done.pair_ref, bf16[288,128]{1,0:T(8,128)(2,1)S(1)} %collective-permute-done.1.side_ref, bf16[128,4096]{1,0:T(8,128)(2,1)S(1)} %get-tuple-element.15.act_ref, ...), custom_call_target="tpu_custom_call" | custom-call | flops 30000001024 | bytes 8000000 | tf_op jit(solution)/shard_map/second_layer/pallas_call | solution.py:474
  42.3 36.3 %all_to_all.5.got_ref = bf16[16,272,128]{2,1,0:T(8,128)(2,1)S(1)} all-to-all(bf16[16,272,128]{2,1,0:T(8,128)(2,1)S(1)} %second_layer.1), channel_id=1, replica_groups=mesh['groups'=2,'wide'=8,'narrow'=2] {'wide','narrow'}, dimensions={0} | all-to-all | bytes 2228224 | tf_op jit(solution)/shard_map/all_to_all | solution.py:495
  78.6 5.6 %hilbert_order.1 = bf16[4096,128]{1,0:T(8,128)(2,1)} custom-call(bf16[16,272,128]{2,1,0:T(8,128)(2,1)S(1)} %all_to_all.5.got_ref), custom_call_target="tpu_custom_call" | custom-call | tf_op jit(solution)/shard_map/hilbert_order/pallas_call | solution.py:496
Async XLA Ops:
  0.0 3.8 %copy-start = (bf16[4096,128]{1,0:T(8,128)(2,1)S(1)}, bf16[4096,128]{1,0:T(8,128)(2,1)}, u32[]{:S(2)}) copy-start(bf16[4096,128]{1,0:T(8,128)(2,1)} %voxels_ref.1) | copy-start | bytes 3145732
  0.0 3.8 %copy-start.1 = (s32[27,4096]{1,0:T(8,128)S(1)}, s32[27,4096]{1,0:T(8,128)}, u32[]{:S(2)}) copy-start(s32[27,4096]{1,0:T(8,128)} %near_ref.3) | copy-start | bytes 1327108
  0.0 3.8 %copy-start.2 = (bf16[2,128,128]{2,1,0:T(8,128)(2,1)S(1)}, bf16[2,128,128]{2,1,0:T(8,128)(2,1)}, u32[]{:S(2)}) copy-start(bf16[2,128,128]{2,1,0:T(8,128)(2,1)} %linear_ref.3) | copy-start | bytes 196612
  0.0 3.8 %copy-start.3 = (s32[4096]{0:T(1024)S(1)}, s32[4096]{0:T(1024)}, u32[]{:S(2)}) copy-start(s32[4096]{0:T(1024)} %param.11) | copy-start | bytes 49156
  0.0 3.8 %copy-start.4 = (s32[16]{0:T(128)S(1)}, s32[16]{0:T(128)}, u32[]{:S(2)}) copy-start(s32[16]{0:T(128)} %counts_ref.3) | copy-start | bytes 196
  1.7 19.8 %collective-permute-start = (bf16[288,128]{1,0:T(8,128)(2,1)}, bf16[288,128]{1,0:T(8,128)(2,1)S(1)}, u32[]{:S(2)}, u32[]{:S(2)}) collective-permute-start(bf16[288,128]{1,0:T(8,128)(2,1)} %get-tuple-element.13), channel_id=1, source_target_pairs={{0,1},{1,0},{2,3},{3,2},{4,5},{5,4},{6,7},{7,6},{8,9},{9,8},{10,11... | collective-permute-start | bytes 221192 | tf_op jit(solution)/shard_map/ppermute | solution.py:451
  2.3 19.3 %collective-permute-start.1 = (bf16[288,128]{1,0:T(8,128)(2,1)}, bf16[288,128]{1,0:T(8,128)(2,1)S(1)}, u32[]{:S(2)}, u32[]{:S(2)}) collective-permute-start(bf16[288,128]{1,0:T(8,128)(2,1)} %get-tuple-element.14), channel_id=1, source_target_pairs={{0,0},{15,15},{1,2},{2,1},{3,4},{4,3},{5,6},{6,5},{7,8},{8,7},{9,1... | collective-permute-start | bytes 221192 | tf_op jit(solution)/shard_map/ppermute | solution.py:450

commit v8 on v7

--- a/solution.py
+++ b/solution.py
@@ -177,8 +177,7 @@
     weights_in = [
         pltpu.make_async_copy(weight_hbm.at[layer], weight_ref.at[layer], sems.at[layer]) for layer in range(2)
     ]
-    for copy in weights_in:
-        copy.start()
+    weights_in[0].start()
     rows, channels = voxels_ref.shape
     own, before, count, after = device_counts(place_ref, counts_ref)
     groups = rows // 128
@@ -190,8 +189,6 @@
         live = live_lanes(c * BLOCK, BLOCK, rows, before, count, after)
         block = voxels_ref[c * BLOCK : (c + 1) * BLOCK, :].T
         act_ref[:, c * BLOCK : (c + 1) * BLOCK] = jnp.where(live, block.astype(F32), 0.0).astype(BF16)
-    weights_in[0].wait()
-    turn_weights(weight_ref, 0, turned_ref.at[0])
     linear = linear_ref[0].T
 
     def gather(b, picked):
@@ -203,17 +200,19 @@
         conv[:, columns(b * BLOCK)] = dot(turned_ref[0], picked[...]).astype(BF16)
 
     blocks = rows // BLOCK
+    gather(1, even)
+    weights_in[0].wait()
+    weights_in[1].start()
+    turn_weights(weight_ref, 0, turned_ref.at[0])
 
     def step(t, _):
-        gather(2 * t + 1, even)
-        convolve(2 * t, odd)
         gather(2 * t + 2, odd)
         convolve(2 * t + 1, even)
+        gather(2 * t + 3, even)
+        convolve(2 * t + 2, odd)
         return 0
 
     lax.fori_loop(0, (blocks - 2) // 2, step, 0)
-    gather(blocks - 1, even)
-    convolve(blocks - 2, odd)
     convolve(blocks - 1, even)
 
     def norm(b):

time: 84.7 us -> 83.5 us (0.986)
  Pallas kernels: 45.9 us -> 44.7 us
    pallas_call x1, Pallas kernels: 17.7 us -> 16.5 us  [local(): pl.pallas_call(functools.partial(inner_kernel, shards), out_shape=(struct...]
  transfers between devices with their start and end apart: 2 -> 2, of which waited for: 0 -> 0; matrix products, arithmetic and copies ran while one was open for 0% -> 0% of each run, Pallas kernels for 21% -> 20%
where the time goes in v8:
time: 83.5 us; the launch traced here: 83.3 us
  Pallas kernels  44.7 us (54%)
  blocking collectives  36.3 us (43%)
  starting transfers between devices  2.06 us (2%)
    all_to_all x1, blocking collectives, local(): got = lax.all_to_all(send, both, split_axis=0, concat_axis=0, tiled=True)  36.3 us
    pallas_call x1, Pallas kernels, local(): pl.pallas_call(outer_kernel, out_shape=struct((shards, depth, channels),...  20.8 us
    pallas_call x1, Pallas kernels, local(): pl.pallas_call(functools.partial(inner_kernel, shards), out_shape=(struct...  16.5 us
    pallas_call x1, Pallas kernels, local(): pl.pallas_call(final_kernel, out_shape=struct((rows, channels), BF16), in...  5.64 us
    pallas_call x1, Pallas kernels, local(): pl.pallas_call(edges_kernel, out_shape=(packed, packed), in_specs=[smem,...  1.72 us
  transfers between devices with their start and end apart: 2, of which 0 were waited for; matrix products, arithmetic and copies ran while one was open for 0% of the time, Pallas kernels for 20%

profile of v8, /device:TPU:0, one launch (start us, length us, event | category | flops | bytes accessed | tf_op | source)
XLA Modules:
  0.0 83.3 jit_solution(1594279697734002036)
XLA Ops:
  0.0 0.0 copy-start
  0.0 0.0 copy-start.1
  0.0 0.0 copy-start.2
  0.0 0.0 copy-start.3
  0.0 0.0 copy-start.4
  0.0 1.7 %edges.1 = (bf16[288,128]{1,0:T(8,128)(2,1)}, bf16[288,128]{1,0:T(8,128)(2,1)}) custom-call(s32[1]{0:T(128)} %bitcast.place_ref, bf16[4096,128]{1,0:T(8,128)(2,1)} %voxels_ref.1, s32[27,4096]{1,0:T(8,128)} %near_ref.3), custom_call_target="tpu_custom_call" | custom-call | flops 20000000000 | bytes 500000 | tf_op jit(solution)/shard_map/edges/pallas_call | solution.py:436
  1.7 0.5 collective-permute-start
  2.3 1.5 %collective-permute-start.1 = (bf16[288,128]{1,0:T(8,128)(2,1)}, bf16[288,128]{1,0:T(8,128)(2,1)S(1)}, u32[]{:S(2)}, u32[]{:S(2)}) collective-permute-start(bf16[288,128]{1,0:T(8,128)(2,1)} %get-tuple-element.14), channel_id=1, source_target_pairs={{0,0},{15,15},{1,2},{2,1},{3,4},{4,3},{5,6},{6,5},{7,8},{8,7},{9,1... | collective-permute-start | bytes 221192 | tf_op jit(solution)/shard_map/ppermute | solution.py:449
  3.8 0.0 copy-done
  3.8 0.0 copy-done.1
  3.8 0.0 copy-done.2
  3.8 0.0 copy-done.3
  3.8 0.0 copy-done.4
  3.8 16.5 %first_layer.1 = (bf16[128,4096]{1,0:T(8,128)(2,1)S(1)}, bf16[128,4352]{1,0:T(8,128)(2,1)S(1)}, s32[32,128]{1,0:T(8,128)S(1)}, f32[32,128]{1,0:T(8,128)S(1)}, f3...) custom-call(s32[1]{0:T(128)} %bitcast.place_ref, s32[16]{0:T(128)S(1)} %copy-done.4, ...), custom_call_target="tpu_custom_call" | custom-call | flops 20000000000 | bytes 6000000 | tf_op jit(solution)/shard_map/first_layer/pallas_call | solution.py:456
  20.4 0.0 collective-permute-done.pair_ref
  20.4 0.0 collective-permute-done.1.side_ref
  20.4 20.8 %second_layer.1 = bf16[16,272,128]{2,1,0:T(8,128)(2,1)S(1)} custom-call(s32[1]{0:T(128)} %bitcast.place_ref, s32[16]{0:T(128)S(1)} %copy-done.4, bf16[288,128]{1,0:T(8,128)(2,1)S(1)} %collective-permute-done.pair_ref, bf16[288,128]{1,0:T(8,128)(2,1)S(1)} %collective-permute-done.1.side_ref, bf16[128,4096]{1,0:T(8,128)(2,1)S(1)} %get-tuple-element.15.act_ref, ...), custom_call_target="tpu_custom_call" | custom-call | flops 30000001024 | bytes 8000000 | tf_op jit(solution)/shard_map/second_layer/pallas_call | solution.py:473
  41.2 36.3 %all_to_all.5.got_ref = bf16[16,272,128]{2,1,0:T(8,128)(2,1)S(1)} all-to-all(bf16[16,272,128]{2,1,0:T(8,128)(2,1)S(1)} %second_layer.1), channel_id=1, replica_groups=mesh['groups'=2,'wide'=8,'narrow'=2] {'wide','narrow'}, dimensions={0} | all-to-all | bytes 2228224 | tf_op jit(solution)/shard_map/all_to_all | solution.py:494
  77.5 5.6 %hilbert_order.1 = bf16[4096,128]{1,0:T(8,128)(2,1)} custom-call(bf16[16,272,128]{2,1,0:T(8,128)(2,1)S(1)} %all_to_all.5.got_ref), custom_call_target="tpu_custom_call" | custom-call | tf_op jit(solution)/shard_map/hilbert_order/pallas_call | solution.py:495
Async XLA Ops:
  0.0 3.8 %copy-start = (bf16[4096,128]{1,0:T(8,128)(2,1)S(1)}, bf16[4096,128]{1,0:T(8,128)(2,1)}, u32[]{:S(2)}) copy-start(bf16[4096,128]{1,0:T(8,128)(2,1)} %voxels_ref.1) | copy-start | bytes 3145732
  0.0 3.8 %copy-start.1 = (s32[27,4096]{1,0:T(8,128)S(1)}, s32[27,4096]{1,0:T(8,128)}, u32[]{:S(2)}) copy-start(s32[27,4096]{1,0:T(8,128)} %near_ref.3) | copy-start | bytes 1327108
  0.0 3.8 %copy-start.2 = (bf16[2,128,128]{2,1,0:T(8,128)(2,1)S(1)}, bf16[2,128,128]{2,1,0:T(8,128)(2,1)}, u32[]{:S(2)}) copy-start(bf16[2,128,128]{2,1,0:T(8,128)(2,1)} %linear_ref.3) | copy-start | bytes 196612
  0.0 3.8 %copy-start.3 = (s32[4096]{0:T(1024)S(1)}, s32[4096]{0:T(1024)}, u32[]{:S(2)}) copy-start(s32[4096]{0:T(1024)} %param.11) | copy-start | bytes 49156
  0.0 3.8 %copy-start.4 = (s32[16]{0:T(128)S(1)}, s32[16]{0:T(128)}, u32[]{:S(2)}) copy-start(s32[16]{0:T(128)} %counts_ref.3) | copy-start | bytes 196
  1.7 18.6 %collective-permute-start = (bf16[288,128]{1,0:T(8,128)(2,1)}, bf16[288,128]{1,0:T(8,128)(2,1)S(1)}, u32[]{:S(2)}, u32[]{:S(2)}) collective-permute-start(bf16[288,128]{1,0:T(8,128)(2,1)} %get-tuple-element.13), channel_id=1, source_target_pairs={{0,1},{1,0},{2,3},{3,2},{4,5},{5,4},{6,7},{7,6},{8,9},{9,8},{10,11... | collective-permute-start | bytes 221192 | tf_op jit(solution)/shard_map/ppermute | solution.py:450
  2.3 18.1 %collective-permute-start.1 = (bf16[288,128]{1,0:T(8,128)(2,1)}, bf16[288,128]{1,0:T(8,128)(2,1)S(1)}, u32[]{:S(2)}, u32[]{:S(2)}) collective-permute-start(bf16[288,128]{1,0:T(8,128)(2,1)} %get-tuple-element.14), channel_id=1, source_target_pairs={{0,0},{15,15},{1,2},{2,1},{3,4},{4,3},{5,6},{6,5},{7,8},{8,7},{9,1... | collective-permute-start | bytes 221192 | tf_op jit(solution)/shard_map/ppermute | solution.py:449

commit v9 on v8

--- a/solution.py
+++ b/solution.py
@@ -222,14 +222,18 @@
             act_ref[:, columns(first)], conv[:, columns(b * BLOCK)], linear, live
         )
 
-    in_turn(1, blocks, norm)
     weights_in[1].wait()
     turn_weights(weight_ref, 1, turned_ref.at[1])
+    in_turn(1, blocks, norm)
 
 
 def in_turn(first, last, body, most=16):
     count = last - first
     unroll = max(u for u in range(1, most + 1) if count % u == 0)
+    if unroll == count:
+        for b in range(first, last):
+            body(b)
+        return
 
     def step(t, _):
         for u in range(unroll):

time: 83.5 us -> 83.8 us (level)
  no operation moved by 1% of the time
where the time goes in v9:
time: 83.8 us; the launch traced here: 83.6 us
  Pallas kernels  45 us (54%)
  blocking collectives  36.3 us (43%)
  starting transfers between devices  2.06 us (2%)
    all_to_all x1, blocking collectives, local(): got = lax.all_to_all(send, both, split_axis=0, concat_axis=0, tiled=True)  36.3 us
    pallas_call x1, Pallas kernels, local(): pl.pallas_call(outer_kernel, out_shape=struct((shards, depth, channels),...  20.8 us
    pallas_call x1, Pallas kernels, local(): pl.pallas_call(functools.partial(inner_kernel, shards), out_shape=(struct...  16.8 us
    pallas_call x1, Pallas kernels, local(): pl.pallas_call(final_kernel, out_shape=struct((rows, channels), BF16), in...  5.64 us
    pallas_call x1, Pallas kernels, local(): pl.pallas_call(edges_kernel, out_shape=(packed, packed), in_specs=[smem,...  1.72 us
  transfers between devices with their start and end apart: 2, of which 0 were waited for; matrix products, arithmetic and copies ran while one was open for 0% of the time, Pallas kernels for 20%

profile of v9, /device:TPU:0, one launch (start us, length us, event | category | flops | bytes accessed | tf_op | source)
XLA Modules:
  0.0 83.6 jit_solution(2517211425776397365)
XLA Ops:
  0.0 0.0 copy-start
  0.0 0.0 copy-start.1
  0.0 0.0 copy-start.2
  0.0 0.0 copy-start.3
  0.0 0.0 copy-start.4
  0.0 1.7 %edges.1 = (bf16[288,128]{1,0:T(8,128)(2,1)}, bf16[288,128]{1,0:T(8,128)(2,1)}) custom-call(s32[1]{0:T(128)} %bitcast.place_ref, bf16[4096,128]{1,0:T(8,128)(2,1)} %voxels_ref.1, s32[27,4096]{1,0:T(8,128)} %near_ref.3), custom_call_target="tpu_custom_call" | custom-call | flops 20000000000 | bytes 500000 | tf_op jit(solution)/shard_map/edges/pallas_call | solution.py:440
  1.7 0.5 collective-permute-start
  2.3 1.5 %collective-permute-start.1 = (bf16[288,128]{1,0:T(8,128)(2,1)}, bf16[288,128]{1,0:T(8,128)(2,1)S(1)}, u32[]{:S(2)}, u32[]{:S(2)}) collective-permute-start(bf16[288,128]{1,0:T(8,128)(2,1)} %get-tuple-element.14), channel_id=1, source_target_pairs={{0,0},{15,15},{1,2},{2,1},{3,4},{4,3},{5,6},{6,5},{7,8},{8,7},{9,1... | collective-permute-start | bytes 221192 | tf_op jit(solution)/shard_map/ppermute | solution.py:453
  3.8 0.0 copy-done
  3.8 0.0 copy-done.1
  3.8 0.0 copy-done.2
  3.8 0.0 copy-done.3
  3.8 0.0 copy-done.4
  3.8 16.8 %first_layer.1 = (bf16[128,4096]{1,0:T(8,128)(2,1)S(1)}, bf16[128,4352]{1,0:T(8,128)(2,1)S(1)}, s32[32,128]{1,0:T(8,128)S(1)}, f32[32,128]{1,0:T(8,128)S(1)}, f3...) custom-call(s32[1]{0:T(128)} %bitcast.place_ref, s32[16]{0:T(128)S(1)} %copy-done.4, ...), custom_call_target="tpu_custom_call" | custom-call | flops 20000000000 | bytes 6000000 | tf_op jit(solution)/shard_map/first_layer/pallas_call | solution.py:460
  20.6 0.0 collective-permute-done.pair_ref
  20.7 0.0 collective-permute-done.1.side_ref
  20.7 20.8 %second_layer.1 = bf16[16,272,128]{2,1,0:T(8,128)(2,1)S(1)} custom-call(s32[1]{0:T(128)} %bitcast.place_ref, s32[16]{0:T(128)S(1)} %copy-done.4, bf16[288,128]{1,0:T(8,128)(2,1)S(1)} %collective-permute-done.pair_ref, bf16[288,128]{1,0:T(8,128)(2,1)S(1)} %collective-permute-done.1.side_ref, bf16[128,4096]{1,0:T(8,128)(2,1)S(1)} %get-tuple-element.15.act_ref, ...), custom_call_target="tpu_custom_call" | custom-call | flops 30000001024 | bytes 8000000 | tf_op jit(solution)/shard_map/second_layer/pallas_call | solution.py:477
  41.5 36.3 %all_to_all.5.got_ref = bf16[16,272,128]{2,1,0:T(8,128)(2,1)S(1)} all-to-all(bf16[16,272,128]{2,1,0:T(8,128)(2,1)S(1)} %second_layer.1), channel_id=1, replica_groups=mesh['groups'=2,'wide'=8,'narrow'=2] {'wide','narrow'}, dimensions={0} | all-to-all | bytes 2228224 | tf_op jit(solution)/shard_map/all_to_all | solution.py:498
  77.7 5.6 %hilbert_order.1 = bf16[4096,128]{1,0:T(8,128)(2,1)} custom-call(bf16[16,272,128]{2,1,0:T(8,128)(2,1)S(1)} %all_to_all.5.got_ref), custom_call_target="tpu_custom_call" | custom-call | tf_op jit(solution)/shard_map/hilbert_order/pallas_call | solution.py:499
Async XLA Ops:
  0.0 3.8 %copy-start = (bf16[4096,128]{1,0:T(8,128)(2,1)S(1)}, bf16[4096,128]{1,0:T(8,128)(2,1)}, u32[]{:S(2)}) copy-start(bf16[4096,128]{1,0:T(8,128)(2,1)} %voxels_ref.1) | copy-start | bytes 3145732
  0.0 3.8 %copy-start.1 = (s32[27,4096]{1,0:T(8,128)S(1)}, s32[27,4096]{1,0:T(8,128)}, u32[]{:S(2)}) copy-start(s32[27,4096]{1,0:T(8,128)} %near_ref.3) | copy-start | bytes 1327108
  0.0 3.8 %copy-start.2 = (bf16[2,128,128]{2,1,0:T(8,128)(2,1)S(1)}, bf16[2,128,128]{2,1,0:T(8,128)(2,1)}, u32[]{:S(2)}) copy-start(bf16[2,128,128]{2,1,0:T(8,128)(2,1)} %linear_ref.3) | copy-start | bytes 196612
  0.0 3.8 %copy-start.3 = (s32[4096]{0:T(1024)S(1)}, s32[4096]{0:T(1024)}, u32[]{:S(2)}) copy-start(s32[4096]{0:T(1024)} %param.11) | copy-start | bytes 49156
  0.0 3.8 %copy-start.4 = (s32[16]{0:T(128)S(1)}, s32[16]{0:T(128)}, u32[]{:S(2)}) copy-start(s32[16]{0:T(128)} %counts_ref.3) | copy-start | bytes 196
  1.7 18.9 %collective-permute-start = (bf16[288,128]{1,0:T(8,128)(2,1)}, bf16[288,128]{1,0:T(8,128)(2,1)S(1)}, u32[]{:S(2)}, u32[]{:S(2)}) collective-permute-start(bf16[288,128]{1,0:T(8,128)(2,1)} %get-tuple-element.13), channel_id=1, source_target_pairs={{0,1},{1,0},{2,3},{3,2},{4,5},{5,4},{6,7},{7,6},{8,9},{9,8},{10,11... | collective-permute-start | bytes 221192 | tf_op jit(solution)/shard_map/ppermute | solution.py:454
  2.3 18.4 %collective-permute-start.1 = (bf16[288,128]{1,0:T(8,128)(2,1)}, bf16[288,128]{1,0:T(8,128)(2,1)S(1)}, u32[]{:S(2)}, u32[]{:S(2)}) collective-permute-start(bf16[288,128]{1,0:T(8,128)(2,1)} %get-tuple-element.14), channel_id=1, source_target_pairs={{0,0},{15,15},{1,2},{2,1},{3,4},{4,3},{5,6},{6,5},{7,8},{8,7},{9,1... | collective-permute-start | bytes 221192 | tf_op jit(solution)/shard_map/ppermute | solution.py:453

commit v10 on v8

--- a/solution.py
+++ b/solution.py
@@ -180,27 +180,27 @@
     weights_in[0].start()
     rows, channels = voxels_ref.shape
     own, before, count, after = device_counts(place_ref, counts_ref)
+    for c in range(rows // BLOCK):
+        live = live_lanes(c * BLOCK, BLOCK, rows, before, count, after)
+        block = voxels_ref[c * BLOCK : (c + 1) * BLOCK, :].T
+        act_ref[:, c * BLOCK : (c + 1) * BLOCK] = jnp.where(live, block.astype(F32), 0.0).astype(BF16)
+    linear = linear_ref[0].T
+
+    def gather(b, picked):
+        first = (b - 1) * BLOCK
+        targets = jnp.maximum(near_ref[:, columns(first + HALO)] - (own * rows + first), -1)
+        gather_block(lambda at, n: act_ref[:, pl.ds(pl.multiple_of(first + at, HALO), n)], targets, picked)
+
+    def convolve(b, picked):
+        conv[:, columns(b * BLOCK)] = dot(turned_ref[0], picked[...]).astype(BF16)
+
+    blocks = rows // BLOCK
+    gather(1, even)
     groups = rows // 128
     total = slots_table(destination_ref, shards)
     perm_ref[...] = joined(total, 0, groups)
     high_ref[...] = total[2 * groups : 3 * groups, :]
     low_ref[...] = total[3 * groups :, :]
-    for c in range(rows // BLOCK):
-        live = live_lanes(c * BLOCK, BLOCK, rows, before, count, after)
-        block = voxels_ref[c * BLOCK : (c + 1) * BLOCK, :].T
-        act_ref[:, c * BLOCK : (c + 1) * BLOCK] = jnp.where(live, block.astype(F32), 0.0).astype(BF16)
-    linear = linear_ref[0].T
-
-    def gather(b, picked):
-        first = (b - 1) * BLOCK
-        targets = jnp.maximum(near_ref[:, columns(first + HALO)] - (own * rows + first), -1)
-        gather_block(lambda at, n: act_ref[:, pl.ds(pl.multiple_of(first + at, HALO), n)], targets, picked)
-
-    def convolve(b, picked):
-        conv[:, columns(b * BLOCK)] = dot(turned_ref[0], picked[...]).astype(BF16)
-
-    blocks = rows // BLOCK
-    gather(1, even)
     weights_in[0].wait()
     weights_in[1].start()
     turn_weights(weight_ref, 0, turned_ref.at[0])

time: 83.5 us -> 84.7 us (1.014)
  Pallas kernels: 44.7 us -> 45.9 us
    pallas_call x1, Pallas kernels: 16.5 us -> 17.8 us  [local(): pl.pallas_call(functools.partial(inner_kernel, shards), out_shape=(struct...]
  transfers between devices with their start and end apart: 2 -> 2, of which waited for: 0 -> 0; matrix products, arithmetic and copies ran while one was open for 0% -> 0% of each run, Pallas kernels for 20% -> 21%
where the time goes in v10:
time: 84.7 us; the launch traced here: 84.5 us
  Pallas kernels  45.9 us (54%)
  blocking collectives  36.3 us (43%)
  starting transfers between devices  2.06 us (2%)
    all_to_all x1, blocking collectives, local(): got = lax.all_to_all(send, both, split_axis=0, concat_axis=0, tiled=True)  36.3 us
    pallas_call x1, Pallas kernels, local(): pl.pallas_call(outer_kernel, out_shape=struct((shards, depth, channels),...  20.8 us
    pallas_call x1, Pallas kernels, local(): pl.pallas_call(functools.partial(inner_kernel, shards), out_shape=(struct...  17.8 us
    pallas_call x1, Pallas kernels, local(): pl.pallas_call(final_kernel, out_shape=struct((rows, channels), BF16), in...  5.64 us
    pallas_call x1, Pallas kernels, local(): pl.pallas_call(edges_kernel, out_shape=(packed, packed), in_specs=[smem,...  1.72 us
  transfers between devices with their start and end apart: 2, of which 0 were waited for; matrix products, arithmetic and copies ran while one was open for 0% of the time, Pallas kernels for 21%

profile of v10, /device:TPU:0, one launch (start us, length us, event | category | flops | bytes accessed | tf_op | source)
XLA Modules:
  0.0 84.5 jit_solution(15489840231739075272)
XLA Ops:
  0.0 0.0 copy-start
  0.0 0.0 copy-start.1
  0.0 0.0 copy-start.2
  0.0 0.0 copy-start.3
  0.0 0.0 copy-start.4
  0.0 1.7 %edges.1 = (bf16[288,128]{1,0:T(8,128)(2,1)}, bf16[288,128]{1,0:T(8,128)(2,1)}) custom-call(s32[1]{0:T(128)} %bitcast.place_ref, bf16[4096,128]{1,0:T(8,128)(2,1)} %voxels_ref.1, s32[27,4096]{1,0:T(8,128)} %near_ref.3), custom_call_target="tpu_custom_call" | custom-call | flops 20000000000 | bytes 500000 | tf_op jit(solution)/shard_map/edges/pallas_call | solution.py:436
  1.7 0.5 collective-permute-start
  2.3 1.5 %collective-permute-start.1 = (bf16[288,128]{1,0:T(8,128)(2,1)}, bf16[288,128]{1,0:T(8,128)(2,1)S(1)}, u32[]{:S(2)}, u32[]{:S(2)}) collective-permute-start(bf16[288,128]{1,0:T(8,128)(2,1)} %get-tuple-element.14), channel_id=1, source_target_pairs={{0,0},{15,15},{1,2},{2,1},{3,4},{4,3},{5,6},{6,5},{7,8},{8,7},{9,1... | collective-permute-start | bytes 221192 | tf_op jit(solution)/shard_map/ppermute | solution.py:449
  3.8 0.0 copy-done
  3.8 0.0 copy-done.1
  3.8 0.0 copy-done.2
  3.8 0.0 copy-done.3
  3.8 0.0 copy-done.4
  3.8 17.8 %first_layer.1 = (bf16[128,4096]{1,0:T(8,128)(2,1)S(1)}, bf16[128,4352]{1,0:T(8,128)(2,1)S(1)}, s32[32,128]{1,0:T(8,128)S(1)}, f32[32,128]{1,0:T(8,128)S(1)}, f3...) custom-call(s32[1]{0:T(128)} %bitcast.place_ref, s32[16]{0:T(128)S(1)} %copy-done.4, ...), custom_call_target="tpu_custom_call" | custom-call | flops 20000000000 | bytes 6000000 | tf_op jit(solution)/shard_map/first_layer/pallas_call | solution.py:456
  21.6 0.0 collective-permute-done.pair_ref
  21.6 0.0 collective-permute-done.1.side_ref
  21.6 20.8 %second_layer.1 = bf16[16,272,128]{2,1,0:T(8,128)(2,1)S(1)} custom-call(s32[1]{0:T(128)} %bitcast.place_ref, s32[16]{0:T(128)S(1)} %copy-done.4, bf16[288,128]{1,0:T(8,128)(2,1)S(1)} %collective-permute-done.pair_ref, bf16[288,128]{1,0:T(8,128)(2,1)S(1)} %collective-permute-done.1.side_ref, bf16[128,4096]{1,0:T(8,128)(2,1)S(1)} %get-tuple-element.15.act_ref, ...), custom_call_target="tpu_custom_call" | custom-call | flops 30000001024 | bytes 8000000 | tf_op jit(solution)/shard_map/second_layer/pallas_call | solution.py:473
  42.4 36.3 %all_to_all.5.got_ref = bf16[16,272,128]{2,1,0:T(8,128)(2,1)S(1)} all-to-all(bf16[16,272,128]{2,1,0:T(8,128)(2,1)S(1)} %second_layer.1), channel_id=1, replica_groups=mesh['groups'=2,'wide'=8,'narrow'=2] {'wide','narrow'}, dimensions={0} | all-to-all | bytes 2228224 | tf_op jit(solution)/shard_map/all_to_all | solution.py:494
  78.7 5.6 %hilbert_order.1 = bf16[4096,128]{1,0:T(8,128)(2,1)} custom-call(bf16[16,272,128]{2,1,0:T(8,128)(2,1)S(1)} %all_to_all.5.got_ref), custom_call_target="tpu_custom_call" | custom-call | tf_op jit(solution)/shard_map/hilbert_order/pallas_call | solution.py:495
Async XLA Ops:
  0.0 3.8 %copy-start = (bf16[4096,128]{1,0:T(8,128)(2,1)S(1)}, bf16[4096,128]{1,0:T(8,128)(2,1)}, u32[]{:S(2)}) copy-start(bf16[4096,128]{1,0:T(8,128)(2,1)} %voxels_ref.1) | copy-start | bytes 3145732
  0.0 3.8 %copy-start.1 = (s32[27,4096]{1,0:T(8,128)S(1)}, s32[27,4096]{1,0:T(8,128)}, u32[]{:S(2)}) copy-start(s32[27,4096]{1,0:T(8,128)} %near_ref.3) | copy-start | bytes 1327108
  0.0 3.8 %copy-start.2 = (bf16[2,128,128]{2,1,0:T(8,128)(2,1)S(1)}, bf16[2,128,128]{2,1,0:T(8,128)(2,1)}, u32[]{:S(2)}) copy-start(bf16[2,128,128]{2,1,0:T(8,128)(2,1)} %linear_ref.3) | copy-start | bytes 196612
  0.0 3.8 %copy-start.3 = (s32[4096]{0:T(1024)S(1)}, s32[4096]{0:T(1024)}, u32[]{:S(2)}) copy-start(s32[4096]{0:T(1024)} %param.11) | copy-start | bytes 49156
  0.0 3.8 %copy-start.4 = (s32[16]{0:T(128)S(1)}, s32[16]{0:T(128)}, u32[]{:S(2)}) copy-start(s32[16]{0:T(128)} %counts_ref.3) | copy-start | bytes 196
  1.7 19.9 %collective-permute-start = (bf16[288,128]{1,0:T(8,128)(2,1)}, bf16[288,128]{1,0:T(8,128)(2,1)S(1)}, u32[]{:S(2)}, u32[]{:S(2)}) collective-permute-start(bf16[288,128]{1,0:T(8,128)(2,1)} %get-tuple-element.13), channel_id=1, source_target_pairs={{0,1},{1,0},{2,3},{3,2},{4,5},{5,4},{6,7},{7,6},{8,9},{9,8},{10,11... | collective-permute-start | bytes 221192 | tf_op jit(solution)/shard_map/ppermute | solution.py:450
  2.3 19.3 %collective-permute-start.1 = (bf16[288,128]{1,0:T(8,128)(2,1)}, bf16[288,128]{1,0:T(8,128)(2,1)S(1)}, u32[]{:S(2)}, u32[]{:S(2)}) collective-permute-start(bf16[288,128]{1,0:T(8,128)(2,1)} %get-tuple-element.14), channel_id=1, source_target_pairs={{0,0},{15,15},{1,2},{2,1},{3,4},{4,3},{5,6},{6,5},{7,8},{8,7},{9,1... | collective-permute-start | bytes 221192 | tf_op jit(solution)/shard_map/ppermute | solution.py:449
